TPU v7x, 512 devices: a whole 4x4x16 slice. The times are simulated.
512 devices in a mesh: sec: 2 (over x_hi), vocab: 32 (over z, x_lo), rows: 8 (over y, core).
Axes of the slice: x: 4 (x_hi: 2, x_lo: 2; x = x_hi * 2 + x_lo), y: 4, z: 16, core: 2. Of those that a mesh axis runs over, the one named last changes fastest.
Arguments:
- logits: bfloat16 [2, 2048, 65536], P('sec', 'rows', 'vocab'), may hold values from -400 to 400
- hidden: bfloat16 [2048, 2048], P('rows', 'sec'), may hold values from -6 to 6
- head_weight: bfloat16 [2048, 65536], P(('sec', 'rows'), 'vocab'), may hold values from -0.125 to 0.125
Outputs:
- hidden_grad: bfloat16 [2, 1024, 2048], P('sec', 'rows', 'vocab')
- weight_grad: bfloat16 [2048, 65536], P(('sec', 'rows'), 'vocab')
All inputs are finite; a program needn't handle non-finite values.
Results may differ from a plain program's by a relative error of at most 0.0059.
Values may be sent and summed in bfloat16 or wider, within the bound.
No kernel may reach another device: no remote copies, remote signals or barrier semaphores. Data moves between devices by JAX's collectives and lax.ppermute only.
A program may use at most 64 MiB of HBM per device.

v0:
```python
import jax
import jax.numpy as jnp
from jax import lax
from jax.sharding import PartitionSpec as P

loss_scale = 64.0


def merged_2(part, axis, combine):
    gathered = jax.tree.map(lambda a: lax.all_gather(a, axis), part)

    def take(source):
        return jax.tree.map(lambda a: lax.dynamic_index_in_dim(a, source, 0, False), gathered)

    return lax.fori_loop(
        1, lax.axis_size(axis), lambda source, state: combine(state, take(source)), take(0)
    )


def swapped(value, axis, distance):
    mask = 2**distance
    pairs = [(source, source ^ mask) for source in range(lax.axis_size(axis))]
    return lax.ppermute(value, axis, pairs)


def local_stats(values):
    highest = jnp.max(values, axis=1)
    totals = jnp.sum(jnp.exp(values - highest[:, None]), axis=1)
    return (highest, totals)


def pair_combine(former, latter):
    merged = []
    for position in range(0, len(former), 2):
        upper = jnp.maximum(former[position], latter[position])
        merged.append(upper)
        merged.append(
            former[position + 1] * jnp.exp(former[position] - upper)
            + latter[position + 1] * jnp.exp(latter[position] - upper)
        )
    return tuple(merged)


def normalized(values, highest, totals):
    weights = jnp.exp(values - highest[:, None]) / totals[:, None]
    return lax.optimization_barrier(weights.astype(jnp.bfloat16))


def body(logits, hidden, head_weight):
    section = lax.axis_index("sec")
    logit_tile = logits[0]
    half_rows = logit_tile.shape[0] // 2
    keep_offset = section * half_rows
    send_offset = (1 - section) * half_rows
    values = logit_tile.astype(jnp.float32)
    highest, totals = local_stats(values)
    highest, totals = merged_2((highest, totals), "vocab", pair_combine)
    probability = normalized(values, highest, totals)
    kept_probs = lax.dynamic_slice_in_dim(probability, keep_offset, half_rows, 0)
    outgoing = lax.dynamic_slice_in_dim(probability, send_offset, half_rows, 0)
    peer_probs = swapped(outgoing, "sec", 0)
    direction = (1 - 2 * section).astype(jnp.float32)
    difference = peer_probs.astype(jnp.float32) - kept_probs.astype(jnp.float32)
    grad_tile = (loss_scale * (direction * difference)).astype(jnp.bfloat16)
    blocks = head_weight.shape[0]
    stacked = hidden.reshape(2, half_rows, hidden.shape[1])
    spread = lax.all_to_all(stacked, "rows", split_axis=2, concat_axis=1, tiled=True)
    columns_all = spread.reshape(-1, blocks)
    partial_value = lax.dot_general(
        grad_tile,
        lax.all_gather(head_weight, ("sec", "rows"), axis=0, tiled=True),
        (((1,), (1,)), ((), ())),
        preferred_element_type=jnp.float32,
    )
    summed = lax.psum_scatter(partial_value, "vocab", scatter_dimension=1, tiled=True)
    weight_total = lax.dot_general(
        columns_all,
        lax.all_gather(grad_tile, ("sec", "rows"), axis=0, tiled=True),
        (((0,), (0,)), ((), ())),
        preferred_element_type=jnp.float32,
    )
    hidden_grad = summed.astype(jnp.bfloat16)[None]
    return (hidden_grad, weight_total.astype(jnp.bfloat16))


def solution(mesh):
    in_specs = (P("sec", "rows", "vocab"), P("rows", "sec"), P(("sec", "rows"), "vocab"))
    out_specs = (P("sec", "rows", "vocab"), P(("sec", "rows"), "vocab"))
    return jax.shard_map(body, mesh=mesh, in_specs=in_specs, out_specs=out_specs, check_vma=False)
```

profile of v0, /device:TPU:24, one launch (start us, length us, event | category | flops | bytes accessed | tf_op | source)
XLA Modules:
  0.0 383.5 jit_solution(2005799744163455716)
XLA Ops:
  7.2 0.0 all-gather.7.cloned.1.call-start
  7.2 0.7 all-gather.7.cloned.1.call-update
  7.9 0.0 all-gather.9.cloned.1.call-start
  8.0 1.5 reduce_max.18
  9.4 68.9 %all-gather.2 = f32[32,1,256]{2,1,0:T(1,128)S(1)} all-gather(f32[1,1,256]{2,1,0:T(1,128)S(1)} %bitcast.42), channel_id=2, replica_groups=mesh['sec'=2,'vocab'=32,'rows'=8] {'vocab'}, dimensions={0}, use_global_device_ids=true | all-gather | bytes 33792 | tf_op jit(solution)/shard_map/all_gather | solution.py:10
  78.3 1.7 fusion.2
  80.0 58.5 %all-gather.3 = f32[32,1,256]{2,1,0:T(1,128)S(1)} all-gather(f32[1,1,256]{2,1,0:T(1,128)S(1)} %bitcast.43), channel_id=3, replica_groups=mesh['sec'=2,'vocab'=32,'rows'=8] {'vocab'}, dimensions={0}, use_global_device_ids=true | all-gather | bytes 33792 | tf_op jit(solution)/shard_map/all_gather | solution.py:10
  138.5 1.8 while.17
  140.3 0.5 fusion.5
  140.8 4.6 %collective-permute-start = (bf16[128,2048]{1,0:T(8,128)(2,1)S(1)}, bf16[128,2048]{1,0:T(8,128)(2,1)S(1)}, u32[]{:S(2)}, u32[]{:S(2)}) collective-permute-start(bf16[128,2048]{1,0:T(8,128)(2,1)S(1)} %constant_dynamic-slice_fusion.2), channel_id=1, source_target_pairs={{0,256},{256,0},{1,257},{257,1},{2,258},{258,2},{3,259},{259,3},{4... | collective-permute-start | bytes 1572872 | tf_op jit(solution)/shard_map/ppermute | solution.py:23
  145.4 8.0 %collective-permute-done = bf16[128,2048]{1,0:T(8,128)(2,1)S(1)} collective-permute-done((bf16[128,2048]{1,0:T(8,128)(2,1)S(1)}, bf16[128,2048]{1,0:T(8,128)(2,1)S(1)}, u32[]{:S(2)}, u32[]{:S(2)}) %collective-permute-start) | collective-permute-done | bytes 524320 | tf_op jit(solution)/shard_map/ppermute | solution.py:23
  153.3 1.0 multiply_convert_fusion
  154.4 0.0 reduce-scatter.2.cloned.1.call-start
  154.4 0.0 all-gather.7.cloned.1.call-done
  154.4 6.9 %fusion.6 = f32[128,2048]{0,1:T(8,128)} fusion(bf16[128,2048]{1,0:T(8,128)(2,1)} %multiply_convert_fusion, bf16[2048,2048]{1,0:T(8,128)(2,1)} %all-gather.7.cloned.1.call-done), kind=kOutput, calls=%fused_computation.17 | convolution fusion | flops 1073741824 | bytes 9961472 | tf_op jit(solution)/shard_map/dot_general | solution.py:69
  161.4 0.4 copy.12
  161.8 16.3 %all_to_all.15 = bf16[2,128,1024]{1,0,2:T(2,128)(2,1)S(1)} all-to-all(bf16[2,128,1024]{1,0,2:T(2,128)(2,1)S(1)} %copy.12), channel_id=1, replica_groups=mesh['sec'=2,'vocab'=32,'rows'=8] {'rows'}, dimensions={2} | all-to-all | bytes 1048576 | tf_op jit(solution)/shard_map/all_to_all | solution.py:67
  178.2 0.1 copy.13
  178.3 0.3 copy.14
  178.5 58.2 %all-gather.9.cloned.1.call-done = bf16[2048,2048]{1,0:T(8,128)(2,1)} async-done(((bf16[128,2048]{1,0:T(8,128)(2,1)}), bf16[2048,2048]{1,0:T(8,128)(2,1)}) %all-gather.9.cloned.1.call-update) | async-done | bytes 8388624 | tf_op jit(solution)/shard_map/all_gather | solution.py:78
  236.8 5.8 %fusion = bf16[128,2048]{0,1:T(8,128)(2,1)S(1)} fusion(bf16[2048,2048]{1,0:T(8,128)(2,1)} %all-gather.9.cloned.1.call-done, bf16[2048,128]{1,0:T(8,128)(2,1)S(1)} %bitcast.35), kind=kOutput, calls=%fused_computation.6 | convolution fusion | flops 1074003968 | bytes 9437184 | tf_op jit(solution)/shard_map/dot_general | solution.py:76
  242.5 1.0 copy.15
  243.6 132.1 %reduce-scatter.2.cloned.1.call-done = f32[128,64]{0,1:T(8,128)} async-done(((f32[128,2048]{0,1:T(8,128)}), f32[128,64]{0,1:T(8,128)}) %reduce-scatter.2.cloned.1.call-update) | async-done | bytes 32784 | tf_op jit(solution)/shard_map/reduce_scatter | solution.py:75
  375.6 1.4 convert_bitcast_fusion
  (74 shorter events, 1.1 us)
Async XLA Ops:
  7.2 133.1 %copy-start = (bf16[1,256,2048]{2,1,0:T(8,128)(2,1)S(1)}, bf16[1,256,2048]{2,1,0:T(8,128)(2,1)}, u32[]{:S(2)}) copy-start(bf16[1,256,2048]{2,1,0:T(8,128)(2,1)} %param.5) | copy-start | bytes 3145732
  7.2 147.3 %all-gather.7.cloned.1.call-start = ((), (), s32[]{:S(2)}) async-start(), calls=%async_computation.2 | async-start | bytes 8912896 | tf_op jit(solution)/shard_map/all_gather | solution.py:71
  7.9 228.9 %all-gather.9.cloned.1.call-start = ((), (), s32[]{:S(2)}) async-start(), calls=%async_computation.4 | async-start | bytes 8912896 | tf_op jit(solution)/shard_map/all_gather | solution.py:78
  140.8 12.6 %collective-permute-start = (bf16[128,2048]{1,0:T(8,128)(2,1)S(1)}, bf16[128,2048]{1,0:T(8,128)(2,1)S(1)}, u32[]{:S(2)}, u32[]{:S(2)}) collective-permute-start(bf16[128,2048]{1,0:T(8,128)(2,1)S(1)} %constant_dynamic-slice_fusion.2), channel_id=1, source_target_pairs={{0,256},{256,0},{1,257},{257,1},{2,258},{258,2},{3,259},{259,3},{4... | collective-permute-start | bytes 1572872 | tf_op jit(solution)/shard_map/ppermute | solution.py:23
  154.4 7.1 %copy-start.1 = (bf16[256,1024]{1,0:T(8,128)(2,1)S(1)}, bf16[256,1024]{1,0:T(8,128)(2,1)}, u32[]{:S(2)}) copy-start(bf16[256,1024]{1,0:T(8,128)(2,1)} %param.6) | copy-start | bytes 1572868
  154.4 221.2 %reduce-scatter.2.cloned.1.call-start = ((), (), s32[]{:S(2)}) async-start(), calls=%async_computation.3 | async-start | bytes 1081344 | tf_op jit(solution)/shard_map/reduce_scatter | solution.py:75
Sparse Core Ops, SparseCore 0:
  11.3 90.9 all-gather.6
  154.5 82.2 all-gather.8
  239.6 135.9 reduce-scatter.1
where the time goes:
time: 384 us
  waiting for transfers between devices  199 us (52%)
  blocking collectives  144 us (38%)
  between operations  13.9 us (4%)
  matrix products  12.7 us (3%)
  other arithmetic  6.61 us (2%)
  starting transfers between devices  4.72 us (1%)
    reduce_scatter x1, waiting for transfers between devices, body(): lax.psum_scatter(partial_value, 'vocab', scatter_dimension=1, tiled=True)  132 us
    all_gather x2, blocking collectives, merged_2(): gathered = jax.tree.map(lambda a: lax.all_gather(a, axis), part)  127 us
    all_gather x1, waiting for transfers between devices, body(): lax.all_gather(grad_tile, ('sec', 'rows'), axis=0, tiled=True)  58.2 us
    all_to_all x1, blocking collectives, body(): lax.all_to_all(stacked, 'rows', split_axis=2, concat_axis=1, tiled=True)  16.3 us
    ppermute x1, waiting for transfers between devices, swapped(): return lax.ppermute(value, axis, pairs)  7.96 us
  transfers between devices with their start and end apart: 4, of which 3 were waited for; matrix products, arithmetic and copies ran while one was open for 5% of the time, Pallas kernels for 0%

commit v1 on v0

v1 whole, which is shorter than its diff:
```python
import jax
import jax.numpy as jnp
from jax import lax
from jax.sharding import PartitionSpec as P

loss_scale = 64.0
swap_sec = [(0, 1), (1, 0)]
swap_core = [(i, i ^ 1) for i in range(8)]
same_core = [[0, 2, 4, 6], [1, 3, 5, 7]]


def body(logits, hidden, head_weight):
    f32, bf16 = jnp.float32, jnp.bfloat16
    section = lax.axis_index("sec")
    core = lax.axis_index("rows") % 2
    own = logits[0]
    rows, width = own.shape
    half_rows = rows // 2
    n_vocab = lax.axis_size("vocab")
    groups = lax.axis_size("rows")
    head_rows = head_weight.shape[0]
    piece = head_rows // 4

    blocks = head_weight.reshape(2, 2, piece, width)
    kept = lax.dynamic_index_in_dim(blocks, section, 1, False).reshape(2 * piece, width)
    outgoing = lax.dynamic_index_in_dim(blocks, 1 - section, 1, False).reshape(2 * piece, width)
    received = lax.ppermute(outgoing, "sec", swap_sec)
    peer = lax.ppermute(own, "sec", swap_sec)
    head_kept = lax.all_gather(kept, "rows", tiled=True)
    head_received = lax.all_gather(received, "rows", tiled=True)

    columns = hidden.reshape(rows, groups // 2, 2, head_rows)
    own_columns = lax.dynamic_index_in_dim(columns, core, 2, False).reshape(rows, -1)
    other_columns = lax.dynamic_index_in_dim(columns, 1 - core, 2, False).reshape(rows, -1)
    core_columns = lax.ppermute(other_columns, "rows", swap_core)

    values = own.astype(f32)
    highest = jnp.max(values, axis=1)
    totals = jnp.sum(jnp.exp(values - highest[:, None]), axis=1)
    part = jnp.stack([highest, totals])
    copies = jnp.broadcast_to(part[None], (2 * n_vocab, 2, rows))
    parts = lax.all_to_all(copies, ("sec", "vocab"), 0, 0, tiled=True)
    parts = parts.reshape(2, n_vocab, 2, rows)
    top = jnp.max(parts[:, :, 0], axis=1)
    total = jnp.sum(parts[:, :, 1] * jnp.exp(parts[:, :, 0] - top[:, None]), axis=1)

    def probability(tile, which):
        m = lax.dynamic_index_in_dim(top, which, 0, False)
        t = lax.dynamic_index_in_dim(total, which, 0, False)
        weights = jnp.exp(tile.astype(f32) - m[:, None]) / t[:, None]
        return weights.astype(bf16)

    own_probs, peer_probs = lax.optimization_barrier(
        (probability(own, section), probability(peer, 1 - section))
    )
    direction = (1 - 2 * section).astype(f32)
    difference = peer_probs.astype(f32) - own_probs.astype(f32)
    grad = (loss_scale * (direction * difference)).astype(bf16)

    def terms(head):
        out = lax.dot_general(head, grad, (((1,), (1,)), ((), ())), preferred_element_type=f32)
        return out.astype(bf16).reshape(groups, 2, piece, 2, half_rows)

    first, second = terms(head_kept), terms(head_received)
    lower = jnp.where(section == 0, first, second)
    upper = jnp.where(section == 0, second, first)
    outgoing_terms = jnp.concatenate([lower, upper]).transpose(3, 0, 1, 2, 4)
    outgoing_terms = outgoing_terms.reshape(2 * n_vocab, piece, half_rows)
    incoming_terms = lax.all_to_all(outgoing_terms, ("sec", "vocab"), 0, 0, tiled=True)
    summed = jnp.sum(incoming_terms.reshape(2, n_vocab, piece, half_rows).astype(f32), axis=1)
    hidden_grad = summed.reshape(2 * piece, half_rows).T.astype(bf16)[None]

    core_grad = lax.ppermute(grad, "rows", swap_core)
    dims = (((0,), (0,)), ((), ()))
    weight_part = lax.dot_general(own_columns, grad, dims, preferred_element_type=f32)
    weight_part = weight_part + lax.dot_general(core_columns, core_grad, dims, preferred_element_type=f32)
    weight_part = weight_part.astype(bf16).reshape(groups // 2, head_rows, width)
    weight_parts = lax.all_to_all(weight_part, "rows", 0, 0, axis_index_groups=same_core, tiled=True)
    weight_grad = jnp.sum(weight_parts.astype(f32), axis=0).astype(bf16)
    return hidden_grad, weight_grad


def solution(mesh):
    in_specs = (P("sec", "rows", "vocab"), P("rows", "sec"), P(("sec", "rows"), "vocab"))
    out_specs = (P("sec", "rows", "vocab"), P(("sec", "rows"), "vocab"))
    return jax.shard_map(body, mesh=mesh, in_specs=in_specs, out_specs=out_specs, check_vma=False)
```

time: 384 us -> 160 us (0.42)
  the two profiles are of different devices: /device:TPU:24 before, /device:TPU:10 now
where the time goes in v1:
time: 160 us
  waiting for transfers between devices  74.8 us (47%)
  starting transfers between devices  50.7 us (32%)
  between operations  14.2 us (9%)
  matrix products  8.88 us (6%)
  other arithmetic  6.35 us (4%)
  local copies, waits for them, and re-layouts  4.68 us (3%)
    all_to_all x1, waiting for transfers between devices, body(): lax.all_to_all(outgoing_terms, ('sec', 'vocab'), 0, 0, tiled=True)  31.2 us
    all_to_all x1, starting transfers between devices, body(): parts = lax.all_to_all(copies, ('sec', 'vocab'), 0, 0, tiled=True)  18.6 us
    ppermute x1, waiting for transfers between devices, body(): peer = lax.ppermute(own, 'sec', swap_sec)  17 us
    all_to_all x1, waiting for transfers between devices, body(): lax.all_to_all(weight_part, 'rows', 0, 0, axis_index_groups=same_core, ti...  16.1 us
    all_to_all x1, starting transfers between devices, body(): lax.all_to_all(outgoing_terms, ('sec', 'vocab'), 0, 0, tiled=True)  15.4 us
    dot_general x2, matrix products, terms(): lax.dot_general(head, grad, (((1,), (1,)), ((), ())), preferred_element_t...  6.1 us
    ppermute x1, waiting for transfers between devices, body(): received = lax.ppermute(outgoing, 'sec', swap_sec)  6.08 us
    all_to_all x1, starting transfers between devices, body(): lax.all_to_all(weight_part, 'rows', 0, 0, axis_index_groups=same_core, ti...  4.92 us
  transfers between devices with their start and end apart: 9, of which 7 were waited for; matrix products, arithmetic and copies ran while one was open for 10% of the time, Pallas kernels for 0%

profile of v1, /device:TPU:10, one launch (start us, length us, event | category | flops | bytes accessed | tf_op | source)
XLA Modules:
  0.0 159.6 jit_solution(15288530475443125631)
XLA Ops:
  7.2 1.9 %constant_dynamic-slice_fusion.7 = (bf16[2,1,32,2048]{3,2,1,0:T(8,128)(2,1)}, bf16[2,1,32,2048]{3,2,1,0:T(8,128)(2,1)S(1)}) fusion(bf16[2,2,32,2048]{3,2,1,0:T(8,128)(2,1)} %bitcast.54, s32[]{:T(128)S(6)} %select_n.45, s32[]{:T(128)S(6)} %select_n.46), kind=kLoop, calls=%fused_computation.30 | loop fusion | bytes 1048584 | tf_op jit(solution)/shard_map/jit(dynamic_index_in_dim)/dynamic_slice | solution.py:25
  9.1 1.5 reduce_max.27
  11.1 0.7 broadcast_in_dim.4
  11.8 18.6 %all-to-all-start = ((f32[64,2,256]{2,1,0:T(2,128)}), f32[64,2,256]{2,1,0:T(2,128)S(1)}, u32[]{:S(2)}, u32[]{:S(2)}) async-start(f32[64,2,256]{2,1,0:T(2,128)} %broadcast_in_dim.4), calls=%async_computation | async-start | bytes 262144 | tf_op jit(solution)/shard_map/all_to_all | solution.py:42
  30.5 4.1 %collective-permute-start.1 = (bf16[64,2048]{1,0:T(8,128)(2,1)S(1)}, bf16[64,2048]{1,0:T(8,128)(2,1)S(1)}, u32[]{:S(2)}, u32[]{:S(2)}) collective-permute-start(bf16[64,2048]{1,0:T(8,128)(2,1)S(1)} %bitcast.56), channel_id=1, source_target_pairs={{0,256},{256,0},{1,257},{257,1},{2,258},{258,2},{3,259},{259,3},{4... | collective-permute-start | bytes 786440 | tf_op jit(solution)/shard_map/ppermute | solution.py:27
  34.6 3.3 %collective-permute-start = (bf16[256,2048]{1,0:T(8,128)(2,1)S(1)}, bf16[256,2048]{1,0:T(8,128)(2,1)S(1)}, u32[]{:S(2)}, u32[]{:S(2)}) collective-permute-start(bf16[256,2048]{1,0:T(8,128)(2,1)S(1)} %bitcast.49), channel_id=1, source_target_pairs={{0,256},{256,0},{1,257},{257,1},{2,258},{258,2},{3,259},{259,3},{4... | collective-permute-start | bytes 3145736 | tf_op jit(solution)/shard_map/ppermute | solution.py:28
  37.8 6.1 %collective-permute-done.1 = bf16[64,2048]{1,0:T(8,128)(2,1)S(1)} collective-permute-done((bf16[64,2048]{1,0:T(8,128)(2,1)S(1)}, bf16[64,2048]{1,0:T(8,128)(2,1)S(1)}, u32[]{:S(2)}, u32[]{:S(2)}) %collective-permute-start.1) | collective-permute-done | bytes 262176 | tf_op jit(solution)/shard_map/ppermute | solution.py:27
  43.9 0.7 copy-done.2
  44.6 2.7 %all-to-all-done = f32[64,2,256]{2,1,0:T(2,128)S(1)} async-done(((f32[64,2,256]{2,1,0:T(2,128)}), f32[64,2,256]{2,1,0:T(2,128)S(1)}, u32[]{:S(2)}, u32[]{:S(2)}) %all-to-all-start) | async-done | bytes 131104 | tf_op jit(solution)/shard_map/all_to_all | solution.py:42
  48.0 17.0 %collective-permute-done = bf16[256,2048]{1,0:T(8,128)(2,1)S(1)} collective-permute-done((bf16[256,2048]{1,0:T(8,128)(2,1)S(1)}, bf16[256,2048]{1,0:T(8,128)(2,1)S(1)}, u32[]{:S(2)}, u32[]{:S(2)}) %collective-permute-start) | collective-permute-done | bytes 1048608 | tf_op jit(solution)/shard_map/ppermute | solution.py:28
  66.0 1.9 %collective-permute-start.3 = (bf16[256,2048]{1,0:T(8,128)(2,1)S(1)}, bf16[256,2048]{1,0:T(8,128)(2,1)S(1)}, u32[]{:S(2)}, u32[]{:S(2)}) collective-permute-start(bf16[256,2048]{1,0:T(8,128)(2,1)S(1)} %multiply_convert_fusion), channel_id=1, source_target_pairs={{0,1},{1,0},{2,3},{3,2},{4,5},{5,4},{6,7},{7,6},{8,9},{9,8},{10,11... | collective-permute-start | bytes 3145736 | tf_op jit(solution)/shard_map/ppermute | solution.py:73
  68.2 2.4 %collective-permute-start.2 = (bf16[256,512]{0,1:T(8,128)(2,1)S(1)}, bf16[256,512]{0,1:T(8,128)(2,1)S(1)}, u32[]{:S(2)}, u32[]{:S(2)}) collective-permute-start(bf16[256,512]{0,1:T(8,128)(2,1)S(1)} %bitcast.57), channel_id=1, source_target_pairs={{0,1},{1,0},{2,3},{3,2},{4,5},{5,4},{6,7},{7,6},{8,9},{9,8},{10,11... | collective-permute-start | bytes 786440 | tf_op jit(solution)/shard_map/ppermute | solution.py:35
  70.6 0.7 fusion.9
  71.8 2.1 %add_convert_fusion = bf16[512,2048]{1,0:T(8,128)(2,1)} fusion(f32[512,2048]{1,0:T(8,128)S(1)} %fusion.9, bf16[256,512]{0,1:T(8,128)(2,1)S(1)} %collective-permute-done.2, bf16[256,2048]{1,0:T(8,128)(2,1)S(1)} %collective-permute-done.3), kind=kOutput, calls=%fused_computation | convolution fusion | flops 538968064 | bytes 7602176 | tf_op jit(solution)/shard_map/dot_general | solution.py:76
  73.8 4.9 %all-to-all-start.2 = ((bf16[4,128,2048]{2,1,0:T(8,128)(2,1)}), bf16[4,128,2048]{2,1,0:T(8,128)(2,1)S(1)}, u32[]{:S(2)}, u32[]{:S(2)}) async-start(bf16[4,128,2048]{2,1,0:T(8,128)(2,1)} %bitcast.50), calls=%async_computation.2 | async-start | bytes 4194304 | tf_op jit(solution)/shard_map/all_to_all | solution.py:78
  78.7 3.1 %convolution_convert_fusion.1 = bf16[512,256]{1,0:T(8,128)(2,1)} fusion(bf16[512,2048]{1,0:T(8,128)(2,1)} %all-gather.3.cloned.1.call-done, bf16[256,2048]{1,0:T(8,128)(2,1)S(1)} %multiply_convert_fusion), kind=kOutput, calls=%fused_computation.11 | convolution fusion | flops 537001984 | bytes 3407872 | tf_op jit(solution)/shard_map/dot_general | solution.py:61
  81.8 1.3 all-gather.5.cloned.1.call-done
  83.1 3.0 %broadcast_select_fusion.1 = (bf16[512,256]{1,0:T(8,128)(2,1)S(1)}, bf16[512,256]{1,0:T(8,128)(2,1)}) fusion(bf16[512,256]{1,0:T(8,128)(2,1)} %convolution_convert_fusion.1, pred[]{:T(512)S(6)} %eq.6, bf16[512,2048]{1,0:T(8,128)(2,1)} %all-gather.5.cloned.1.call-done, bf16[256,2048]{1,0:T(8,128)(2,1)S(1)} %multiply_convert_fusion), kind=kOutput, calls=%fused_computation.15 | convolution fusion | flops 537264128 | bytes 3932161 | tf_op jit(solution)/shard_map/dot_general | solution.py:61
  86.1 1.0 select_n.50
  87.3 0.8 pad_maximum_fusion
  88.1 16.1 %all-to-all-done.2 = bf16[4,128,2048]{2,1,0:T(8,128)(2,1)S(1)} async-done(((bf16[4,128,2048]{2,1,0:T(8,128)(2,1)}), bf16[4,128,2048]{2,1,0:T(8,128)(2,1)S(1)}, u32[]{:S(2)}, u32[]{:S(2)}) %all-to-all-start.2) | async-done | bytes 2097184 | tf_op jit(solution)/shard_map/all_to_all | solution.py:78
  104.3 15.4 %all-to-all-start.1 = ((bf16[64,32,128]{2,1,0:T(8,128)(2,1)}), bf16[64,32,128]{2,1,0:T(8,128)(2,1)S(1)}, u32[]{:S(2)}, u32[]{:S(2)}) async-start(bf16[64,32,128]{2,1,0:T(8,128)(2,1)} %bitcast.14), calls=%async_computation.1 | async-start | bytes 1048576 | tf_op jit(solution)/shard_map/all_to_all | solution.py:69
  119.6 1.3 reduce_sum.42
  120.9 31.2 %all-to-all-done.1 = bf16[64,32,128]{2,1,0:T(8,128)(2,1)S(1)} async-done(((bf16[64,32,128]{2,1,0:T(8,128)(2,1)}), bf16[64,32,128]{2,1,0:T(8,128)(2,1)S(1)}, u32[]{:S(2)}, u32[]{:S(2)}) %all-to-all-start.1) | async-done | bytes 524320 | tf_op jit(solution)/shard_map/all_to_all | solution.py:69
  (27 shorter events, 3.7 us)
Async XLA Ops:
  7.2 3.4 %copy-start = (bf16[1,256,2048]{2,1,0:T(8,128)(2,1)S(1)}, bf16[1,256,2048]{2,1,0:T(8,128)(2,1)}, u32[]{:S(2)}) copy-start(bf16[1,256,2048]{2,1,0:T(8,128)(2,1)} %param.3) | copy-start | bytes 3145732
  7.2 71.6 %all-gather.3.cloned.1.call-start = ((), (), s32[]{:S(2)}) async-start(), calls=%async_computation.3 | async-start | bytes 2359296 | tf_op jit(solution)/shard_map/all_gather | solution.py:29
  11.8 35.6 %all-to-all-start = ((f32[64,2,256]{2,1,0:T(2,128)}), f32[64,2,256]{2,1,0:T(2,128)S(1)}, u32[]{:S(2)}, u32[]{:S(2)}) async-start(f32[64,2,256]{2,1,0:T(2,128)} %broadcast_in_dim.4), calls=%async_computation | async-start | bytes 262144 | tf_op jit(solution)/shard_map/all_to_all | solution.py:42
  30.4 52.7 %all-gather.5.cloned.1.call-start = ((), (), s32[]{:S(2)}) async-start(), calls=%async_computation.4 | async-start | bytes 2359296 | tf_op jit(solution)/shard_map/all_gather | solution.py:30
  30.5 13.4 %collective-permute-start.1 = (bf16[64,2048]{1,0:T(8,128)(2,1)S(1)}, bf16[64,2048]{1,0:T(8,128)(2,1)S(1)}, u32[]{:S(2)}, u32[]{:S(2)}) collective-permute-start(bf16[64,2048]{1,0:T(8,128)(2,1)S(1)} %bitcast.56), channel_id=1, source_target_pairs={{0,256},{256,0},{1,257},{257,1},{2,258},{258,2},{3,259},{259,3},{4... | collective-permute-start | bytes 786440 | tf_op jit(solution)/shard_map/ppermute | solution.py:27
  34.6 30.4 %collective-permute-start = (bf16[256,2048]{1,0:T(8,128)(2,1)S(1)}, bf16[256,2048]{1,0:T(8,128)(2,1)S(1)}, u32[]{:S(2)}, u32[]{:S(2)}) collective-permute-start(bf16[256,2048]{1,0:T(8,128)(2,1)S(1)} %bitcast.49), channel_id=1, source_target_pairs={{0,256},{256,0},{1,257},{257,1},{2,258},{258,2},{3,259},{259,3},{4... | collective-permute-start | bytes 3145736 | tf_op jit(solution)/shard_map/ppermute | solution.py:28
  43.9 0.7 copy-start.2
  65.5 2.5 %copy-start.1 = (bf16[256,1024]{1,0:T(8,128)(2,1)S(1)}, bf16[256,1024]{1,0:T(8,128)(2,1)}, u32[]{:S(2)}) copy-start(bf16[256,1024]{1,0:T(8,128)(2,1)} %param.4) | copy-start | bytes 1572868
  66.0 5.8 %collective-permute-start.3 = (bf16[256,2048]{1,0:T(8,128)(2,1)S(1)}, bf16[256,2048]{1,0:T(8,128)(2,1)S(1)}, u32[]{:S(2)}, u32[]{:S(2)}) collective-permute-start(bf16[256,2048]{1,0:T(8,128)(2,1)S(1)} %multiply_convert_fusion), channel_id=1, source_target_pairs={{0,1},{1,0},{2,3},{3,2},{4,5},{5,4},{6,7},{7,6},{8,9},{9,8},{10,11... | collective-permute-start | bytes 3145736 | tf_op jit(solution)/shard_map/ppermute | solution.py:73
  68.2 3.6 %collective-permute-start.2 = (bf16[256,512]{0,1:T(8,128)(2,1)S(1)}, bf16[256,512]{0,1:T(8,128)(2,1)S(1)}, u32[]{:S(2)}, u32[]{:S(2)}) collective-permute-start(bf16[256,512]{0,1:T(8,128)(2,1)S(1)} %bitcast.57), channel_id=1, source_target_pairs={{0,1},{1,0},{2,3},{3,2},{4,5},{5,4},{6,7},{7,6},{8,9},{9,8},{10,11... | collective-permute-start | bytes 786440 | tf_op jit(solution)/shard_map/ppermute | solution.py:35
  73.8 30.4 %all-to-all-start.2 = ((bf16[4,128,2048]{2,1,0:T(8,128)(2,1)}), bf16[4,128,2048]{2,1,0:T(8,128)(2,1)S(1)}, u32[]{:S(2)}, u32[]{:S(2)}) async-start(bf16[4,128,2048]{2,1,0:T(8,128)(2,1)} %bitcast.50), calls=%async_computation.2 | async-start | bytes 4194304 | tf_op jit(solution)/shard_map/all_to_all | solution.py:78
  104.3 47.9 %all-to-all-start.1 = ((bf16[64,32,128]{2,1,0:T(8,128)(2,1)}), bf16[64,32,128]{2,1,0:T(8,128)(2,1)S(1)}, u32[]{:S(2)}, u32[]{:S(2)}) async-start(bf16[64,32,128]{2,1,0:T(8,128)(2,1)} %bitcast.14), calls=%async_computation.1 | async-start | bytes 1048576 | tf_op jit(solution)/shard_map/all_to_all | solution.py:69
Sparse Core Ops, SparseCore 0:
  10.7 35.9 all-gather.2
  48.9 34.1 all-gather.4

commit v2 on v1

v2 whole, which is shorter than its diff:
```python
import jax
import jax.numpy as jnp
from jax import lax
from jax.experimental import pallas as pl
from jax.experimental.pallas import tpu as pltpu
from jax.sharding import PartitionSpec as P

loss_scale = 64.0
f32, bf16 = jnp.float32, jnp.bfloat16
swap_sec = [(0, 1), (1, 0)]
swap_core = [(i, i ^ 1) for i in range(8)]
near_groups = [
    [256 * sec + 8 * (8 * far + near) + 2 * y + core for sec in range(2) for core in range(2) for near in range(8)]
    for far in range(4)
    for y in range(4)
]
far_groups = [[8 * far + near for far in range(4)] for near in range(8)]


def shifted(value, distance):
    pairs = [(i, (i + 2 * distance) % 8) for i in range(8)]
    return lax.ppermute(value, "rows", pairs)


def spread(value, step):
    pairs = [(2 * y + o, (y + 2 * o + step) % 4 * 2 + y // 2) for y in range(4) for o in range(2)]
    return lax.ppermute(value, "rows", pairs)


def call(kernel, out_shape, micros, name, smem=0, grid=1, in_blocks=None, out_blocks=None, scratch=(), limit=24):
    def spec(array, dimension):
        block = list(array.shape)
        if dimension is not None:
            block[dimension] //= grid
        index = lambda i: tuple(i if d == dimension else 0 for d in range(len(block)))
        return pl.BlockSpec(tuple(block), index)

    def run(*args):
        cuts = in_blocks or [None] * (len(args) - smem)
        outs = jax.tree.leaves(out_shape)
        out_specs = [spec(o, d) for o, d in zip(outs, out_blocks or [None] * len(outs))]
        return pl.pallas_call(
            kernel,
            out_shape=out_shape,
            grid=(grid,),
            in_specs=[pl.BlockSpec(memory_space=pltpu.SMEM)] * smem
            + [spec(x, d) for x, d in zip(args[smem:], cuts)],
            out_specs=out_specs if len(outs) > 1 else out_specs[0],
            scratch_shapes=scratch,
            compiler_params=pltpu.CompilerParams(vmem_limit_bytes=limit * 1024 * 1024),
            cost_estimate=pl.CostEstimate(flops=int(micros * 1.0e9), bytes_accessed=int(micros * 3.0e6), transcendentals=0),
            name=name,
        )(*args)

    return run


def row_of(column):
    return jnp.broadcast_to(column, (column.shape[0], 128)).T[0:1]


def stats_kernel(values_ref, copies_ref):
    rows, width = values_ref.shape
    highest = values_ref[:, 0:128]
    for c in range(128, width, 128):
        highest = jnp.maximum(highest, values_ref[:, c : c + 128])
    highest = jnp.max(highest.astype(f32), axis=1, keepdims=True)
    totals = jnp.zeros((rows, 128), f32)
    for c in range(0, width, 128):
        totals = totals + jnp.exp(values_ref[:, c : c + 128].astype(f32) - highest)
    totals = jnp.sum(totals, axis=1, keepdims=True)
    part = jnp.concatenate([row_of(highest), row_of(totals)])
    copies_ref[...] = jnp.broadcast_to(part[None], copies_ref.shape)


def grad_kernel(place_ref, parts_ref, own_hbm, peer_hbm, grad_ref, own_ref, peer_ref, own_sems, peer_sems):
    section = place_ref[0]
    rows, width = grad_ref.shape
    pieces = own_sems.shape[0]
    piece = rows // pieces
    copies = []
    for i in range(pieces):
        here = pl.ds(i * piece, piece)
        pair = (
            pltpu.make_async_copy(own_hbm.at[here], own_ref.at[here], own_sems.at[i]),
            pltpu.make_async_copy(peer_hbm.at[here], peer_ref.at[here], peer_sems.at[i]),
        )
        for copy in pair:
            copy.start()
        copies.append(pair)

    def whole(which):
        highest, totals = parts_ref[which, :, 0], parts_ref[which, :, 1]
        top = jnp.max(highest, axis=0, keepdims=True)
        total = jnp.sum(totals * jnp.exp(highest - top), axis=0, keepdims=True)
        return jnp.broadcast_to(top, (128, rows)).T, jnp.broadcast_to(1.0 / total, (128, rows)).T

    own_tops, own_scales = whole(section)
    peer_tops, peer_scales = whole(1 - section)
    factor = loss_scale * (1 - 2 * section).astype(f32)
    for i in range(pieces):
        for copy in copies[i]:
            copy.wait()
        first = i * piece
        for c in range(0, width, 128):
            cut = (slice(first, first + piece), slice(c, c + 128))
            own = jnp.exp(own_ref[cut].astype(f32) - own_tops[cut[0]]) * own_scales[cut[0]]
            peer = jnp.exp(peer_ref[cut].astype(f32) - peer_tops[cut[0]]) * peer_scales[cut[0]]
            difference = peer.astype(bf16).astype(f32) - own.astype(bf16).astype(f32)
            grad_ref[cut] = (factor * difference).astype(bf16)


def logit_grad(place, parts, own, peer, micros):
    pieces = 4
    hbm, vmem = pl.BlockSpec(memory_space=pltpu.HBM), pl.BlockSpec(memory_space=pltpu.VMEM)
    sems = pltpu.SemaphoreType.DMA((pieces,))
    return pl.pallas_call(
        grad_kernel,
        out_shape=jax.ShapeDtypeStruct(own.shape, bf16),
        in_specs=[pl.BlockSpec(memory_space=pltpu.SMEM), vmem, hbm, hbm],
        out_specs=vmem,
        scratch_shapes=[pltpu.VMEM(own.shape, bf16), pltpu.VMEM(own.shape, bf16), sems, sems],
        compiler_params=pltpu.CompilerParams(vmem_limit_bytes=24 * 1024 * 1024),
        cost_estimate=pl.CostEstimate(flops=int(micros * 1.0e9), bytes_accessed=int(micros * 3.0e6), transcendentals=0),
        name="logit_grad",
    )(place, parts, own, peer)


def weight_kernel(own_columns_ref, core_columns_ref, own_ref, core_ref, *out_refs):
    sides = (((0,), (0,)), ((), ()))
    terms = lax.dot_general(own_columns_ref[...], own_ref[...], sides, preferred_element_type=f32)
    terms = terms + lax.dot_general(core_columns_ref[...], core_ref[...], sides, preferred_element_type=f32)
    for j, ref in enumerate(out_refs):
        ref[...] = terms[j * 128 : j * 128 + 128].astype(ref.dtype)


def sum_kernel(*refs):
    total = refs[0][...].astype(f32)
    for ref in refs[1:-1]:
        total = total + ref[...].astype(f32)
    refs[-1][...] = total.astype(bf16)


def terms_kernel(place_ref, *refs):
    heads, own_ref, core_ref, out_ref = refs[:4], refs[4], refs[5], refs[6]
    chip, core = place_ref[1], place_ref[2]
    head = jnp.concatenate([ref[...] for ref in heads])
    for o, ref in enumerate((own_ref, core_ref)):
        terms = lax.dot_general(head, ref[...], (((1,), (1,)), ((), ())), preferred_element_type=f32)
        terms = terms.astype(bf16)
        for step in range(4):
            source = (chip + (8 - 2 * core) - step) % 4
            slot = source % 2 * 4 + source // 2 * 2
            for x in range(2):
                first = step * 128 + x * 64
                for s in range(2):
                    out_ref[s, (core + o) % 2, slot + x] = terms[first : first + 64, s * 128 : s * 128 + 128]


def total_kernel(parts_ref, out_ref):
    total = parts_ref[:, 0].astype(f32)
    for i in range(1, parts_ref.shape[1]):
        total = total + parts_ref[:, i].astype(f32)
    out_ref[...] = total.astype(bf16)


def body(logits, hidden, head_weight):
    section = lax.axis_index("sec")
    core = lax.axis_index("rows") % 2
    chip = lax.axis_index("rows") // 2
    own = logits[0]
    rows, width = own.shape
    half_rows = rows // 2
    n_vocab = lax.axis_size("vocab")
    chips = lax.axis_size("rows") // 2
    head_rows = head_weight.shape[0]

    peer = lax.ppermute(own, "sec", swap_sec)
    heads = [spread(head_weight, step) for step in range(chips)]

    def ahead(index):
        offsets = [((chip + j) % chips * 2 + index) * head_rows for j in range(chips)]
        return [lax.dynamic_slice_in_dim(hidden, o, head_rows, 1) for o in offsets]

    own_columns = jnp.concatenate(ahead(core), axis=1)
    core_columns = lax.ppermute(jnp.concatenate(ahead(1 - core), axis=1), "rows", swap_core)

    peer, heads[:2] = lax.optimization_barrier((peer, heads[:2]))

    copies = jax.ShapeDtypeStruct((2 * n_vocab, 2, rows), f32)
    copies = call(stats_kernel, copies, 3, "row_stats", 0, 2, [0], [2])(own)
    parts = lax.all_to_all(copies, ("sec", "vocab"), 0, 0, tiled=True)
    parts = parts.reshape(2, n_vocab, 2, rows)
    place = jnp.stack([section, chip, core]).astype(jnp.int32)
    grad = logit_grad(place, parts, own, peer, 40)

    columns = (own_columns, core_columns)
    grad, heads, columns = lax.optimization_barrier((grad, heads, columns))
    core_grad = lax.ppermute(grad, "rows", swap_core)
    near = jax.ShapeDtypeStruct((2, 2, 8, 64, half_rows), bf16)
    near = call(terms_kernel, near, 3, "hidden_terms", 1)(place, *heads, grad, core_grad)
    near = near.reshape(32, 64, half_rows)
    near = lax.all_to_all(near, ("sec", "vocab", "rows"), 0, 0, axis_index_groups=near_groups, tiled=True)
    far = jax.ShapeDtypeStruct((4, 64, half_rows), bf16)
    far = call(total_kernel, far, 2, "near_total")(near.reshape(4, 8, 64, half_rows))
    far = lax.all_to_all(far, "vocab", 0, 0, axis_index_groups=far_groups, tiled=True)
    hidden_grad = jax.ShapeDtypeStruct((1, 64, half_rows), bf16)
    hidden_grad = call(total_kernel, hidden_grad, 1, "far_total")(far[None]).transpose(0, 2, 1)

    block = lambda kind: jax.ShapeDtypeStruct((head_rows, width), kind)
    outs = (block(bf16),) * chips
    ahead_terms = call(weight_kernel, outs, 4, "weight_terms", 0, 4, [None, None, 1, 1], [1] * 4)(
        *columns, grad, core_grad
    )
    moved = [shifted(ahead_terms[j], j) for j in (2, 1, 3)]
    weight_grad = call(sum_kernel, block(bf16), 100, "weight_total", 0, 2, [0] * 4, [0])(ahead_terms[0], *moved)
    return hidden_grad, weight_grad


def solution(mesh):
    in_specs = (P("sec", "rows", "vocab"), P("rows", "sec"), P(("sec", "rows"), "vocab"))
    out_specs = (P("sec", "rows", "vocab"), P(("sec", "rows"), "vocab"))
    return jax.shard_map(body, mesh=mesh, in_specs=in_specs, out_specs=out_specs, check_vma=False)
```

time: 160 us -> 108 us (0.68)
  the two profiles are of different devices: /device:TPU:10 before, /device:TPU:2 now
where the time goes in v2:
time: 108 us; the launch traced here: 107 us
  starting transfers between devices  67.3 us (62%)
  waiting for transfers between devices  22.7 us (21%)
  Pallas kernels  12.4 us (11%)
  local copies, waits for them, and re-layouts  3.15 us (3%)
    all_to_all x1, starting transfers between devices, body(): parts = lax.all_to_all(copies, ('sec', 'vocab'), 0, 0, tiled=True)  17.7 us
    ppermute x3, starting transfers between devices, shifted(): return lax.ppermute(value, 'rows', pairs)  12.9 us
    ppermute x4, starting transfers between devices, spread(): return lax.ppermute(value, 'rows', pairs)  12.8 us
    pallas_call x6, Pallas kernels, run(): pl.pallas_call(kernel, out_shape=out_shape, grid=(grid,), in_specs=[pl.Bl...  10.2 us
    all_to_all x1, starting transfers between devices, body(): lax.all_to_all(far, 'vocab', 0, 0, axis_index_groups=far_groups, tiled=True)  8.86 us
    ppermute x3, waiting for transfers between devices, shifted(): return lax.ppermute(value, 'rows', pairs)  7.78 us
    all_to_all x1, waiting for transfers between devices, body(): parts = lax.all_to_all(copies, ('sec', 'vocab'), 0, 0, tiled=True)  7.12 us
    all_to_all x1, starting transfers between devices, body(): lax.all_to_all(near, ('sec', 'vocab', 'rows'), 0, 0, axis_index_groups=ne...  5.58 us
  transfers between devices with their start and end apart: 13, of which 5 were waited for; matrix products, arithmetic and copies ran while one was open for 1% of the time, Pallas kernels for 8%

profile of v2, /device:TPU:2, one launch (start us, length us, event | category | flops | bytes accessed | tf_op | source)
XLA Modules:
  0.0 107.2 jit_solution(17675736080160572519)
XLA Ops:
  0.6 4.0 %collective-permute-start = (bf16[256,2048]{1,0:T(8,128)(2,1)}, bf16[256,2048]{1,0:T(8,128)(2,1)S(1)}, u32[]{:S(2)}, u32[]{:S(2)}) collective-permute-start(bf16[256,2048]{1,0:T(8,128)(2,1)} %bitcast.12), channel_id=1, source_target_pairs={{0,256},{256,0},{1,257},{257,1},{2,258},{258,2},{3,259},{259,3},{4... | collective-permute-start | bytes 3145736 | tf_op jit(solution)/shard_map/ppermute | solution.py:178
  4.7 3.5 %collective-permute-start.2 = (bf16[128,2048]{1,0:T(8,128)(2,1)}, bf16[128,2048]{1,0:T(8,128)(2,1)S(1)}, u32[]{:S(2)}, u32[]{:S(2)}) collective-permute-start(bf16[128,2048]{1,0:T(8,128)(2,1)} %param.5), channel_id=1, source_target_pairs={{0,2},{1,6},{2,4},{3,0},{4,7},{5,3},{6,1},{7,5},{8,10},{9,14},{10,... | collective-permute-start | bytes 1572872 | tf_op jit(solution)/shard_map/ppermute | solution.py:27
  8.2 5.4 %collective-permute-start.1 = (bf16[128,2048]{1,0:T(8,128)(2,1)}, bf16[128,2048]{1,0:T(8,128)(2,1)}, u32[]{:S(2)}, u32[]{:S(2)}) collective-permute-start(bf16[128,2048]{1,0:T(8,128)(2,1)} %param.5), channel_id=1, source_target_pairs={{0,0},{1,4},{2,2},{3,6},{4,5},{5,1},{6,7},{7,3},{8,8},{9,12},{10,1... | collective-permute-start | bytes 1572872 | tf_op jit(solution)/shard_map/ppermute | solution.py:27
  13.6 1.2 %copy-done = bf16[1,256,2048]{2,1,0:T(8,128)(2,1)S(1)} copy-done((bf16[1,256,2048]{2,1,0:T(8,128)(2,1)S(1)}, bf16[1,256,2048]{2,1,0:T(8,128)(2,1)}, u32[]{:S(2)}) %copy-start) | copy-done | bytes 1048600
  14.8 1.4 %row_stats.1 = f32[64,2,256]{2,1,0:T(2,128)} custom-call(bf16[256,2048]{1,0:T(8,128)(2,1)S(1)} %bitcast.13), custom_call_target="tpu_custom_call" | custom-call | flops 3000000000 | bytes 9000000 | tf_op jit(solution)/shard_map/row_stats/pallas_call | solution.py:42
  16.2 17.7 %all-to-all-start = ((f32[64,2,256]{2,1,0:T(2,128)}), f32[64,2,256]{2,1,0:T(2,128)S(1)}, u32[]{:S(2)}, u32[]{:S(2)}) async-start(f32[64,2,256]{2,1,0:T(2,128)} %row_stats.1), calls=%async_computation | async-start | bytes 262144 | tf_op jit(solution)/shard_map/all_to_all | solution.py:192
  33.9 1.9 %collective-permute-start.4 = (bf16[128,2048]{1,0:T(8,128)(2,1)}, bf16[128,2048]{1,0:T(8,128)(2,1)}, u32[]{:S(2)}, u32[]{:S(2)}) collective-permute-start(bf16[128,2048]{1,0:T(8,128)(2,1)} %param.5), channel_id=1, source_target_pairs={{0,6},{1,2},{2,0},{3,4},{4,3},{5,7},{6,5},{7,1},{8,14},{9,10},{10,... | collective-permute-start | bytes 1572872 | tf_op jit(solution)/shard_map/ppermute | solution.py:27
  35.8 2.0 %collective-permute-start.3 = (bf16[128,2048]{1,0:T(8,128)(2,1)}, bf16[128,2048]{1,0:T(8,128)(2,1)}, u32[]{:S(2)}, u32[]{:S(2)}) collective-permute-start(bf16[128,2048]{1,0:T(8,128)(2,1)} %param.5), channel_id=1, source_target_pairs={{0,4},{1,0},{2,6},{3,2},{4,1},{5,5},{6,3},{7,7},{8,12},{9,8},{10,1... | collective-permute-start | bytes 1572872 | tf_op jit(solution)/shard_map/ppermute | solution.py:27
  38.9 3.5 %collective-permute-start.5 = (bf16[256,512]{1,0:T(8,128)(2,1)}, bf16[256,512]{1,0:T(8,128)(2,1)S(1)}, u32[]{:S(2)}, u32[]{:S(2)}) collective-permute-start(bf16[256,512]{1,0:T(8,128)(2,1)} %pad_maximum_fusion.1), channel_id=1, source_target_pairs={{0,1},{1,0},{2,3},{3,2},{4,5},{5,4},{6,7},{7,6},{8,9},{9,8},{10,11... | collective-permute-start | bytes 786440 | tf_op jit(solution)/shard_map/ppermute | solution.py:186
  42.5 7.1 %all-to-all-done = f32[64,2,256]{2,1,0:T(2,128)S(1)} async-done(((f32[64,2,256]{2,1,0:T(2,128)}), f32[64,2,256]{2,1,0:T(2,128)S(1)}, u32[]{:S(2)}, u32[]{:S(2)}) %all-to-all-start) | async-done | bytes 131104 | tf_op jit(solution)/shard_map/all_to_all | solution.py:192
  49.6 2.1 %logit_grad.1.refs_4_.own_ref = bf16[256,2048]{1,0:T(8,128)(2,1)S(1)} custom-call(s32[3]{0:T(128)S(1)} %pad_add_fusion.place_ref, f32[2,32,2,256]{3,2,1,0:T(2,128)S(1)} %bitcast.10, bf16[256,2048]{1,0:T(8,128)(2,1)S(1)} %bitcast.14, bf16[256,2048]{1,0:T(8,128)(2,1)S(1)} %collective-permute-done.peer_hbm), custom_call_target="tpu_custom_call" | custom-call | flops 40000000000 | bytes 120000000 | tf_op jit(solution)/shard_map/logit_grad/pallas_call | solution.py:117
  51.8 1.9 %collective-permute-start.6 = (bf16[256,2048]{1,0:T(8,128)(2,1)S(1)}, bf16[256,2048]{1,0:T(8,128)(2,1)S(1)}, u32[]{:S(2)}, u32[]{:S(2)}) collective-permute-start(bf16[256,2048]{1,0:T(8,128)(2,1)S(1)} %logit_grad.1.refs_4_.own_ref), channel_id=1, source_target_pairs={{0,1},{1,0},{2,3},{3,2},{4,5},{5,4},{6,7},{7,6},{8,9},{9,8},{10,11... | collective-permute-start | bytes 3145736 | tf_op jit(solution)/shard_map/ppermute | solution.py:199
  53.7 2.6 %collective-permute-done.6.refs_5_.core_ref = bf16[256,2048]{1,0:T(8,128)(2,1)S(1)} collective-permute-done((bf16[256,2048]{1,0:T(8,128)(2,1)S(1)}, bf16[256,2048]{1,0:T(8,128)(2,1)S(1)}, u32[]{:S(2)}, u32[]{:S(2)}) %collective-permute-start.6) | collective-permute-done | bytes 1048608 | tf_op jit(solution)/shard_map/ppermute | solution.py:199
  56.4 3.5 %hidden_terms.1 = bf16[2,2,8,64,128]{4,3,2,1,0:T(8,128)(2,1)} custom-call(s32[3]{0:T(128)S(1)} %pad_add_fusion.place_ref, bf16[128,2048]{1,0:T(8,128)(2,1)} %collective-permute-done.1.refs_0_, bf16[128,2048]{1,0:T(8,128)(2,1)S(1)} %collective-permute-done.2.refs_1_, bf16[128,2048]{1,0:T(8,128)(2,1)} %collective-permute-done.3.refs_2_, ...), custom_call_target="tpu_custom_call" | custom-call | flops 3000000000 | bytes 9000000 | tf_op jit(solution)/shard_map/hidden_terms/pallas_call | solution.py:42
  59.8 5.6 %all-to-all-start.1 = ((bf16[32,64,128]{2,1,0:T(8,128)(2,1)}), bf16[32,64,128]{2,1,0:T(8,128)(2,1)S(1)}, u32[]{:S(2)}, u32[]{:S(2)}) async-start(bf16[32,64,128]{2,1,0:T(8,128)(2,1)} %bitcast.5), calls=%async_computation.1 | async-start | bytes 1048576 | tf_op jit(solution)/shard_map/all_to_all | solution.py:203
  65.4 0.9 copy-done.5
  66.4 3.0 %weight_terms.1 = (bf16[128,2048]{1,0:T(8,128)(2,1)S(1)}, bf16[128,2048]{1,0:T(8,128)(2,1)}, bf16[128,2048]{1,0:T(8,128)(2,1)}, bf16[128,2048]{1,0:T(8,128)(2,1)S(1)}) custom-call(bf16[256,512]{1,0:T(8,128)(2,1)S(1)} %pad_maximum_fusion.own_columns_ref, bf16[256,512]{1,0:T(8,128)(2,1)S(1)} %copy-done.5, bf16[256,2048]{1,0:T(8,128)(2,1)S(1)} %copy-done.3, ...), custom_call_target="tpu_custom_call" | custom-call | flops 4000000000 | bytes 12000000 | tf_op jit(solution)/shard_map/weight_terms/pallas_call | solution.py:42
  70.2 5.8 %collective-permute-start.7 = (bf16[128,2048]{1,0:T(8,128)(2,1)}, bf16[128,2048]{1,0:T(8,128)(2,1)S(1)}, u32[]{:S(2)}, u32[]{:S(2)}) collective-permute-start(bf16[128,2048]{1,0:T(8,128)(2,1)} %get-tuple-element.27), channel_id=1, source_target_pairs={{0,4},{1,5},{2,6},{3,7},{4,0},{5,1},{6,2},{7,3},{8,12},{9,13},{10,... | collective-permute-start | bytes 1572872 | tf_op jit(solution)/shard_map/ppermute | solution.py:22
  76.1 2.9 %collective-permute-start.8 = (bf16[128,2048]{1,0:T(8,128)(2,1)}, bf16[128,2048]{1,0:T(8,128)(2,1)S(1)}, u32[]{:S(2)}, u32[]{:S(2)}) collective-permute-start(bf16[128,2048]{1,0:T(8,128)(2,1)} %get-tuple-element.28), channel_id=1, source_target_pairs={{0,2},{1,3},{2,4},{3,5},{4,6},{5,7},{6,0},{7,1},{8,10},{9,11},{10,... | collective-permute-start | bytes 1572872 | tf_op jit(solution)/shard_map/ppermute | solution.py:22
  79.0 4.1 %collective-permute-start.9 = (bf16[128,2048]{1,0:T(8,128)(2,1)S(1)}, bf16[128,2048]{1,0:T(8,128)(2,1)S(1)}, u32[]{:S(2)}, u32[]{:S(2)}) collective-permute-start(bf16[128,2048]{1,0:T(8,128)(2,1)S(1)} %get-tuple-element.29), channel_id=1, source_target_pairs={{0,6},{1,7},{2,0},{3,1},{4,2},{5,3},{6,4},{7,5},{8,14},{9,15},{10,... | collective-permute-start | bytes 1572872 | tf_op jit(solution)/shard_map/ppermute | solution.py:22
  83.9 8.9 %all-to-all-start.2 = ((bf16[4,64,128]{2,1,0:T(8,128)(2,1)}), bf16[4,64,128]{2,1,0:T(8,128)(2,1)S(1)}, u32[]{:S(2)}, u32[]{:S(2)}) async-start(bf16[4,64,128]{2,1,0:T(8,128)(2,1)} %near_total.1), calls=%async_computation.2 | async-start | bytes 131072 | tf_op jit(solution)/shard_map/all_to_all | solution.py:206
  92.7 7.0 %collective-permute-done.8.refs_2_ = bf16[128,2048]{1,0:T(8,128)(2,1)S(1)} collective-permute-done((bf16[128,2048]{1,0:T(8,128)(2,1)}, bf16[128,2048]{1,0:T(8,128)(2,1)S(1)}, u32[]{:S(2)}, u32[]{:S(2)}) %collective-permute-start.8) | collective-permute-done | bytes 524320 | tf_op jit(solution)/shard_map/ppermute | solution.py:22
  100.5 1.0 weight_total.1
  101.5 5.1 %all-to-all-done.2 = bf16[4,64,128]{2,1,0:T(8,128)(2,1)S(1)} async-done(((bf16[4,64,128]{2,1,0:T(8,128)(2,1)}), bf16[4,64,128]{2,1,0:T(8,128)(2,1)S(1)}, u32[]{:S(2)}, u32[]{:S(2)}) %all-to-all-start.2) | async-done | bytes 65568 | tf_op jit(solution)/shard_map/all_to_all | solution.py:206
  (31 shorter events, 3.9 us)
Async XLA Ops:
  0.6 41.9 %collective-permute-start = (bf16[256,2048]{1,0:T(8,128)(2,1)}, bf16[256,2048]{1,0:T(8,128)(2,1)S(1)}, u32[]{:S(2)}, u32[]{:S(2)}) collective-permute-start(bf16[256,2048]{1,0:T(8,128)(2,1)} %bitcast.12), channel_id=1, source_target_pairs={{0,256},{256,0},{1,257},{257,1},{2,258},{258,2},{3,259},{259,3},{4... | collective-permute-start | bytes 3145736 | tf_op jit(solution)/shard_map/ppermute | solution.py:178
  4.7 34.2 %collective-permute-start.2 = (bf16[128,2048]{1,0:T(8,128)(2,1)}, bf16[128,2048]{1,0:T(8,128)(2,1)S(1)}, u32[]{:S(2)}, u32[]{:S(2)}) collective-permute-start(bf16[128,2048]{1,0:T(8,128)(2,1)} %param.5), channel_id=1, source_target_pairs={{0,2},{1,6},{2,4},{3,0},{4,7},{5,3},{6,1},{7,5},{8,10},{9,14},{10,... | collective-permute-start | bytes 1572872 | tf_op jit(solution)/shard_map/ppermute | solution.py:27
  8.2 34.3 %collective-permute-start.1 = (bf16[128,2048]{1,0:T(8,128)(2,1)}, bf16[128,2048]{1,0:T(8,128)(2,1)}, u32[]{:S(2)}, u32[]{:S(2)}) collective-permute-start(bf16[128,2048]{1,0:T(8,128)(2,1)} %param.5), channel_id=1, source_target_pairs={{0,0},{1,4},{2,2},{3,6},{4,5},{5,1},{6,7},{7,3},{8,8},{9,12},{10,1... | collective-permute-start | bytes 1572872 | tf_op jit(solution)/shard_map/ppermute | solution.py:27
  13.6 1.2 %copy-start = (bf16[1,256,2048]{2,1,0:T(8,128)(2,1)S(1)}, bf16[1,256,2048]{2,1,0:T(8,128)(2,1)}, u32[]{:S(2)}) copy-start(bf16[1,256,2048]{2,1,0:T(8,128)(2,1)} %param.3) | copy-start | bytes 3145732
  14.8 23.2 %copy-start.8 = (bf16[256,1024]{1,0:T(8,128)(2,1)S(1)}, bf16[256,1024]{1,0:T(8,128)(2,1)}, u32[]{:S(2)}) copy-start(bf16[256,1024]{1,0:T(8,128)(2,1)} %param.4) | copy-start | bytes 1572868
  16.2 33.4 %all-to-all-start = ((f32[64,2,256]{2,1,0:T(2,128)}), f32[64,2,256]{2,1,0:T(2,128)S(1)}, u32[]{:S(2)}, u32[]{:S(2)}) async-start(f32[64,2,256]{2,1,0:T(2,128)} %row_stats.1), calls=%async_computation | async-start | bytes 262144 | tf_op jit(solution)/shard_map/all_to_all | solution.py:192
  33.9 17.9 %collective-permute-start.4 = (bf16[128,2048]{1,0:T(8,128)(2,1)}, bf16[128,2048]{1,0:T(8,128)(2,1)}, u32[]{:S(2)}, u32[]{:S(2)}) collective-permute-start(bf16[128,2048]{1,0:T(8,128)(2,1)} %param.5), channel_id=1, source_target_pairs={{0,6},{1,2},{2,0},{3,4},{4,3},{5,7},{6,5},{7,1},{8,14},{9,10},{10,... | collective-permute-start | bytes 1572872 | tf_op jit(solution)/shard_map/ppermute | solution.py:27
  35.8 16.0 %collective-permute-start.3 = (bf16[128,2048]{1,0:T(8,128)(2,1)}, bf16[128,2048]{1,0:T(8,128)(2,1)}, u32[]{:S(2)}, u32[]{:S(2)}) collective-permute-start(bf16[128,2048]{1,0:T(8,128)(2,1)} %param.5), channel_id=1, source_target_pairs={{0,4},{1,0},{2,6},{3,2},{4,1},{5,5},{6,3},{7,7},{8,12},{9,8},{10,1... | collective-permute-start | bytes 1572872 | tf_op jit(solution)/shard_map/ppermute | solution.py:27
  38.0 11.6 %copy-start.1 = (bf16[1,256,2048]{2,1,0:T(8,128)(2,1)S(1)}, bf16[1,256,2048]{2,1,0:T(8,128)(2,1)}, u32[]{:S(2)}) copy-start(bf16[1,256,2048]{2,1,0:T(8,128)(2,1)} %param.3) | copy-start | bytes 3145732
  38.9 12.8 %collective-permute-start.5 = (bf16[256,512]{1,0:T(8,128)(2,1)}, bf16[256,512]{1,0:T(8,128)(2,1)S(1)}, u32[]{:S(2)}, u32[]{:S(2)}) collective-permute-start(bf16[256,512]{1,0:T(8,128)(2,1)} %pad_maximum_fusion.1), channel_id=1, source_target_pairs={{0,1},{1,0},{2,3},{3,2},{4,5},{5,4},{6,7},{7,6},{8,9},{9,8},{10,11... | collective-permute-start | bytes 786440 | tf_op jit(solution)/shard_map/ppermute | solution.py:186
  51.7 8.1 %copy-start.2 = (bf16[256,2048]{1,0:T(8,128)(2,1)}, bf16[256,2048]{1,0:T(8,128)(2,1)S(1)}, u32[]{:S(2)}) copy-start(bf16[256,2048]{1,0:T(8,128)(2,1)S(1)} %logit_grad.1.refs_4_.own_ref) | copy-start | bytes 3145732
  51.8 8.1 %copy-start.4 = (bf16[256,512]{1,0:T(8,128)(2,1)}, bf16[256,512]{1,0:T(8,128)(2,1)S(1)}, u32[]{:S(2)}) copy-start(bf16[256,512]{1,0:T(8,128)(2,1)S(1)} %collective-permute-done.5.core_columns_ref) | copy-start | bytes 786436
  51.8 4.6 %collective-permute-start.6 = (bf16[256,2048]{1,0:T(8,128)(2,1)S(1)}, bf16[256,2048]{1,0:T(8,128)(2,1)S(1)}, u32[]{:S(2)}, u32[]{:S(2)}) collective-permute-start(bf16[256,2048]{1,0:T(8,128)(2,1)S(1)} %logit_grad.1.refs_4_.own_ref), channel_id=1, source_target_pairs={{0,1},{1,0},{2,3},{3,2},{4,5},{5,4},{6,7},{7,6},{8,9},{9,8},{10,11... | collective-permute-start | bytes 3145736 | tf_op jit(solution)/shard_map/ppermute | solution.py:199
  59.8 5.6 %copy-start.3 = (bf16[256,2048]{1,0:T(8,128)(2,1)S(1)}, bf16[256,2048]{1,0:T(8,128)(2,1)}, u32[]{:S(2)}) copy-start(bf16[256,2048]{1,0:T(8,128)(2,1)} %copy-done.2) | copy-start | bytes 3145732
  59.8 23.3 %all-to-all-start.1 = ((bf16[32,64,128]{2,1,0:T(8,128)(2,1)}), bf16[32,64,128]{2,1,0:T(8,128)(2,1)S(1)}, u32[]{:S(2)}, u32[]{:S(2)}) async-start(bf16[32,64,128]{2,1,0:T(8,128)(2,1)} %bitcast.5), calls=%async_computation.1 | async-start | bytes 1048576 | tf_op jit(solution)/shard_map/all_to_all | solution.py:203
  65.4 1.0 copy-start.5
  69.4 0.8 copy-start.6
  70.2 22.5 %collective-permute-start.7 = (bf16[128,2048]{1,0:T(8,128)(2,1)}, bf16[128,2048]{1,0:T(8,128)(2,1)S(1)}, u32[]{:S(2)}, u32[]{:S(2)}) collective-permute-start(bf16[128,2048]{1,0:T(8,128)(2,1)} %get-tuple-element.27), channel_id=1, source_target_pairs={{0,4},{1,5},{2,6},{3,7},{4,0},{5,1},{6,2},{7,3},{8,12},{9,13},{10,... | collective-permute-start | bytes 1572872 | tf_op jit(solution)/shard_map/ppermute | solution.py:22
  76.1 23.7 %collective-permute-start.8 = (bf16[128,2048]{1,0:T(8,128)(2,1)}, bf16[128,2048]{1,0:T(8,128)(2,1)S(1)}, u32[]{:S(2)}, u32[]{:S(2)}) collective-permute-start(bf16[128,2048]{1,0:T(8,128)(2,1)} %get-tuple-element.28), channel_id=1, source_target_pairs={{0,2},{1,3},{2,4},{3,5},{4,6},{5,7},{6,0},{7,1},{8,10},{9,11},{10,... | collective-permute-start | bytes 1572872 | tf_op jit(solution)/shard_map/ppermute | solution.py:22
  79.0 21.5 %collective-permute-start.9 = (bf16[128,2048]{1,0:T(8,128)(2,1)S(1)}, bf16[128,2048]{1,0:T(8,128)(2,1)S(1)}, u32[]{:S(2)}, u32[]{:S(2)}) collective-permute-start(bf16[128,2048]{1,0:T(8,128)(2,1)S(1)} %get-tuple-element.29), channel_id=1, source_target_pairs={{0,6},{1,7},{2,0},{3,1},{4,2},{5,3},{6,4},{7,5},{8,14},{9,15},{10,... | collective-permute-start | bytes 1572872 | tf_op jit(solution)/shard_map/ppermute | solution.py:22
  83.2 17.4 %copy-start.7 = (bf16[128,2048]{1,0:T(8,128)(2,1)S(1)}, bf16[128,2048]{1,0:T(8,128)(2,1)}, u32[]{:S(2)}) copy-start(bf16[128,2048]{1,0:T(8,128)(2,1)} %copy-done.6) | copy-start | bytes 1572868
  83.9 22.7 %all-to-all-start.2 = ((bf16[4,64,128]{2,1,0:T(8,128)(2,1)}), bf16[4,64,128]{2,1,0:T(8,128)(2,1)S(1)}, u32[]{:S(2)}, u32[]{:S(2)}) async-start(bf16[4,64,128]{2,1,0:T(8,128)(2,1)} %near_total.1), calls=%async_computation.2 | async-start | bytes 131072 | tf_op jit(solution)/shard_map/all_to_all | solution.py:206

commit v3 on v2

v3 whole, which is shorter than its diff:
```python
import jax
import jax.numpy as jnp
from jax import lax
from jax.experimental import pallas as pl
from jax.experimental.pallas import tpu as pltpu
from jax.sharding import PartitionSpec as P

loss_scale = 64.0
f32, bf16 = jnp.float32, jnp.bfloat16
swap_sec = [(0, 1), (1, 0)]
swap_core = [(i, i ^ 1) for i in range(8)]
near_groups = [
    [256 * sec + 8 * (8 * far + near) + 2 * y + core for sec in range(2) for core in range(2) for near in range(8)]
    for far in range(4)
    for y in range(4)
]
far_groups = [[8 * far + near for far in range(4)] for near in range(8)]


def shifted(value, distance):
    pairs = [(i, (i + 2 * distance) % 8) for i in range(8)]
    return lax.ppermute(value, "rows", pairs)


def spread(value, step):
    pairs = [(2 * y + o, (y + 2 * o + step) % 4 * 2 + y // 2) for y in range(4) for o in range(2)]
    return lax.ppermute(value, "rows", pairs)


def call(kernel, out_shape, micros, name, smem=0, grid=1, in_blocks=None, out_blocks=None, scratch=(), limit=24):
    def spec(array, dimension):
        if isinstance(dimension, pl.BlockSpec):
            return dimension
        block = list(array.shape)
        if dimension is not None:
            block[dimension] //= grid
        index = lambda i: tuple(i if d == dimension else 0 for d in range(len(block)))
        return pl.BlockSpec(tuple(block), index)

    def run(*args):
        cuts = in_blocks or [None] * (len(args) - smem)
        outs = jax.tree.leaves(out_shape)
        out_specs = [spec(o, d) for o, d in zip(outs, out_blocks or [None] * len(outs))]
        return pl.pallas_call(
            kernel,
            out_shape=out_shape,
            grid=(grid,),
            in_specs=[pl.BlockSpec(memory_space=pltpu.SMEM)] * smem
            + [spec(x, d) if grid > 1 else pl.BlockSpec(memory_space=pltpu.VMEM) for x, d in zip(args[smem:], cuts)],
            out_specs=out_specs if len(outs) > 1 else out_specs[0],
            scratch_shapes=scratch,
            compiler_params=pltpu.CompilerParams(vmem_limit_bytes=limit * 1024 * 1024),
            cost_estimate=pl.CostEstimate(flops=int(micros * 1.0e9), bytes_accessed=int(micros * 3.0e6), transcendentals=0),
            name=name,
        )(*args)

    return run


def row_of(column):
    return jnp.broadcast_to(column, (column.shape[0], 128)).T[0:1]


def stats_kernel(values_hbm, copies_ref, values_ref, sems):
    rows, width = values_ref.shape
    pieces = sems.shape[0]
    piece = rows // pieces
    copies = []
    for i in range(pieces):
        here = pl.ds(i * piece, piece)
        copies.append(pltpu.make_async_copy(values_hbm.at[here], values_ref.at[here], sems.at[i]))
        copies[i].start()
    tops, sums = [], []
    for i in range(pieces):
        copies[i].wait()
        here = slice(i * piece, i * piece + piece)
        highest = values_ref[here, 0:128]
        for c in range(128, width, 128):
            highest = jnp.maximum(highest, values_ref[here, c : c + 128])
        highest = jnp.max(highest.astype(f32), axis=1, keepdims=True)
        totals = jnp.zeros((piece, 128), f32)
        for c in range(0, width, 128):
            totals = totals + jnp.exp(values_ref[here, c : c + 128].astype(f32) - highest)
        tops.append(highest)
        sums.append(jnp.sum(totals, axis=1, keepdims=True))
    part = jnp.concatenate([row_of(jnp.concatenate(tops)), row_of(jnp.concatenate(sums))])
    copies_ref[...] = jnp.broadcast_to(part[None], copies_ref.shape)


def row_stats(values, copies, micros):
    pieces = 4
    return pl.pallas_call(
        stats_kernel,
        out_shape=jax.ShapeDtypeStruct((copies, 2, values.shape[0]), f32),
        in_specs=[pl.BlockSpec(memory_space=pltpu.HBM)],
        out_specs=pl.BlockSpec(memory_space=pltpu.VMEM),
        scratch_shapes=[pltpu.VMEM(values.shape, bf16), pltpu.SemaphoreType.DMA((pieces,))],
        compiler_params=pltpu.CompilerParams(vmem_limit_bytes=60 * 1024 * 1024),
        cost_estimate=pl.CostEstimate(flops=int(micros * 1.0e9), bytes_accessed=int(micros * 3.0e6), transcendentals=0),
        name="row_stats",
    )(values)


def grad_kernel(place_ref, parts_ref, hidden_ref, own_ref, peer_ref, pair_ref, columns_ref):
    section, chip, core = place_ref[0], place_ref[1], place_ref[2]
    rows, width = own_ref.shape
    for j in range(4):
        first = (chip + j) % 4 * 256
        cut = slice(j * 128, j * 128 + 128)
        columns_ref[:, cut] = hidden_ref[:, pl.ds(pl.multiple_of(first + core * 128, 128), 128)]
        other = hidden_ref[:, pl.ds(pl.multiple_of(first + (1 - core) * 128, 128), 128)]
        pair_ref[:, width + j * 128 : width + j * 128 + 128] = other

    def whole(which):
        highest, totals = parts_ref[which, :, 0], parts_ref[which, :, 1]
        top = jnp.max(highest, axis=0, keepdims=True)
        total = jnp.sum(totals * jnp.exp(highest - top), axis=0, keepdims=True)
        return jnp.broadcast_to(top, (128, rows)).T, jnp.broadcast_to(1.0 / total, (128, rows)).T

    own_tops, own_scales = whole(section)
    peer_tops, peer_scales = whole(1 - section)
    factor = loss_scale * (1 - 2 * section).astype(f32)
    piece = 64
    for first in range(0, rows, piece):
        for c in range(0, width, 128):
            cut = (slice(first, first + piece), slice(c, c + 128))
            own = jnp.exp(own_ref[cut].astype(f32) - own_tops[cut[0]]) * own_scales[cut[0]]
            peer = jnp.exp(peer_ref[cut].astype(f32) - peer_tops[cut[0]]) * peer_scales[cut[0]]
            difference = peer.astype(bf16).astype(f32) - own.astype(bf16).astype(f32)
            pair_ref[cut] = (factor * difference).astype(bf16)


def logit_grad(place, parts, hidden, own, peer, micros):
    rows, width = own.shape
    half = hidden.shape[1] // 2
    vmem = pl.BlockSpec(memory_space=pltpu.VMEM)
    return pl.pallas_call(
        grad_kernel,
        out_shape=(jax.ShapeDtypeStruct((rows, width + half), bf16), jax.ShapeDtypeStruct((rows, half), bf16)),
        in_specs=[pl.BlockSpec(memory_space=pltpu.SMEM), vmem, vmem, vmem, vmem],
        out_specs=(vmem, vmem),
        compiler_params=pltpu.CompilerParams(vmem_limit_bytes=24 * 1024 * 1024),
        cost_estimate=pl.CostEstimate(flops=int(micros * 1.0e9), bytes_accessed=int(micros * 3.0e6), transcendentals=0),
        name="logit_grad",
    )(place, parts, hidden, own, peer)


def weight_kernel(own_columns_ref, core_columns_ref, own_ref, core_ref, *out_refs):
    sides = (((0,), (0,)), ((), ()))
    terms = lax.dot_general(own_columns_ref[...], own_ref[...], sides, preferred_element_type=f32)
    terms = terms + lax.dot_general(core_columns_ref[...], core_ref[...], sides, preferred_element_type=f32)
    for j, ref in enumerate(out_refs):
        ref[...] = terms[j * 128 : j * 128 + 128].astype(ref.dtype)


def sum_kernel(*refs):
    total = refs[0][...].astype(f32)
    for ref in refs[1:-1]:
        total = total + ref[...].astype(f32)
    refs[-1][...] = total.astype(bf16)


def terms_of(place_ref, head_refs, grad_ref, store):
    chip, core = place_ref[1], place_ref[2]
    head = jnp.concatenate([ref[...] for ref in head_refs])
    grad = grad_ref[:, : head.shape[1]]
    terms = lax.dot_general(head, grad, (((1,), (1,)), ((), ())), preferred_element_type=f32)
    terms = terms.astype(bf16)
    for step in range(4):
        source = (chip + (8 - 2 * core) - step) % 4
        slot = source % 2 * 4 + source // 2 * 2
        for x in range(2):
            first = step * 128 + x * 64
            for s in range(2):
                store(s, slot + x, terms[first : first + 64, s * 128 : s * 128 + 128])


def own_terms_kernel(place_ref, *refs):
    def store(s, slot, terms):
        refs[5][s, slot] = terms

    terms_of(place_ref, refs[:4], refs[4], store)


def terms_kernel(place_ref, *refs):
    core, own_ref, out_ref = place_ref[2], refs[5], refs[6]

    def store(s, slot, terms):
        out_ref[s, 1 - core, slot] = terms

    for s in range(2):
        out_ref[s, core] = own_ref[s]
    terms_of(place_ref, refs[:4], refs[4], store)


def total_kernel(parts_ref, out_ref):
    total = parts_ref[:, 0].astype(f32)
    for i in range(1, parts_ref.shape[1]):
        total = total + parts_ref[:, i].astype(f32)
    out_ref[...] = total.astype(bf16)


def body(logits, hidden, head_weight):
    section = lax.axis_index("sec")
    core = lax.axis_index("rows") % 2
    chip = lax.axis_index("rows") // 2
    own = logits[0]
    rows, width = own.shape
    half_rows = rows // 2
    n_vocab = lax.axis_size("vocab")
    chips = lax.axis_size("rows") // 2
    head_rows = head_weight.shape[0]

    peer = lax.ppermute(own, "sec", swap_sec)
    heads = [spread(head_weight, step) for step in range(chips)]

    peer, heads[1], heads[3] = lax.optimization_barrier((peer, heads[1], heads[3]))

    copies = row_stats(own, 2 * n_vocab, 3)
    parts = lax.all_to_all(copies, ("sec", "vocab"), 0, 0, tiled=True)
    parts = parts.reshape(2, n_vocab, 2, rows)
    place = jnp.stack([section, chip, core]).astype(jnp.int32)
    pair, own_columns = logit_grad(place, parts, hidden, own, peer, 40)

    core_pair = lax.ppermute(pair, "rows", swap_core)
    own_terms = jax.ShapeDtypeStruct((2, 8, 64, half_rows), bf16)
    own_terms = call(own_terms_kernel, own_terms, 40, "own_terms", 1)(place, *heads, pair)
    near = jax.ShapeDtypeStruct((2, 2, 8, 64, half_rows), bf16)
    near = call(terms_kernel, near, 2, "hidden_terms", 1)(place, *heads, core_pair, own_terms)
    near = near.reshape(32, 64, half_rows)
    near = lax.all_to_all(near, ("sec", "vocab", "rows"), 0, 0, axis_index_groups=near_groups, tiled=True)
    far = jax.ShapeDtypeStruct((4, 64, half_rows), bf16)
    far = call(total_kernel, far, 2, "near_total")(near.reshape(4, 8, 64, half_rows))
    far = lax.all_to_all(far, "vocab", 0, 0, axis_index_groups=far_groups, tiled=True)
    hidden_grad = jax.ShapeDtypeStruct((1, 64, half_rows), bf16)
    hidden_grad = call(total_kernel, hidden_grad, 1, "far_total")(far[None]).transpose(0, 2, 1)

    block = lambda kind: jax.ShapeDtypeStruct((head_rows, width), kind)
    outs = (block(bf16),) * chips
    quarter = width // 4
    columns = pl.BlockSpec((rows, quarter), lambda i: (0, 4))
    tile = pl.BlockSpec((rows, quarter), lambda i: (0, i))
    ahead_terms = call(weight_kernel, outs, 4, "weight_terms", 0, 4, [None, columns, tile, tile], [1] * 4)(
        own_columns, core_pair, pair, core_pair
    )
    moved = [shifted(ahead_terms[j], j) for j in (2, 1, 3)]
    weight_grad = call(sum_kernel, block(bf16), 100, "weight_total", 0, 2, [0] * 4, [0])(ahead_terms[0], *moved)
    return hidden_grad, weight_grad


def solution(mesh):
    in_specs = (P("sec", "rows", "vocab"), P("rows", "sec"), P(("sec", "rows"), "vocab"))
    out_specs = (P("sec", "rows", "vocab"), P(("sec", "rows"), "vocab"))
    return jax.shard_map(body, mesh=mesh, in_specs=in_specs, out_specs=out_specs, check_vma=False)
```

time: 108 us -> 102 us (0.944)
  the two profiles are of different devices: /device:TPU:2 before, /device:TPU:1 now
where the time goes in v3:
time: 102 us; the launch traced here: 101 us
  starting transfers between devices  60 us (59%)
  waiting for transfers between devices  20.7 us (20%)
  Pallas kernels  15.2 us (15%)
  local copies, waits for them, and re-layouts  3.85 us (4%)
    all_to_all x1, starting transfers between devices, body(): parts = lax.all_to_all(copies, ('sec', 'vocab'), 0, 0, tiled=True)  16.4 us
    ppermute x4, starting transfers between devices, spread(): return lax.ppermute(value, 'rows', pairs)  15.4 us
    ppermute x3, waiting for transfers between devices, shifted(): return lax.ppermute(value, 'rows', pairs)  11.3 us
    pallas_call x6, Pallas kernels, run(): pl.pallas_call(kernel, out_shape=out_shape, grid=(grid,), in_specs=[pl.Bl...  10.5 us
    ppermute x3, starting transfers between devices, shifted(): return lax.ppermute(value, 'rows', pairs)  8.96 us
    all_to_all x1, waiting for transfers between devices, body(): parts = lax.all_to_all(copies, ('sec', 'vocab'), 0, 0, tiled=True)  6.05 us
    ppermute x1, starting transfers between devices, body(): peer = lax.ppermute(own, 'sec', swap_sec)  5.61 us
    ppermute x1, starting transfers between devices, body(): core_pair = lax.ppermute(pair, 'rows', swap_core)  4.88 us
  transfers between devices with their start and end apart: 12, of which 4 were waited for; matrix products, arithmetic and copies ran while one was open for 0% of the time, Pallas kernels for 12%

profile of v3, /device:TPU:1, one launch (start us, length us, event | category | flops | bytes accessed | tf_op | source)
XLA Modules:
  0.0 100.7 jit_solution(3544445292952913450)
XLA Ops:
  0.6 5.6 %collective-permute-start.1 = (bf16[256,2048]{1,0:T(8,128)(2,1)}, bf16[256,2048]{1,0:T(8,128)(2,1)S(1)}, u32[]{:S(2)}, u32[]{:S(2)}) collective-permute-start(bf16[256,2048]{1,0:T(8,128)(2,1)} %bitcast.12), channel_id=1, source_target_pairs={{0,256},{256,0},{1,257},{257,1},{2,258},{258,2},{3,259},{259,3},{4... | collective-permute-start | bytes 3145736 | tf_op jit(solution)/shard_map/ppermute | solution.py:214
  6.3 5.5 %collective-permute-start.2 = (bf16[128,2048]{1,0:T(8,128)(2,1)}, bf16[128,2048]{1,0:T(8,128)(2,1)S(1)}, u32[]{:S(2)}, u32[]{:S(2)}) collective-permute-start(bf16[128,2048]{1,0:T(8,128)(2,1)} %param.5), channel_id=1, source_target_pairs={{0,2},{1,6},{2,4},{3,0},{4,7},{5,3},{6,1},{7,5},{8,10},{9,14},{10,... | collective-permute-start | bytes 1572872 | tf_op jit(solution)/shard_map/ppermute | solution.py:27
  11.8 2.0 %collective-permute-start.3 = (bf16[128,2048]{1,0:T(8,128)(2,1)}, bf16[128,2048]{1,0:T(8,128)(2,1)}, u32[]{:S(2)}, u32[]{:S(2)}) collective-permute-start(bf16[128,2048]{1,0:T(8,128)(2,1)} %param.5), channel_id=1, source_target_pairs={{0,6},{1,2},{2,0},{3,4},{4,3},{5,7},{6,5},{7,1},{8,14},{9,10},{10,... | collective-permute-start | bytes 1572872 | tf_op jit(solution)/shard_map/ppermute | solution.py:27
  13.8 2.8 %row_stats.1 = f32[64,2,256]{2,1,0:T(2,128)} custom-call(bf16[256,2048]{1,0:T(8,128)(2,1)} %bitcast.13), custom_call_target="tpu_custom_call" | custom-call | flops 3000000000 | bytes 9000000 | tf_op jit(solution)/shard_map/row_stats/pallas_call | solution.py:92
  16.7 16.4 %all-to-all-start = ((f32[64,2,256]{2,1,0:T(2,128)}), f32[64,2,256]{2,1,0:T(2,128)S(1)}, u32[]{:S(2)}, u32[]{:S(2)}) async-start(f32[64,2,256]{2,1,0:T(2,128)} %row_stats.1), calls=%async_computation | async-start | bytes 262144 | tf_op jit(solution)/shard_map/all_to_all | solution.py:220
  33.1 2.9 %collective-permute-start = (bf16[128,2048]{1,0:T(8,128)(2,1)}, bf16[128,2048]{1,0:T(8,128)(2,1)}, u32[]{:S(2)}, u32[]{:S(2)}) collective-permute-start(bf16[128,2048]{1,0:T(8,128)(2,1)} %param.5), channel_id=1, source_target_pairs={{0,0},{1,4},{2,2},{3,6},{4,5},{5,1},{6,7},{7,3},{8,8},{9,12},{10,1... | collective-permute-start | bytes 1572872 | tf_op jit(solution)/shard_map/ppermute | solution.py:27
  35.9 5.0 %collective-permute-start.4 = (bf16[128,2048]{1,0:T(8,128)(2,1)}, bf16[128,2048]{1,0:T(8,128)(2,1)}, u32[]{:S(2)}, u32[]{:S(2)}) collective-permute-start(bf16[128,2048]{1,0:T(8,128)(2,1)} %param.5), channel_id=1, source_target_pairs={{0,4},{1,0},{2,6},{3,2},{4,1},{5,5},{6,3},{7,7},{8,12},{9,8},{10,1... | collective-permute-start | bytes 1572872 | tf_op jit(solution)/shard_map/ppermute | solution.py:27
  41.0 0.8 copy-done.4
  41.8 1.0 %copy-done.1 = bf16[256,2048]{1,0:T(8,128)(2,1)} copy-done((bf16[256,2048]{1,0:T(8,128)(2,1)}, bf16[256,2048]{1,0:T(8,128)(2,1)S(1)}, u32[]{:S(2)}) %copy-start.1) | copy-done | bytes 1048600
  42.8 6.0 %all-to-all-done = f32[64,2,256]{2,1,0:T(2,128)S(1)} async-done(((f32[64,2,256]{2,1,0:T(2,128)}), f32[64,2,256]{2,1,0:T(2,128)S(1)}, u32[]{:S(2)}, u32[]{:S(2)}) %all-to-all-start) | async-done | bytes 131104 | tf_op jit(solution)/shard_map/all_to_all | solution.py:220
  48.9 1.2 %copy-done.2 = bf16[256,2048]{1,0:T(8,128)(2,1)S(1)} copy-done((bf16[256,2048]{1,0:T(8,128)(2,1)S(1)}, bf16[256,2048]{1,0:T(8,128)(2,1)}, u32[]{:S(2)}) %copy-start.2) | copy-done | bytes 1048600
  50.1 1.9 %logit_grad.1 = (bf16[256,2560]{1,0:T(8,128)(2,1)S(1)}, bf16[256,512]{1,0:T(8,128)(2,1)S(1)}) custom-call(s32[3]{0:T(128)S(1)} %pad_add_fusion.place_ref, f32[2,32,2,256]{3,2,1,0:T(2,128)S(1)} %bitcast.10, bf16[256,1024]{1,0:T(8,128)(2,1)S(1)} %copy-done.3, bf16[256,2048]{1,0:T(8,128)(2,1)S(1)} %bitcast.14, bf16[256,2048]{1,0:T(8,128)(2,1)S(1)} %copy-done.2), custom_call_target="tpu_custom_call" | custom-call | flops 40000000000 | bytes 120000000 | tf_op jit(solution)/shard_map/logit_grad/pallas_call | solution.py:137
  52.0 4.9 %collective-permute-start.5 = (bf16[256,2560]{1,0:T(8,128)(2,1)S(1)}, bf16[256,2560]{1,0:T(8,128)(2,1)S(1)}, u32[]{:S(2)}, u32[]{:S(2)}) collective-permute-start(bf16[256,2560]{1,0:T(8,128)(2,1)S(1)} %get-tuple-element.14.refs_4_.own_ref), channel_id=1, source_target_pairs={{0,1},{1,0},{2,3},{3,2},{4,5},{5,4},{6,7},{7,6},{8,9},{9,8},{10,11... | collective-permute-start | bytes 3932168 | tf_op jit(solution)/shard_map/ppermute | solution.py:225
  56.9 2.1 %own_terms.1.refs_5_ = bf16[2,8,64,128]{3,2,1,0:T(8,128)(2,1)S(1)} custom-call(s32[3]{0:T(128)S(1)} %pad_add_fusion.place_ref, bf16[128,2048]{1,0:T(8,128)(2,1)} %collective-permute-done.refs_0_, bf16[128,2048]{1,0:T(8,128)(2,1)S(1)} %copy-done.5, bf16[128,2048]{1,0:T(8,128)(2,1)} %collective-permute-done.4.refs_2_, ...), custom_call_target="tpu_custom_call" | custom-call | flops 40000000000 | bytes 120000000 | tf_op jit(solution)/shard_map/own_terms/pallas_call | solution.py:44
  59.5 2.9 %hidden_terms.1 = bf16[2,2,8,64,128]{4,3,2,1,0:T(8,128)(2,1)} custom-call(s32[3]{0:T(128)S(1)} %pad_add_fusion.place_ref, bf16[128,2048]{1,0:T(8,128)(2,1)} %collective-permute-done.refs_0_, bf16[128,2048]{1,0:T(8,128)(2,1)S(1)} %copy-done.5, bf16[128,2048]{1,0:T(8,128)(2,1)} %collective-permute-done.4.refs_2_, ...), custom_call_target="tpu_custom_call" | custom-call | flops 2000000000 | bytes 6000000 | tf_op jit(solution)/shard_map/hidden_terms/pallas_call | solution.py:44
  62.5 4.0 %all-to-all-start.1 = ((bf16[32,64,128]{2,1,0:T(8,128)(2,1)}), bf16[32,64,128]{2,1,0:T(8,128)(2,1)S(1)}, u32[]{:S(2)}, u32[]{:S(2)}) async-start(bf16[32,64,128]{2,1,0:T(8,128)(2,1)} %bitcast.5), calls=%async_computation.1 | async-start | bytes 1048576 | tf_op jit(solution)/shard_map/all_to_all | solution.py:231
  66.5 3.2 %weight_terms.1 = (bf16[128,2048]{1,0:T(8,128)(2,1)S(1)}, bf16[128,2048]{1,0:T(8,128)(2,1)}, bf16[128,2048]{1,0:T(8,128)(2,1)}, bf16[128,2048]{1,0:T(8,128)(2,1)}) custom-call(bf16[256,512]{1,0:T(8,128)(2,1)S(1)} %copy-done.9, bf16[256,2560]{1,0:T(8,128)(2,1)S(1)} %collective-permute-done.5.refs_4_.core_columns_ref.core_ref, ...), custom_call_target="tpu_custom_call" | custom-call | flops 4000000000 | bytes 12000000 | tf_op jit(solution)/shard_map/weight_terms/pallas_call | solution.py:44
  70.4 2.5 %collective-permute-start.6 = (bf16[128,2048]{1,0:T(8,128)(2,1)}, bf16[128,2048]{1,0:T(8,128)(2,1)S(1)}, u32[]{:S(2)}, u32[]{:S(2)}) collective-permute-start(bf16[128,2048]{1,0:T(8,128)(2,1)} %get-tuple-element.17), channel_id=1, source_target_pairs={{0,4},{1,5},{2,6},{3,7},{4,0},{5,1},{6,2},{7,3},{8,12},{9,13},{10,... | collective-permute-start | bytes 1572872 | tf_op jit(solution)/shard_map/ppermute | solution.py:22
  72.9 2.0 %collective-permute-start.7 = (bf16[128,2048]{1,0:T(8,128)(2,1)}, bf16[128,2048]{1,0:T(8,128)(2,1)S(1)}, u32[]{:S(2)}, u32[]{:S(2)}) collective-permute-start(bf16[128,2048]{1,0:T(8,128)(2,1)} %get-tuple-element.18), channel_id=1, source_target_pairs={{0,2},{1,3},{2,4},{3,5},{4,6},{5,7},{6,0},{7,1},{8,10},{9,11},{10,... | collective-permute-start | bytes 1572872 | tf_op jit(solution)/shard_map/ppermute | solution.py:22
  74.9 4.5 %collective-permute-start.8 = (bf16[128,2048]{1,0:T(8,128)(2,1)}, bf16[128,2048]{1,0:T(8,128)(2,1)S(1)}, u32[]{:S(2)}, u32[]{:S(2)}) collective-permute-start(bf16[128,2048]{1,0:T(8,128)(2,1)} %get-tuple-element.19), channel_id=1, source_target_pairs={{0,6},{1,7},{2,0},{3,1},{4,2},{5,3},{6,4},{7,5},{8,14},{9,15},{10,... | collective-permute-start | bytes 1572872 | tf_op jit(solution)/shard_map/ppermute | solution.py:22
  79.4 2.8 %all-to-all-done.1 = bf16[32,64,128]{2,1,0:T(8,128)(2,1)S(1)} async-done(((bf16[32,64,128]{2,1,0:T(8,128)(2,1)}), bf16[32,64,128]{2,1,0:T(8,128)(2,1)S(1)}, u32[]{:S(2)}, u32[]{:S(2)}) %all-to-all-start.1) | async-done | bytes 524320 | tf_op jit(solution)/shard_map/all_to_all | solution.py:231
  82.9 4.9 %all-to-all-start.2 = ((bf16[4,64,128]{2,1,0:T(8,128)(2,1)}), bf16[4,64,128]{2,1,0:T(8,128)(2,1)S(1)}, u32[]{:S(2)}, u32[]{:S(2)}) async-start(bf16[4,64,128]{2,1,0:T(8,128)(2,1)} %near_total.1), calls=%async_computation.2 | async-start | bytes 131072 | tf_op jit(solution)/shard_map/all_to_all | solution.py:234
  87.8 11.3 %collective-permute-done.7.refs_2_ = bf16[128,2048]{1,0:T(8,128)(2,1)S(1)} collective-permute-done((bf16[128,2048]{1,0:T(8,128)(2,1)}, bf16[128,2048]{1,0:T(8,128)(2,1)S(1)}, u32[]{:S(2)}, u32[]{:S(2)}) %collective-permute-start.7) | collective-permute-done | bytes 524320 | tf_op jit(solution)/shard_map/ppermute | solution.py:22
  99.1 1.0 weight_total.1
  (29 shorter events, 2.7 us)
Async XLA Ops:
  0.6 48.2 %copy-start = (bf16[1,256,2048]{2,1,0:T(8,128)(2,1)S(1)}, bf16[1,256,2048]{2,1,0:T(8,128)(2,1)}, u32[]{:S(2)}) copy-start(bf16[1,256,2048]{2,1,0:T(8,128)(2,1)} %param.3) | copy-start | bytes 3145732
  0.6 48.2 %copy-start.3 = (bf16[256,1024]{1,0:T(8,128)(2,1)S(1)}, bf16[256,1024]{1,0:T(8,128)(2,1)}, u32[]{:S(2)}) copy-start(bf16[256,1024]{1,0:T(8,128)(2,1)} %hidden_ref.1) | copy-start | bytes 1572868
  0.6 41.2 %collective-permute-start.1 = (bf16[256,2048]{1,0:T(8,128)(2,1)}, bf16[256,2048]{1,0:T(8,128)(2,1)S(1)}, u32[]{:S(2)}, u32[]{:S(2)}) collective-permute-start(bf16[256,2048]{1,0:T(8,128)(2,1)} %bitcast.12), channel_id=1, source_target_pairs={{0,256},{256,0},{1,257},{257,1},{2,258},{258,2},{3,259},{259,3},{4... | collective-permute-start | bytes 3145736 | tf_op jit(solution)/shard_map/ppermute | solution.py:214
  6.3 34.7 %collective-permute-start.2 = (bf16[128,2048]{1,0:T(8,128)(2,1)}, bf16[128,2048]{1,0:T(8,128)(2,1)S(1)}, u32[]{:S(2)}, u32[]{:S(2)}) collective-permute-start(bf16[128,2048]{1,0:T(8,128)(2,1)} %param.5), channel_id=1, source_target_pairs={{0,2},{1,6},{2,4},{3,0},{4,7},{5,3},{6,1},{7,5},{8,10},{9,14},{10,... | collective-permute-start | bytes 1572872 | tf_op jit(solution)/shard_map/ppermute | solution.py:27
  11.8 30.0 %collective-permute-start.3 = (bf16[128,2048]{1,0:T(8,128)(2,1)}, bf16[128,2048]{1,0:T(8,128)(2,1)}, u32[]{:S(2)}, u32[]{:S(2)}) collective-permute-start(bf16[128,2048]{1,0:T(8,128)(2,1)} %param.5), channel_id=1, source_target_pairs={{0,6},{1,2},{2,0},{3,4},{4,3},{5,7},{6,5},{7,1},{8,14},{9,10},{10,... | collective-permute-start | bytes 1572872 | tf_op jit(solution)/shard_map/ppermute | solution.py:27
  16.7 32.2 %all-to-all-start = ((f32[64,2,256]{2,1,0:T(2,128)}), f32[64,2,256]{2,1,0:T(2,128)S(1)}, u32[]{:S(2)}, u32[]{:S(2)}) async-start(f32[64,2,256]{2,1,0:T(2,128)} %row_stats.1), calls=%async_computation | async-start | bytes 262144 | tf_op jit(solution)/shard_map/all_to_all | solution.py:220
  33.1 23.8 %collective-permute-start = (bf16[128,2048]{1,0:T(8,128)(2,1)}, bf16[128,2048]{1,0:T(8,128)(2,1)}, u32[]{:S(2)}, u32[]{:S(2)}) collective-permute-start(bf16[128,2048]{1,0:T(8,128)(2,1)} %param.5), channel_id=1, source_target_pairs={{0,0},{1,4},{2,2},{3,6},{4,5},{5,1},{6,7},{7,3},{8,8},{9,12},{10,1... | collective-permute-start | bytes 1572872 | tf_op jit(solution)/shard_map/ppermute | solution.py:27
  35.9 21.0 %collective-permute-start.4 = (bf16[128,2048]{1,0:T(8,128)(2,1)}, bf16[128,2048]{1,0:T(8,128)(2,1)}, u32[]{:S(2)}, u32[]{:S(2)}) collective-permute-start(bf16[128,2048]{1,0:T(8,128)(2,1)} %param.5), channel_id=1, source_target_pairs={{0,4},{1,0},{2,6},{3,2},{4,1},{5,5},{6,3},{7,7},{8,12},{9,8},{10,1... | collective-permute-start | bytes 1572872 | tf_op jit(solution)/shard_map/ppermute | solution.py:27
  41.0 0.8 copy-start.4
  41.8 1.0 %copy-start.1 = (bf16[256,2048]{1,0:T(8,128)(2,1)}, bf16[256,2048]{1,0:T(8,128)(2,1)S(1)}, u32[]{:S(2)}) copy-start(bf16[256,2048]{1,0:T(8,128)(2,1)S(1)} %collective-permute-done.1.peer_ref) | copy-start | bytes 3145732
  48.9 1.2 %copy-start.2 = (bf16[256,2048]{1,0:T(8,128)(2,1)S(1)}, bf16[256,2048]{1,0:T(8,128)(2,1)}, u32[]{:S(2)}) copy-start(bf16[256,2048]{1,0:T(8,128)(2,1)} %copy-done.1) | copy-start | bytes 3145732
  50.1 6.8 %copy-start.5 = (bf16[128,2048]{1,0:T(8,128)(2,1)S(1)}, bf16[128,2048]{1,0:T(8,128)(2,1)}, u32[]{:S(2)}) copy-start(bf16[128,2048]{1,0:T(8,128)(2,1)} %copy-done.4) | copy-start | bytes 1572868
  52.0 7.1 %copy-start.8 = (bf16[256,512]{1,0:T(8,128)(2,1)}, bf16[256,512]{1,0:T(8,128)(2,1)S(1)}, u32[]{:S(2)}) copy-start(bf16[256,512]{1,0:T(8,128)(2,1)S(1)} %get-tuple-element.15.own_columns_ref) | copy-start | bytes 786436
  52.0 7.5 %collective-permute-start.5 = (bf16[256,2560]{1,0:T(8,128)(2,1)S(1)}, bf16[256,2560]{1,0:T(8,128)(2,1)S(1)}, u32[]{:S(2)}, u32[]{:S(2)}) collective-permute-start(bf16[256,2560]{1,0:T(8,128)(2,1)S(1)} %get-tuple-element.14.refs_4_.own_ref), channel_id=1, source_target_pairs={{0,1},{1,0},{2,3},{3,2},{4,5},{5,4},{6,7},{7,6},{8,9},{9,8},{10,11... | collective-permute-start | bytes 3932168 | tf_op jit(solution)/shard_map/ppermute | solution.py:225
  59.5 6.9 %copy-start.9 = (bf16[256,512]{1,0:T(8,128)(2,1)S(1)}, bf16[256,512]{1,0:T(8,128)(2,1)}, u32[]{:S(2)}) copy-start(bf16[256,512]{1,0:T(8,128)(2,1)} %copy-done.8) | copy-start | bytes 786436
  62.5 19.7 %all-to-all-start.1 = ((bf16[32,64,128]{2,1,0:T(8,128)(2,1)}), bf16[32,64,128]{2,1,0:T(8,128)(2,1)S(1)}, u32[]{:S(2)}, u32[]{:S(2)}) async-start(bf16[32,64,128]{2,1,0:T(8,128)(2,1)} %bitcast.5), calls=%async_computation.1 | async-start | bytes 1048576 | tf_op jit(solution)/shard_map/all_to_all | solution.py:231
  69.6 0.8 copy-start.6
  70.4 17.4 %collective-permute-start.6 = (bf16[128,2048]{1,0:T(8,128)(2,1)}, bf16[128,2048]{1,0:T(8,128)(2,1)S(1)}, u32[]{:S(2)}, u32[]{:S(2)}) collective-permute-start(bf16[128,2048]{1,0:T(8,128)(2,1)} %get-tuple-element.17), channel_id=1, source_target_pairs={{0,4},{1,5},{2,6},{3,7},{4,0},{5,1},{6,2},{7,3},{8,12},{9,13},{10,... | collective-permute-start | bytes 1572872 | tf_op jit(solution)/shard_map/ppermute | solution.py:22
  72.9 26.2 %collective-permute-start.7 = (bf16[128,2048]{1,0:T(8,128)(2,1)}, bf16[128,2048]{1,0:T(8,128)(2,1)S(1)}, u32[]{:S(2)}, u32[]{:S(2)}) collective-permute-start(bf16[128,2048]{1,0:T(8,128)(2,1)} %get-tuple-element.18), channel_id=1, source_target_pairs={{0,2},{1,3},{2,4},{3,5},{4,6},{5,7},{6,0},{7,1},{8,10},{9,11},{10,... | collective-permute-start | bytes 1572872 | tf_op jit(solution)/shard_map/ppermute | solution.py:22
  74.9 24.2 %collective-permute-start.8 = (bf16[128,2048]{1,0:T(8,128)(2,1)}, bf16[128,2048]{1,0:T(8,128)(2,1)S(1)}, u32[]{:S(2)}, u32[]{:S(2)}) collective-permute-start(bf16[128,2048]{1,0:T(8,128)(2,1)} %get-tuple-element.19), channel_id=1, source_target_pairs={{0,6},{1,7},{2,0},{3,1},{4,2},{5,3},{6,4},{7,5},{8,14},{9,15},{10,... | collective-permute-start | bytes 1572872 | tf_op jit(solution)/shard_map/ppermute | solution.py:22
  82.2 16.9 %copy-start.7 = (bf16[128,2048]{1,0:T(8,128)(2,1)S(1)}, bf16[128,2048]{1,0:T(8,128)(2,1)}, u32[]{:S(2)}) copy-start(bf16[128,2048]{1,0:T(8,128)(2,1)} %copy-done.6) | copy-start | bytes 1572868
  82.9 17.2 %all-to-all-start.2 = ((bf16[4,64,128]{2,1,0:T(8,128)(2,1)}), bf16[4,64,128]{2,1,0:T(8,128)(2,1)S(1)}, u32[]{:S(2)}, u32[]{:S(2)}) async-start(bf16[4,64,128]{2,1,0:T(8,128)(2,1)} %near_total.1), calls=%async_computation.2 | async-start | bytes 131072 | tf_op jit(solution)/shard_map/all_to_all | solution.py:234

commit v4 on v3

--- a/solution.py
+++ b/solution.py
@@ -27,7 +27,7 @@
     return lax.ppermute(value, "rows", pairs)
 
 
-def call(kernel, out_shape, micros, name, smem=0, grid=1, in_blocks=None, out_blocks=None, scratch=(), limit=24):
+def call(kernel, out_shape, micros, name, smem=0, grid=1, in_blocks=None, out_blocks=None, scratch=(), limit=24, whole=False):
     def spec(array, dimension):
         if isinstance(dimension, pl.BlockSpec):
             return dimension
@@ -41,12 +41,14 @@
         cuts = in_blocks or [None] * (len(args) - smem)
         outs = jax.tree.leaves(out_shape)
         out_specs = [spec(o, d) for o, d in zip(outs, out_blocks or [None] * len(outs))]
+        if whole:
+            out_specs = [pl.BlockSpec(memory_space=pltpu.VMEM)] * len(outs)
         return pl.pallas_call(
             kernel,
             out_shape=out_shape,
             grid=(grid,),
             in_specs=[pl.BlockSpec(memory_space=pltpu.SMEM)] * smem
-            + [spec(x, d) if grid > 1 else pl.BlockSpec(memory_space=pltpu.VMEM) for x, d in zip(args[smem:], cuts)],
+            + [spec(x, d) if grid > 1 or d else pl.BlockSpec(memory_space=pltpu.VMEM) for x, d in zip(args[smem:], cuts)],
             out_specs=out_specs if len(outs) > 1 else out_specs[0],
             scratch_shapes=scratch,
             compiler_params=pltpu.CompilerParams(vmem_limit_bytes=limit * 1024 * 1024),
@@ -70,7 +72,7 @@
         here = pl.ds(i * piece, piece)
         copies.append(pltpu.make_async_copy(values_hbm.at[here], values_ref.at[here], sems.at[i]))
         copies[i].start()
-    tops, sums = [], []
+    parts = []
     for i in range(pieces):
         copies[i].wait()
         here = slice(i * piece, i * piece + piece)
@@ -81,14 +83,14 @@
         totals = jnp.zeros((piece, 128), f32)
         for c in range(0, width, 128):
             totals = totals + jnp.exp(values_ref[here, c : c + 128].astype(f32) - highest)
-        tops.append(highest)
-        sums.append(jnp.sum(totals, axis=1, keepdims=True))
-    part = jnp.concatenate([row_of(jnp.concatenate(tops)), row_of(jnp.concatenate(sums))])
+        totals = jnp.sum(totals, axis=1, keepdims=True)
+        parts.append(jnp.concatenate([row_of(highest), row_of(totals)]))
+    part = jnp.concatenate(parts, axis=1)
     copies_ref[...] = jnp.broadcast_to(part[None], copies_ref.shape)
 
 
 def row_stats(values, copies, micros):
-    pieces = 4
+    pieces = 2
     return pl.pallas_call(
         stats_kernel,
         out_shape=jax.ShapeDtypeStruct((copies, 2, values.shape[0]), f32),
@@ -145,12 +147,15 @@
     )(place, parts, hidden, own, peer)
 
 
-def weight_kernel(own_columns_ref, core_columns_ref, own_ref, core_ref, *out_refs):
+def weight_kernel(own_columns_ref, own_ref, core_ref, *out_refs):
     sides = (((0,), (0,)), ((), ()))
-    terms = lax.dot_general(own_columns_ref[...], own_ref[...], sides, preferred_element_type=f32)
-    terms = terms + lax.dot_general(core_columns_ref[...], core_ref[...], sides, preferred_element_type=f32)
-    for j, ref in enumerate(out_refs):
-        ref[...] = terms[j * 128 : j * 128 + 128].astype(ref.dtype)
+    width = out_refs[0].shape[1]
+    for first in range(0, width, 512):
+        cut = slice(first, first + 512)
+        terms = lax.dot_general(own_columns_ref[...], own_ref[:, cut], sides, preferred_element_type=f32)
+        terms = terms + lax.dot_general(core_ref[:, width:], core_ref[:, cut], sides, preferred_element_type=f32)
+        for j, ref in enumerate(out_refs):
+            ref[:, cut] = terms[j * 128 : j * 128 + 128].astype(ref.dtype)
 
 
 def sum_kernel(*refs):
@@ -160,9 +165,8 @@
     refs[-1][...] = total.astype(bf16)
 
 
-def terms_of(place_ref, head_refs, grad_ref, store):
+def terms_of(place_ref, head, grad_ref, store):
     chip, core = place_ref[1], place_ref[2]
-    head = jnp.concatenate([ref[...] for ref in head_refs])
     grad = grad_ref[:, : head.shape[1]]
     terms = lax.dot_general(head, grad, (((1,), (1,)), ((), ())), preferred_element_type=f32)
     terms = terms.astype(bf16)
@@ -176,21 +180,46 @@
 
 
 def own_terms_kernel(place_ref, *refs):
+    grad_ref, out_ref, head_ref = refs[4:]
+    for i in range(4):
+        head_ref[i * 128 : i * 128 + 128] = refs[i][...]
+
     def store(s, slot, terms):
-        refs[5][s, slot] = terms
-
-    terms_of(place_ref, refs[:4], refs[4], store)
-
-
-def terms_kernel(place_ref, *refs):
-    core, own_ref, out_ref = place_ref[2], refs[5], refs[6]
+        out_ref[s, slot] = terms
+
+    terms_of(place_ref, head_ref[...], grad_ref, store)
+
+
+def terms_kernel(place_ref, head_ref, grad_ref, own_ref, unread_ref, out_hbm, terms_ref, sems):
+    core = place_ref[2]
 
     def store(s, slot, terms):
-        out_ref[s, 1 - core, slot] = terms
-
+        terms_ref[s, slot] = terms
+
+    copies = [pltpu.make_async_copy(own_ref.at[s], out_hbm.at[s, core], sems.at[s]) for s in range(2)]
+    for copy in copies:
+        copy.start()
+    terms_of(place_ref, head_ref[...], grad_ref, store)
     for s in range(2):
-        out_ref[s, core] = own_ref[s]
-    terms_of(place_ref, refs[:4], refs[4], store)
+        copies.append(pltpu.make_async_copy(terms_ref.at[s], out_hbm.at[s, 1 - core], sems.at[2 + s]))
+        copies[-1].start()
+    for copy in copies:
+        copy.wait()
+
+
+def hidden_terms(place, head, grad, own_terms, unread, micros):
+    vmem, anywhere = pl.BlockSpec(memory_space=pltpu.VMEM), pl.BlockSpec(memory_space=pl.ANY)
+    shape = own_terms.shape
+    return pl.pallas_call(
+        terms_kernel,
+        out_shape=jax.ShapeDtypeStruct((shape[0], 2) + shape[1:], bf16),
+        in_specs=[pl.BlockSpec(memory_space=pltpu.SMEM), vmem, vmem, vmem, anywhere],
+        out_specs=pl.BlockSpec(memory_space=pltpu.HBM),
+        scratch_shapes=[pltpu.VMEM(shape, bf16), pltpu.SemaphoreType.DMA((4,))],
+        compiler_params=pltpu.CompilerParams(vmem_limit_bytes=24 * 1024 * 1024),
+        cost_estimate=pl.CostEstimate(flops=int(micros * 1.0e9), bytes_accessed=int(micros * 3.0e6), transcendentals=0),
+        name="hidden_terms",
+    )(place, head, grad, own_terms, unread)
 
 
 def total_kernel(parts_ref, out_ref):
@@ -224,9 +253,12 @@
 
     core_pair = lax.ppermute(pair, "rows", swap_core)
     own_terms = jax.ShapeDtypeStruct((2, 8, 64, half_rows), bf16)
-    own_terms = call(own_terms_kernel, own_terms, 40, "own_terms", 1)(place, *heads, pair)
-    near = jax.ShapeDtypeStruct((2, 2, 8, 64, half_rows), bf16)
-    near = call(terms_kernel, near, 2, "hidden_terms", 1)(place, *heads, core_pair, own_terms)
+    head = jax.ShapeDtypeStruct((chips * head_rows, width), bf16)
+    own_terms, head = call(own_terms_kernel, (own_terms, head), 40, "own_terms", 1, whole=True)(place, *heads, pair)
+    block = lambda kind: jax.ShapeDtypeStruct((head_rows, width), kind)
+    outs = (block(bf16),) * chips
+    ahead_terms = call(weight_kernel, outs, 4, "weight_terms")(own_columns, pair, core_pair)
+    near = hidden_terms(place, head, core_pair, own_terms, ahead_terms[0], 2)
     near = near.reshape(32, 64, half_rows)
     near = lax.all_to_all(near, ("sec", "vocab", "rows"), 0, 0, axis_index_groups=near_groups, tiled=True)
     far = jax.ShapeDtypeStruct((4, 64, half_rows), bf16)
@@ -235,14 +267,6 @@
     hidden_grad = jax.ShapeDtypeStruct((1, 64, half_rows), bf16)
     hidden_grad = call(total_kernel, hidden_grad, 1, "far_total")(far[None]).transpose(0, 2, 1)
 
-    block = lambda kind: jax.ShapeDtypeStruct((head_rows, width), kind)
-    outs = (block(bf16),) * chips
-    quarter = width // 4
-    columns = pl.BlockSpec((rows, quarter), lambda i: (0, 4))
-    tile = pl.BlockSpec((rows, quarter), lambda i: (0, i))
-    ahead_terms = call(weight_kernel, outs, 4, "weight_terms", 0, 4, [None, columns, tile, tile], [1] * 4)(
-        own_columns, core_pair, pair, core_pair
-    )
     moved = [shifted(ahead_terms[j], j) for j in (2, 1, 3)]
     weight_grad = call(sum_kernel, block(bf16), 100, "weight_total", 0, 2, [0] * 4, [0])(ahead_terms[0], *moved)
     return hidden_grad, weight_grad

time: 102 us -> 102 us (level)
  waiting for transfers between devices: 20.7 us -> 24.4 us
  local copies, waits for them, and re-layouts: 3.85 us -> 1.06 us
  Pallas kernels: 15.2 us -> 13 us
  starting transfers between devices: 60 us -> 61.3 us
    ppermute x3, waiting for transfers between devices: 11.3 us -> 5.95 us  [shifted(): return lax.ppermute(value, 'rows', pairs)]
    all_to_all x1, waiting for transfers between devices: 2.81 us -> 6.75 us  [body(): lax.all_to_all(near, ('sec', 'vocab', 'rows'), 0, 0, axis_index_groups=ne...]
    pallas_call x6 -> x5, Pallas kernels: 10.5 us -> 6.63 us  [run(): pl.pallas_call(kernel, out_shape=out_shape, grid=(grid,), in_specs=[pl.Bl...]
    all_to_all x1, waiting for transfers between devices: 0.01 us -> 3.32 us  [body(): lax.all_to_all(far, 'vocab', 0, 0, axis_index_groups=far_groups, tiled=True)]
    unnamed x20 -> x8, local copies, waits for them, and re-layouts: 3.85 us -> 1.06 us
    pallas_call x0 -> x1, Pallas kernels: none -> 2.03 us  [hidden_terms(): pl.pallas_call(terms_kernel, out_shape=jax.ShapeDtypeStruct((shape[0], 2)...]
    all_to_all x1, waiting for transfers between devices: 6.05 us -> 7.88 us  [body(): parts = lax.all_to_all(copies, ('sec', 'vocab'), 0, 0, tiled=True)]
    all_to_all x1, starting transfers between devices: 4.86 us -> 6.09 us  [body(): lax.all_to_all(far, 'vocab', 0, 0, axis_index_groups=far_groups, tiled=True)]
  transfers between devices with their start and end apart: 12 -> 12, of which waited for: 4 -> 5; matrix products, arithmetic and copies ran while one was open for 0% -> 0% of each run, Pallas kernels for 12% -> 9%
where the time goes in v4:
time: 102 us; the launch traced here: 101 us
  starting transfers between devices  61.3 us (60%)
  waiting for transfers between devices  24.4 us (24%)
  Pallas kernels  13 us (13%)
  local copies, waits for them, and re-layouts  1.06 us (1%)
    all_to_all x1, starting transfers between devices, body(): parts = lax.all_to_all(copies, ('sec', 'vocab'), 0, 0, tiled=True)  16.4 us
    ppermute x4, starting transfers between devices, spread(): return lax.ppermute(value, 'rows', pairs)  15.3 us
    ppermute x3, starting transfers between devices, shifted(): return lax.ppermute(value, 'rows', pairs)  8.99 us
    all_to_all x1, waiting for transfers between devices, body(): parts = lax.all_to_all(copies, ('sec', 'vocab'), 0, 0, tiled=True)  7.88 us
    all_to_all x1, waiting for transfers between devices, body(): lax.all_to_all(near, ('sec', 'vocab', 'rows'), 0, 0, axis_index_groups=ne...  6.75 us
    pallas_call x5, Pallas kernels, run(): pl.pallas_call(kernel, out_shape=out_shape, grid=(grid,), in_specs=[pl.Bl...  6.63 us
    all_to_all x1, starting transfers between devices, body(): lax.all_to_all(far, 'vocab', 0, 0, axis_index_groups=far_groups, tiled=True)  6.09 us
    ppermute x3, waiting for transfers between devices, shifted(): return lax.ppermute(value, 'rows', pairs)  5.95 us
  transfers between devices with their start and end apart: 12, of which 5 were waited for; matrix products, arithmetic and copies ran while one was open for 0% of the time, Pallas kernels for 9%

profile of v4, /device:TPU:1, one launch (start us, length us, event | category | flops | bytes accessed | tf_op | source)
XLA Modules:
  0.0 100.6 jit_solution(15468799581814073641)
XLA Ops:
  0.6 5.6 %collective-permute-start.1 = (bf16[256,2048]{1,0:T(8,128)(2,1)}, bf16[256,2048]{1,0:T(8,128)(2,1)S(1)}, u32[]{:S(2)}, u32[]{:S(2)}) collective-permute-start(bf16[256,2048]{1,0:T(8,128)(2,1)} %bitcast.12), channel_id=1, source_target_pairs={{0,256},{256,0},{1,257},{257,1},{2,258},{258,2},{3,259},{259,3},{4... | collective-permute-start | bytes 3145736 | tf_op jit(solution)/shard_map/ppermute | solution.py:243
  6.3 5.5 %collective-permute-start.2 = (bf16[128,2048]{1,0:T(8,128)(2,1)}, bf16[128,2048]{1,0:T(8,128)(2,1)S(1)}, u32[]{:S(2)}, u32[]{:S(2)}) collective-permute-start(bf16[128,2048]{1,0:T(8,128)(2,1)} %param.5), channel_id=1, source_target_pairs={{0,2},{1,6},{2,4},{3,0},{4,7},{5,3},{6,1},{7,5},{8,10},{9,14},{10,... | collective-permute-start | bytes 1572872 | tf_op jit(solution)/shard_map/ppermute | solution.py:27
  11.8 2.0 %collective-permute-start.3 = (bf16[128,2048]{1,0:T(8,128)(2,1)}, bf16[128,2048]{1,0:T(8,128)(2,1)}, u32[]{:S(2)}, u32[]{:S(2)}) collective-permute-start(bf16[128,2048]{1,0:T(8,128)(2,1)} %param.5), channel_id=1, source_target_pairs={{0,6},{1,2},{2,0},{3,4},{4,3},{5,7},{6,5},{7,1},{8,14},{9,10},{10,... | collective-permute-start | bytes 1572872 | tf_op jit(solution)/shard_map/ppermute | solution.py:27
  13.8 2.5 %row_stats.1 = f32[64,2,256]{2,1,0:T(2,128)} custom-call(bf16[256,2048]{1,0:T(8,128)(2,1)} %bitcast.13), custom_call_target="tpu_custom_call" | custom-call | flops 3000000000 | bytes 9000000 | tf_op jit(solution)/shard_map/row_stats/pallas_call | solution.py:94
  16.3 16.4 %all-to-all-start = ((f32[64,2,256]{2,1,0:T(2,128)}), f32[64,2,256]{2,1,0:T(2,128)S(1)}, u32[]{:S(2)}, u32[]{:S(2)}) async-start(f32[64,2,256]{2,1,0:T(2,128)} %row_stats.1), calls=%async_computation | async-start | bytes 262144 | tf_op jit(solution)/shard_map/all_to_all | solution.py:249
  32.7 2.9 %collective-permute-start = (bf16[128,2048]{1,0:T(8,128)(2,1)}, bf16[128,2048]{1,0:T(8,128)(2,1)}, u32[]{:S(2)}, u32[]{:S(2)}) collective-permute-start(bf16[128,2048]{1,0:T(8,128)(2,1)} %param.5), channel_id=1, source_target_pairs={{0,0},{1,4},{2,2},{3,6},{4,5},{5,1},{6,7},{7,3},{8,8},{9,12},{10,1... | collective-permute-start | bytes 1572872 | tf_op jit(solution)/shard_map/ppermute | solution.py:27
  35.6 4.9 %collective-permute-start.4 = (bf16[128,2048]{1,0:T(8,128)(2,1)}, bf16[128,2048]{1,0:T(8,128)(2,1)}, u32[]{:S(2)}, u32[]{:S(2)}) collective-permute-start(bf16[128,2048]{1,0:T(8,128)(2,1)} %param.5), channel_id=1, source_target_pairs={{0,4},{1,0},{2,6},{3,2},{4,1},{5,5},{6,3},{7,7},{8,12},{9,8},{10,1... | collective-permute-start | bytes 1572872 | tf_op jit(solution)/shard_map/ppermute | solution.py:27
  40.7 7.9 %all-to-all-done = f32[64,2,256]{2,1,0:T(2,128)S(1)} async-done(((f32[64,2,256]{2,1,0:T(2,128)}), f32[64,2,256]{2,1,0:T(2,128)S(1)}, u32[]{:S(2)}, u32[]{:S(2)}) %all-to-all-start) | async-done | bytes 131104 | tf_op jit(solution)/shard_map/all_to_all | solution.py:249
  48.5 1.9 %logit_grad.1 = (bf16[256,2560]{1,0:T(8,128)(2,1)S(1)}, bf16[256,512]{1,0:T(8,128)(2,1)S(1)}) custom-call(s32[3]{0:T(128)S(1)} %pad_add_fusion.place_ref, f32[2,32,2,256]{3,2,1,0:T(2,128)S(1)} %bitcast.10, bf16[256,1024]{1,0:T(8,128)(2,1)S(1)} %copy-done.1, bf16[256,2048]{1,0:T(8,128)(2,1)S(1)} %bitcast.14, bf16[256,2048]{1,0:T(8,128)(2,1)S(1)} %collective-permute-done.1.peer_ref), custom_call_target="tpu_custom_call" | custom-call | flops 40000000000 | bytes 120000000 | tf_op jit(solution)/shard_map/logit_grad/pallas_call | solution.py:139
  50.4 4.9 %collective-permute-start.5 = (bf16[256,2560]{1,0:T(8,128)(2,1)S(1)}, bf16[256,2560]{1,0:T(8,128)(2,1)S(1)}, u32[]{:S(2)}, u32[]{:S(2)}) collective-permute-start(bf16[256,2560]{1,0:T(8,128)(2,1)S(1)} %get-tuple-element.16.refs_4_.own_ref), channel_id=1, source_target_pairs={{0,1},{1,0},{2,3},{3,2},{4,5},{5,4},{6,7},{7,6},{8,9},{9,8},{10,11... | collective-permute-start | bytes 3932168 | tf_op jit(solution)/shard_map/ppermute | solution.py:254
  55.3 2.1 %own_terms.1 = (bf16[2,8,64,128]{3,2,1,0:T(8,128)(2,1)S(1)}, bf16[512,2048]{1,0:T(8,128)(2,1)S(1)}) custom-call(s32[3]{0:T(128)S(1)} %pad_add_fusion.place_ref, bf16[128,2048]{1,0:T(8,128)(2,1)} %collective-permute-done.refs_0_, bf16[128,2048]{1,0:T(8,128)(2,1)S(1)} %collective-permute-done.2.refs_1_, bf16[128,2048]{1,0:T(8,128)(2,1)} %collective-permute-done.4.refs_2_, ...), custom_call_target="tpu_custom_call" | custom-call | flops 40000000000 | bytes 120000000 | tf_op jit(solution)/shard_map/own_terms/pallas_call | solution.py:46
  57.9 1.3 %weight_terms.1 = (bf16[128,2048]{1,0:T(8,128)(2,1)S(1)}, bf16[128,2048]{1,0:T(8,128)(2,1)S(1)}, bf16[128,2048]{1,0:T(8,128)(2,1)S(1)}, bf16[128,2048]{1,0:T(8,128)(2,1)S(1)}) custom-call(bf16[256,512]{1,0:T(8,128)(2,1)S(1)} %get-tuple-element.19.own_columns_ref, bf16[256,2560]{1,0:T(8,128)(2,1)S(1)} %get-tuple-element.16.refs_4_.own_ref, ...), custom_call_target="tpu_custom_call" | custom-call | flops 4000000000 | bytes 12000000 | tf_op jit(solution)/shard_map/weight_terms/pallas_call | solution.py:46
  59.2 2.0 %hidden_terms.1 = bf16[2,2,8,64,128]{4,3,2,1,0:T(8,128)(2,1)} custom-call(s32[3]{0:T(128)S(1)} %pad_add_fusion.place_ref, bf16[512,2048]{1,0:T(8,128)(2,1)S(1)} %get-tuple-element.17.head_ref, bf16[256,2560]{1,0:T(8,128)(2,1)S(1)} %collective-permute-done.5.core_ref.grad_ref, bf16[2,8,64,128]{3,2,1,0:T(8,128)(2,1)S(1)} %get-tuple-element.18.own_ref, ...), custom_call_target="tpu_custom_call" | custom-call | flops 2000000000 | bytes 6000000 | tf_op jit(solution)/shard_map/hidden_terms/pallas_call | solution.py:213
  61.3 4.0 %all-to-all-start.1 = ((bf16[32,64,128]{2,1,0:T(8,128)(2,1)}), bf16[32,64,128]{2,1,0:T(8,128)(2,1)S(1)}, u32[]{:S(2)}, u32[]{:S(2)}) async-start(bf16[32,64,128]{2,1,0:T(8,128)(2,1)} %bitcast.5), calls=%async_computation.1 | async-start | bytes 1048576 | tf_op jit(solution)/shard_map/all_to_all | solution.py:263
  65.3 2.5 %collective-permute-start.6 = (bf16[128,2048]{1,0:T(8,128)(2,1)S(1)}, bf16[128,2048]{1,0:T(8,128)(2,1)S(1)}, u32[]{:S(2)}, u32[]{:S(2)}) collective-permute-start(bf16[128,2048]{1,0:T(8,128)(2,1)S(1)} %get-tuple-element.21), channel_id=1, source_target_pairs={{0,4},{1,5},{2,6},{3,7},{4,0},{5,1},{6,2},{7,3},{8,12},{9,13},{10,... | collective-permute-start | bytes 1572872 | tf_op jit(solution)/shard_map/ppermute | solution.py:22
  67.8 2.0 %collective-permute-start.7 = (bf16[128,2048]{1,0:T(8,128)(2,1)S(1)}, bf16[128,2048]{1,0:T(8,128)(2,1)S(1)}, u32[]{:S(2)}, u32[]{:S(2)}) collective-permute-start(bf16[128,2048]{1,0:T(8,128)(2,1)S(1)} %get-tuple-element.22), channel_id=1, source_target_pairs={{0,2},{1,3},{2,4},{3,5},{4,6},{5,7},{6,0},{7,1},{8,10},{9,11},{10,... | collective-permute-start | bytes 1572872 | tf_op jit(solution)/shard_map/ppermute | solution.py:22
  69.8 4.5 %collective-permute-start.8 = (bf16[128,2048]{1,0:T(8,128)(2,1)S(1)}, bf16[128,2048]{1,0:T(8,128)(2,1)}, u32[]{:S(2)}, u32[]{:S(2)}) collective-permute-start(bf16[128,2048]{1,0:T(8,128)(2,1)S(1)} %get-tuple-element.23), channel_id=1, source_target_pairs={{0,6},{1,7},{2,0},{3,1},{4,2},{5,3},{6,4},{7,5},{8,14},{9,15},{10,... | collective-permute-start | bytes 1572872 | tf_op jit(solution)/shard_map/ppermute | solution.py:22
  74.3 6.7 %all-to-all-done.1 = bf16[32,64,128]{2,1,0:T(8,128)(2,1)S(1)} async-done(((bf16[32,64,128]{2,1,0:T(8,128)(2,1)}), bf16[32,64,128]{2,1,0:T(8,128)(2,1)S(1)}, u32[]{:S(2)}, u32[]{:S(2)}) %all-to-all-start.1) | async-done | bytes 524320 | tf_op jit(solution)/shard_map/all_to_all | solution.py:263
  81.0 0.7 near_total.1
  81.7 6.1 %all-to-all-start.2 = ((bf16[4,64,128]{2,1,0:T(8,128)(2,1)}), bf16[4,64,128]{2,1,0:T(8,128)(2,1)S(1)}, u32[]{:S(2)}, u32[]{:S(2)}) async-start(bf16[4,64,128]{2,1,0:T(8,128)(2,1)} %near_total.1), calls=%async_computation.2 | async-start | bytes 131072 | tf_op jit(solution)/shard_map/all_to_all | solution.py:266
  87.8 5.9 %collective-permute-done.7.refs_2_ = bf16[128,2048]{1,0:T(8,128)(2,1)S(1)} collective-permute-done((bf16[128,2048]{1,0:T(8,128)(2,1)S(1)}, bf16[128,2048]{1,0:T(8,128)(2,1)S(1)}, u32[]{:S(2)}, u32[]{:S(2)}) %collective-permute-start.7) | collective-permute-done | bytes 524320 | tf_op jit(solution)/shard_map/ppermute | solution.py:22
  93.7 1.0 %copy-done.3 = bf16[128,2048]{1,0:T(8,128)(2,1)S(1)} copy-done((bf16[128,2048]{1,0:T(8,128)(2,1)S(1)}, bf16[128,2048]{1,0:T(8,128)(2,1)}, u32[]{:S(2)}) %copy-start.3) | copy-done | bytes 524312
  94.8 1.9 %weight_total.1 = bf16[128,2048]{1,0:T(8,128)(2,1)} custom-call(bf16[128,2048]{1,0:T(8,128)(2,1)S(1)} %copy-done.3, bf16[128,2048]{1,0:T(8,128)(2,1)S(1)} %collective-permute-done.6.refs_1_, bf16[128,2048]{1,0:T(8,128)(2,1)S(1)} %collective-permute-done.7.refs_2_, bf16[128,2048]{1,0:T(8,128)(2,1)} %collective-permute-done.8.refs_3_), custom_call_target="tpu_custom_call" | custom-call | flops 99999997952 | bytes 300000000 | tf_op jit(solution)/shard_map/weight_total/pallas_call | solution.py:46
  96.7 3.3 %all-to-all-done.2 = bf16[4,64,128]{2,1,0:T(8,128)(2,1)S(1)} async-done(((bf16[4,64,128]{2,1,0:T(8,128)(2,1)}), bf16[4,64,128]{2,1,0:T(8,128)(2,1)S(1)}, u32[]{:S(2)}, u32[]{:S(2)}) %all-to-all-start.2) | async-done | bytes 65568 | tf_op jit(solution)/shard_map/all_to_all | solution.py:266
  (17 shorter events, 1.2 us)
Async XLA Ops:
  0.6 47.9 %copy-start = (bf16[1,256,2048]{2,1,0:T(8,128)(2,1)S(1)}, bf16[1,256,2048]{2,1,0:T(8,128)(2,1)}, u32[]{:S(2)}) copy-start(bf16[1,256,2048]{2,1,0:T(8,128)(2,1)} %param.3) | copy-start | bytes 3145732
  0.6 47.9 %copy-start.1 = (bf16[256,1024]{1,0:T(8,128)(2,1)S(1)}, bf16[256,1024]{1,0:T(8,128)(2,1)}, u32[]{:S(2)}) copy-start(bf16[256,1024]{1,0:T(8,128)(2,1)} %hidden_ref.1) | copy-start | bytes 1572868
  0.6 40.0 %collective-permute-start.1 = (bf16[256,2048]{1,0:T(8,128)(2,1)}, bf16[256,2048]{1,0:T(8,128)(2,1)S(1)}, u32[]{:S(2)}, u32[]{:S(2)}) collective-permute-start(bf16[256,2048]{1,0:T(8,128)(2,1)} %bitcast.12), channel_id=1, source_target_pairs={{0,256},{256,0},{1,257},{257,1},{2,258},{258,2},{3,259},{259,3},{4... | collective-permute-start | bytes 3145736 | tf_op jit(solution)/shard_map/ppermute | solution.py:243
  6.3 34.4 %collective-permute-start.2 = (bf16[128,2048]{1,0:T(8,128)(2,1)}, bf16[128,2048]{1,0:T(8,128)(2,1)S(1)}, u32[]{:S(2)}, u32[]{:S(2)}) collective-permute-start(bf16[128,2048]{1,0:T(8,128)(2,1)} %param.5), channel_id=1, source_target_pairs={{0,2},{1,6},{2,4},{3,0},{4,7},{5,3},{6,1},{7,5},{8,10},{9,14},{10,... | collective-permute-start | bytes 1572872 | tf_op jit(solution)/shard_map/ppermute | solution.py:27
  11.8 28.9 %collective-permute-start.3 = (bf16[128,2048]{1,0:T(8,128)(2,1)}, bf16[128,2048]{1,0:T(8,128)(2,1)}, u32[]{:S(2)}, u32[]{:S(2)}) collective-permute-start(bf16[128,2048]{1,0:T(8,128)(2,1)} %param.5), channel_id=1, source_target_pairs={{0,6},{1,2},{2,0},{3,4},{4,3},{5,7},{6,5},{7,1},{8,14},{9,10},{10,... | collective-permute-start | bytes 1572872 | tf_op jit(solution)/shard_map/ppermute | solution.py:27
  16.3 32.2 %all-to-all-start = ((f32[64,2,256]{2,1,0:T(2,128)}), f32[64,2,256]{2,1,0:T(2,128)S(1)}, u32[]{:S(2)}, u32[]{:S(2)}) async-start(f32[64,2,256]{2,1,0:T(2,128)} %row_stats.1), calls=%async_computation | async-start | bytes 262144 | tf_op jit(solution)/shard_map/all_to_all | solution.py:249
  32.7 22.6 %collective-permute-start = (bf16[128,2048]{1,0:T(8,128)(2,1)}, bf16[128,2048]{1,0:T(8,128)(2,1)}, u32[]{:S(2)}, u32[]{:S(2)}) collective-permute-start(bf16[128,2048]{1,0:T(8,128)(2,1)} %param.5), channel_id=1, source_target_pairs={{0,0},{1,4},{2,2},{3,6},{4,5},{5,1},{6,7},{7,3},{8,8},{9,12},{10,1... | collective-permute-start | bytes 1572872 | tf_op jit(solution)/shard_map/ppermute | solution.py:27
  35.6 19.7 %collective-permute-start.4 = (bf16[128,2048]{1,0:T(8,128)(2,1)}, bf16[128,2048]{1,0:T(8,128)(2,1)}, u32[]{:S(2)}, u32[]{:S(2)}) collective-permute-start(bf16[128,2048]{1,0:T(8,128)(2,1)} %param.5), channel_id=1, source_target_pairs={{0,4},{1,0},{2,6},{3,2},{4,1},{5,5},{6,3},{7,7},{8,12},{9,8},{10,1... | collective-permute-start | bytes 1572872 | tf_op jit(solution)/shard_map/ppermute | solution.py:27
  50.4 7.5 %collective-permute-start.5 = (bf16[256,2560]{1,0:T(8,128)(2,1)S(1)}, bf16[256,2560]{1,0:T(8,128)(2,1)S(1)}, u32[]{:S(2)}, u32[]{:S(2)}) collective-permute-start(bf16[256,2560]{1,0:T(8,128)(2,1)S(1)} %get-tuple-element.16.refs_4_.own_ref), channel_id=1, source_target_pairs={{0,1},{1,0},{2,3},{3,2},{4,5},{5,4},{6,7},{7,6},{8,9},{9,8},{10,11... | collective-permute-start | bytes 3932168 | tf_op jit(solution)/shard_map/ppermute | solution.py:254
  59.2 2.0 %copy-start.2 = (bf16[128,2048]{1,0:T(8,128)(2,1)}, bf16[128,2048]{1,0:T(8,128)(2,1)S(1)}, u32[]{:S(2)}) copy-start(bf16[128,2048]{1,0:T(8,128)(2,1)S(1)} %get-tuple-element.20.unread_ref.refs_0_) | copy-start | bytes 1572868
  61.3 19.7 %all-to-all-start.1 = ((bf16[32,64,128]{2,1,0:T(8,128)(2,1)}), bf16[32,64,128]{2,1,0:T(8,128)(2,1)S(1)}, u32[]{:S(2)}, u32[]{:S(2)}) async-start(bf16[32,64,128]{2,1,0:T(8,128)(2,1)} %bitcast.5), calls=%async_computation.1 | async-start | bytes 1048576 | tf_op jit(solution)/shard_map/all_to_all | solution.py:263
  65.3 22.5 %collective-permute-start.6 = (bf16[128,2048]{1,0:T(8,128)(2,1)S(1)}, bf16[128,2048]{1,0:T(8,128)(2,1)S(1)}, u32[]{:S(2)}, u32[]{:S(2)}) collective-permute-start(bf16[128,2048]{1,0:T(8,128)(2,1)S(1)} %get-tuple-element.21), channel_id=1, source_target_pairs={{0,4},{1,5},{2,6},{3,7},{4,0},{5,1},{6,2},{7,3},{8,12},{9,13},{10,... | collective-permute-start | bytes 1572872 | tf_op jit(solution)/shard_map/ppermute | solution.py:22
  67.8 26.0 %collective-permute-start.7 = (bf16[128,2048]{1,0:T(8,128)(2,1)S(1)}, bf16[128,2048]{1,0:T(8,128)(2,1)S(1)}, u32[]{:S(2)}, u32[]{:S(2)}) collective-permute-start(bf16[128,2048]{1,0:T(8,128)(2,1)S(1)} %get-tuple-element.22), channel_id=1, source_target_pairs={{0,2},{1,3},{2,4},{3,5},{4,6},{5,7},{6,0},{7,1},{8,10},{9,11},{10,... | collective-permute-start | bytes 1572872 | tf_op jit(solution)/shard_map/ppermute | solution.py:22
  69.8 24.0 %collective-permute-start.8 = (bf16[128,2048]{1,0:T(8,128)(2,1)S(1)}, bf16[128,2048]{1,0:T(8,128)(2,1)}, u32[]{:S(2)}, u32[]{:S(2)}) collective-permute-start(bf16[128,2048]{1,0:T(8,128)(2,1)S(1)} %get-tuple-element.23), channel_id=1, source_target_pairs={{0,6},{1,7},{2,0},{3,1},{4,2},{5,3},{6,4},{7,5},{8,14},{9,15},{10,... | collective-permute-start | bytes 1572872 | tf_op jit(solution)/shard_map/ppermute | solution.py:22
  81.7 18.3 %all-to-all-start.2 = ((bf16[4,64,128]{2,1,0:T(8,128)(2,1)}), bf16[4,64,128]{2,1,0:T(8,128)(2,1)S(1)}, u32[]{:S(2)}, u32[]{:S(2)}) async-start(bf16[4,64,128]{2,1,0:T(8,128)(2,1)} %near_total.1), calls=%async_computation.2 | async-start | bytes 131072 | tf_op jit(solution)/shard_map/all_to_all | solution.py:266
  93.7 1.0 %copy-start.3 = (bf16[128,2048]{1,0:T(8,128)(2,1)S(1)}, bf16[128,2048]{1,0:T(8,128)(2,1)}, u32[]{:S(2)}) copy-start(bf16[128,2048]{1,0:T(8,128)(2,1)} %copy-done.2) | copy-start | bytes 1572868

commit v5 on v4

--- a/solution.py
+++ b/solution.py
@@ -72,25 +72,29 @@
         here = pl.ds(i * piece, piece)
         copies.append(pltpu.make_async_copy(values_hbm.at[here], values_ref.at[here], sems.at[i]))
         copies[i].start()
-    parts = []
+    tops, sums = [], []
     for i in range(pieces):
         copies[i].wait()
         here = slice(i * piece, i * piece + piece)
-        highest = values_ref[here, 0:128]
+        lanes = values_ref[here, 0:128]
         for c in range(128, width, 128):
-            highest = jnp.maximum(highest, values_ref[here, c : c + 128])
-        highest = jnp.max(highest.astype(f32), axis=1, keepdims=True)
+            lanes = jnp.maximum(lanes, values_ref[here, c : c + 128])
+        lanes = lanes.astype(f32)
         totals = jnp.zeros((piece, 128), f32)
         for c in range(0, width, 128):
-            totals = totals + jnp.exp(values_ref[here, c : c + 128].astype(f32) - highest)
-        totals = jnp.sum(totals, axis=1, keepdims=True)
-        parts.append(jnp.concatenate([row_of(highest), row_of(totals)]))
-    part = jnp.concatenate(parts, axis=1)
+            totals = totals + jnp.exp(values_ref[here, c : c + 128].astype(f32) - lanes)
+        tops.append(lanes)
+        sums.append(totals)
+    lanes = jnp.concatenate(tops).T
+    totals = jnp.concatenate(sums).T
+    highest = jnp.max(lanes, axis=0, keepdims=True)
+    total = jnp.sum(totals * jnp.exp(lanes - highest), axis=0, keepdims=True)
+    part = jnp.concatenate([highest, total])
     copies_ref[...] = jnp.broadcast_to(part[None], copies_ref.shape)
 
 
 def row_stats(values, copies, micros):
-    pieces = 2
+    pieces = 4
     return pl.pallas_call(
         stats_kernel,
         out_shape=jax.ShapeDtypeStruct((copies, 2, values.shape[0]), f32),
@@ -190,7 +194,7 @@
     terms_of(place_ref, head_ref[...], grad_ref, store)
 
 
-def terms_kernel(place_ref, head_ref, grad_ref, own_ref, unread_ref, out_hbm, terms_ref, sems):
+def terms_kernel(place_ref, head_ref, grad_ref, own_ref, out_hbm, terms_ref, sems):
     core = place_ref[2]
 
     def store(s, slot, terms):
@@ -207,19 +211,19 @@
         copy.wait()
 
 
-def hidden_terms(place, head, grad, own_terms, unread, micros):
-    vmem, anywhere = pl.BlockSpec(memory_space=pltpu.VMEM), pl.BlockSpec(memory_space=pl.ANY)
+def hidden_terms(place, head, grad, own_terms, micros):
+    vmem = pl.BlockSpec(memory_space=pltpu.VMEM)
     shape = own_terms.shape
     return pl.pallas_call(
         terms_kernel,
         out_shape=jax.ShapeDtypeStruct((shape[0], 2) + shape[1:], bf16),
-        in_specs=[pl.BlockSpec(memory_space=pltpu.SMEM), vmem, vmem, vmem, anywhere],
+        in_specs=[pl.BlockSpec(memory_space=pltpu.SMEM), vmem, vmem, vmem],
         out_specs=pl.BlockSpec(memory_space=pltpu.HBM),
         scratch_shapes=[pltpu.VMEM(shape, bf16), pltpu.SemaphoreType.DMA((4,))],
         compiler_params=pltpu.CompilerParams(vmem_limit_bytes=24 * 1024 * 1024),
         cost_estimate=pl.CostEstimate(flops=int(micros * 1.0e9), bytes_accessed=int(micros * 3.0e6), transcendentals=0),
         name="hidden_terms",
-    )(place, head, grad, own_terms, unread)
+    )(place, head, grad, own_terms)
 
 
 def total_kernel(parts_ref, out_ref):
@@ -258,7 +262,7 @@
     block = lambda kind: jax.ShapeDtypeStruct((head_rows, width), kind)
     outs = (block(bf16),) * chips
     ahead_terms = call(weight_kernel, outs, 4, "weight_terms")(own_columns, pair, core_pair)
-    near = hidden_terms(place, head, core_pair, own_terms, ahead_terms[0], 2)
+    near = hidden_terms(place, head, core_pair, own_terms, 2)
     near = near.reshape(32, 64, half_rows)
     near = lax.all_to_all(near, ("sec", "vocab", "rows"), 0, 0, axis_index_groups=near_groups, tiled=True)
     far = jax.ShapeDtypeStruct((4, 64, half_rows), bf16)

time: 102 us -> 100 us (0.980)
  waiting for transfers between devices: 24.4 us -> 21.6 us
  local copies, waits for them, and re-layouts: 1.06 us -> 3.84 us
  starting transfers between devices: 61.3 us -> 60 us
    ppermute x3, waiting for transfers between devices: 5.95 us -> 10.6 us  [shifted(): return lax.ppermute(value, 'rows', pairs)]
    all_to_all x1, waiting for transfers between devices: 6.75 us -> 3.58 us  [body(): lax.all_to_all(near, ('sec', 'vocab', 'rows'), 0, 0, axis_index_groups=ne...]
    unnamed x8 -> x20, local copies, waits for them, and re-layouts: 1.06 us -> 3.84 us
    all_to_all x1, waiting for transfers between devices: 3.32 us -> 0.91 us  [body(): lax.all_to_all(far, 'vocab', 0, 0, axis_index_groups=far_groups, tiled=True)]
    all_to_all x1, waiting for transfers between devices: 7.88 us -> 6.07 us  [body(): parts = lax.all_to_all(copies, ('sec', 'vocab'), 0, 0, tiled=True)]
    all_to_all x1, starting transfers between devices: 6.09 us -> 4.86 us  [body(): lax.all_to_all(far, 'vocab', 0, 0, axis_index_groups=far_groups, tiled=True)]
  transfers between devices with their start and end apart: 12 -> 12, of which waited for: 5 -> 5; matrix products, arithmetic and copies ran while one was open for 0% -> 0% of each run, Pallas kernels for 9% -> 10%
where the time goes in v5:
time: 100 us; the launch traced here: 99.3 us
  starting transfers between devices  60 us (60%)
  waiting for transfers between devices  21.6 us (22%)
  Pallas kernels  12.9 us (13%)
  local copies, waits for them, and re-layouts  3.84 us (4%)
    all_to_all x1, starting transfers between devices, body(): parts = lax.all_to_all(copies, ('sec', 'vocab'), 0, 0, tiled=True)  16.4 us
    ppermute x4, starting transfers between devices, spread(): return lax.ppermute(value, 'rows', pairs)  15.3 us
    ppermute x3, waiting for transfers between devices, shifted(): return lax.ppermute(value, 'rows', pairs)  10.6 us
    ppermute x3, starting transfers between devices, shifted(): return lax.ppermute(value, 'rows', pairs)  8.96 us
    pallas_call x5, Pallas kernels, run(): pl.pallas_call(kernel, out_shape=out_shape, grid=(grid,), in_specs=[pl.Bl...  6.78 us
    all_to_all x1, waiting for transfers between devices, body(): parts = lax.all_to_all(copies, ('sec', 'vocab'), 0, 0, tiled=True)  6.07 us
    ppermute x1, starting transfers between devices, body(): peer = lax.ppermute(own, 'sec', swap_sec)  5.61 us
    ppermute x1, starting transfers between devices, body(): core_pair = lax.ppermute(pair, 'rows', swap_core)  4.88 us
  transfers between devices with their start and end apart: 12, of which 5 were waited for; matrix products, arithmetic and copies ran while one was open for 0% of the time, Pallas kernels for 10%

profile of v5, /device:TPU:1, one launch (start us, length us, event | category | flops | bytes accessed | tf_op | source)
XLA Modules:
  0.0 99.3 jit_solution(9519794835048841142)
XLA Ops:
  0.6 5.6 %collective-permute-start.1 = (bf16[256,2048]{1,0:T(8,128)(2,1)}, bf16[256,2048]{1,0:T(8,128)(2,1)S(1)}, u32[]{:S(2)}, u32[]{:S(2)}) collective-permute-start(bf16[256,2048]{1,0:T(8,128)(2,1)} %bitcast.12), channel_id=1, source_target_pairs={{0,256},{256,0},{1,257},{257,1},{2,258},{258,2},{3,259},{259,3},{4... | collective-permute-start | bytes 3145736 | tf_op jit(solution)/shard_map/ppermute | solution.py:247
  6.3 5.5 %collective-permute-start.2 = (bf16[128,2048]{1,0:T(8,128)(2,1)}, bf16[128,2048]{1,0:T(8,128)(2,1)S(1)}, u32[]{:S(2)}, u32[]{:S(2)}) collective-permute-start(bf16[128,2048]{1,0:T(8,128)(2,1)} %param.5), channel_id=1, source_target_pairs={{0,2},{1,6},{2,4},{3,0},{4,7},{5,3},{6,1},{7,5},{8,10},{9,14},{10,... | collective-permute-start | bytes 1572872 | tf_op jit(solution)/shard_map/ppermute | solution.py:27
  11.8 2.0 %collective-permute-start.3 = (bf16[128,2048]{1,0:T(8,128)(2,1)}, bf16[128,2048]{1,0:T(8,128)(2,1)}, u32[]{:S(2)}, u32[]{:S(2)}) collective-permute-start(bf16[128,2048]{1,0:T(8,128)(2,1)} %param.5), channel_id=1, source_target_pairs={{0,6},{1,2},{2,0},{3,4},{4,3},{5,7},{6,5},{7,1},{8,14},{9,10},{10,... | collective-permute-start | bytes 1572872 | tf_op jit(solution)/shard_map/ppermute | solution.py:27
  13.8 2.2 %row_stats.1 = f32[64,2,256]{2,1,0:T(2,128)} custom-call(bf16[256,2048]{1,0:T(8,128)(2,1)} %bitcast.13), custom_call_target="tpu_custom_call" | custom-call | flops 3000000000 | bytes 9000000 | tf_op jit(solution)/shard_map/row_stats/pallas_call | solution.py:98
  16.0 16.4 %all-to-all-start = ((f32[64,2,256]{2,1,0:T(2,128)}), f32[64,2,256]{2,1,0:T(2,128)S(1)}, u32[]{:S(2)}, u32[]{:S(2)}) async-start(f32[64,2,256]{2,1,0:T(2,128)} %row_stats.1), calls=%async_computation | async-start | bytes 262144 | tf_op jit(solution)/shard_map/all_to_all | solution.py:253
  32.5 2.9 %collective-permute-start = (bf16[128,2048]{1,0:T(8,128)(2,1)}, bf16[128,2048]{1,0:T(8,128)(2,1)}, u32[]{:S(2)}, u32[]{:S(2)}) collective-permute-start(bf16[128,2048]{1,0:T(8,128)(2,1)} %param.5), channel_id=1, source_target_pairs={{0,0},{1,4},{2,2},{3,6},{4,5},{5,1},{6,7},{7,3},{8,8},{9,12},{10,1... | collective-permute-start | bytes 1572872 | tf_op jit(solution)/shard_map/ppermute | solution.py:27
  35.3 5.0 %collective-permute-start.4 = (bf16[128,2048]{1,0:T(8,128)(2,1)}, bf16[128,2048]{1,0:T(8,128)(2,1)}, u32[]{:S(2)}, u32[]{:S(2)}) collective-permute-start(bf16[128,2048]{1,0:T(8,128)(2,1)} %param.5), channel_id=1, source_target_pairs={{0,4},{1,0},{2,6},{3,2},{4,1},{5,5},{6,3},{7,7},{8,12},{9,8},{10,1... | collective-permute-start | bytes 1572872 | tf_op jit(solution)/shard_map/ppermute | solution.py:27
  41.2 1.0 %copy-done.1 = bf16[256,2048]{1,0:T(8,128)(2,1)} copy-done((bf16[256,2048]{1,0:T(8,128)(2,1)}, bf16[256,2048]{1,0:T(8,128)(2,1)S(1)}, u32[]{:S(2)}) %copy-start.1) | copy-done | bytes 1048600
  42.2 6.1 %all-to-all-done = f32[64,2,256]{2,1,0:T(2,128)S(1)} async-done(((f32[64,2,256]{2,1,0:T(2,128)}), f32[64,2,256]{2,1,0:T(2,128)S(1)}, u32[]{:S(2)}, u32[]{:S(2)}) %all-to-all-start) | async-done | bytes 131104 | tf_op jit(solution)/shard_map/all_to_all | solution.py:253
  48.3 1.2 %copy-done.2 = bf16[256,2048]{1,0:T(8,128)(2,1)S(1)} copy-done((bf16[256,2048]{1,0:T(8,128)(2,1)S(1)}, bf16[256,2048]{1,0:T(8,128)(2,1)}, u32[]{:S(2)}) %copy-start.2) | copy-done | bytes 1048600
  49.5 1.9 %logit_grad.1 = (bf16[256,2560]{1,0:T(8,128)(2,1)S(1)}, bf16[256,512]{1,0:T(8,128)(2,1)S(1)}) custom-call(s32[3]{0:T(128)S(1)} %pad_add_fusion.place_ref, f32[2,32,2,256]{3,2,1,0:T(2,128)S(1)} %bitcast.10, bf16[256,1024]{1,0:T(8,128)(2,1)S(1)} %copy-done.3, bf16[256,2048]{1,0:T(8,128)(2,1)S(1)} %bitcast.14, bf16[256,2048]{1,0:T(8,128)(2,1)S(1)} %copy-done.2), custom_call_target="tpu_custom_call" | custom-call | flops 40000000000 | bytes 120000000 | tf_op jit(solution)/shard_map/logit_grad/pallas_call | solution.py:143
  51.4 4.9 %collective-permute-start.5 = (bf16[256,2560]{1,0:T(8,128)(2,1)S(1)}, bf16[256,2560]{1,0:T(8,128)(2,1)S(1)}, u32[]{:S(2)}, u32[]{:S(2)}) collective-permute-start(bf16[256,2560]{1,0:T(8,128)(2,1)S(1)} %get-tuple-element.16.refs_4_.own_ref), channel_id=1, source_target_pairs={{0,1},{1,0},{2,3},{3,2},{4,5},{5,4},{6,7},{7,6},{8,9},{9,8},{10,11... | collective-permute-start | bytes 3932168 | tf_op jit(solution)/shard_map/ppermute | solution.py:258
  56.3 2.1 %own_terms.1 = (bf16[2,8,64,128]{3,2,1,0:T(8,128)(2,1)S(1)}, bf16[512,2048]{1,0:T(8,128)(2,1)S(1)}) custom-call(s32[3]{0:T(128)S(1)} %pad_add_fusion.place_ref, bf16[128,2048]{1,0:T(8,128)(2,1)} %collective-permute-done.refs_0_, bf16[128,2048]{1,0:T(8,128)(2,1)S(1)} %copy-done.5, bf16[128,2048]{1,0:T(8,128)(2,1)} %collective-permute-done.4.refs_2_, ...), custom_call_target="tpu_custom_call" | custom-call | flops 40000000000 | bytes 120000000 | tf_op jit(solution)/shard_map/own_terms/pallas_call | solution.py:46
  58.9 2.0 %hidden_terms.1 = bf16[2,2,8,64,128]{4,3,2,1,0:T(8,128)(2,1)} custom-call(s32[3]{0:T(128)S(1)} %pad_add_fusion.place_ref, bf16[512,2048]{1,0:T(8,128)(2,1)S(1)} %get-tuple-element.17.head_ref, bf16[256,2560]{1,0:T(8,128)(2,1)S(1)} %collective-permute-done.5.grad_ref.core_ref, bf16[2,8,64,128]{3,2,1,0:T(8,128)(2,1)S(1)} %get-tuple-element.18.own_ref), custom_call_target="tpu_custom_call" | custom-call | flops 2000000000 | bytes 6000000 | tf_op jit(solution)/shard_map/hidden_terms/pallas_call | solution.py:217
  60.9 4.0 %all-to-all-start.1 = ((bf16[32,64,128]{2,1,0:T(8,128)(2,1)}), bf16[32,64,128]{2,1,0:T(8,128)(2,1)S(1)}, u32[]{:S(2)}, u32[]{:S(2)}) async-start(bf16[32,64,128]{2,1,0:T(8,128)(2,1)} %bitcast.5), calls=%async_computation.1 | async-start | bytes 1048576 | tf_op jit(solution)/shard_map/all_to_all | solution.py:267
  64.9 2.4 %weight_terms.1 = (bf16[128,2048]{1,0:T(8,128)(2,1)S(1)}, bf16[128,2048]{1,0:T(8,128)(2,1)}, bf16[128,2048]{1,0:T(8,128)(2,1)}, bf16[128,2048]{1,0:T(8,128)(2,1)}) custom-call(bf16[256,512]{1,0:T(8,128)(2,1)S(1)} %copy-done.9, bf16[256,2560]{1,0:T(8,128)(2,1)S(1)} %get-tuple-element.16.refs_4_.own_ref, ...), custom_call_target="tpu_custom_call" | custom-call | flops 4000000000 | bytes 12000000 | tf_op jit(solution)/shard_map/weight_terms/pallas_call | solution.py:46
  68.1 2.5 %collective-permute-start.6 = (bf16[128,2048]{1,0:T(8,128)(2,1)}, bf16[128,2048]{1,0:T(8,128)(2,1)S(1)}, u32[]{:S(2)}, u32[]{:S(2)}) collective-permute-start(bf16[128,2048]{1,0:T(8,128)(2,1)} %get-tuple-element.21), channel_id=1, source_target_pairs={{0,4},{1,5},{2,6},{3,7},{4,0},{5,1},{6,2},{7,3},{8,12},{9,13},{10,... | collective-permute-start | bytes 1572872 | tf_op jit(solution)/shard_map/ppermute | solution.py:22
  70.6 2.0 %collective-permute-start.7 = (bf16[128,2048]{1,0:T(8,128)(2,1)}, bf16[128,2048]{1,0:T(8,128)(2,1)S(1)}, u32[]{:S(2)}, u32[]{:S(2)}) collective-permute-start(bf16[128,2048]{1,0:T(8,128)(2,1)} %get-tuple-element.22), channel_id=1, source_target_pairs={{0,2},{1,3},{2,4},{3,5},{4,6},{5,7},{6,0},{7,1},{8,10},{9,11},{10,... | collective-permute-start | bytes 1572872 | tf_op jit(solution)/shard_map/ppermute | solution.py:22
  72.6 4.5 %collective-permute-start.8 = (bf16[128,2048]{1,0:T(8,128)(2,1)}, bf16[128,2048]{1,0:T(8,128)(2,1)S(1)}, u32[]{:S(2)}, u32[]{:S(2)}) collective-permute-start(bf16[128,2048]{1,0:T(8,128)(2,1)} %get-tuple-element.23), channel_id=1, source_target_pairs={{0,6},{1,7},{2,0},{3,1},{4,2},{5,3},{6,4},{7,5},{8,14},{9,15},{10,... | collective-permute-start | bytes 1572872 | tf_op jit(solution)/shard_map/ppermute | solution.py:22
  77.1 3.6 %all-to-all-done.1 = bf16[32,64,128]{2,1,0:T(8,128)(2,1)S(1)} async-done(((bf16[32,64,128]{2,1,0:T(8,128)(2,1)}), bf16[32,64,128]{2,1,0:T(8,128)(2,1)S(1)}, u32[]{:S(2)}, u32[]{:S(2)}) %all-to-all-start.1) | async-done | bytes 524320 | tf_op jit(solution)/shard_map/all_to_all | solution.py:267
  81.4 4.9 %all-to-all-start.2 = ((bf16[4,64,128]{2,1,0:T(8,128)(2,1)}), bf16[4,64,128]{2,1,0:T(8,128)(2,1)S(1)}, u32[]{:S(2)}, u32[]{:S(2)}) async-start(bf16[4,64,128]{2,1,0:T(8,128)(2,1)} %near_total.1), calls=%async_computation.2 | async-start | bytes 131072 | tf_op jit(solution)/shard_map/all_to_all | solution.py:270
  86.2 10.6 %collective-permute-done.7.refs_2_ = bf16[128,2048]{1,0:T(8,128)(2,1)S(1)} collective-permute-done((bf16[128,2048]{1,0:T(8,128)(2,1)}, bf16[128,2048]{1,0:T(8,128)(2,1)S(1)}, u32[]{:S(2)}, u32[]{:S(2)}) %collective-permute-start.7) | collective-permute-done | bytes 524320 | tf_op jit(solution)/shard_map/ppermute | solution.py:22
  96.8 1.0 weight_total.1
  97.8 0.9 all-to-all-done.2
  (29 shorter events, 3.5 us)
Async XLA Ops:
  0.6 47.6 %copy-start = (bf16[1,256,2048]{2,1,0:T(8,128)(2,1)S(1)}, bf16[1,256,2048]{2,1,0:T(8,128)(2,1)}, u32[]{:S(2)}) copy-start(bf16[1,256,2048]{2,1,0:T(8,128)(2,1)} %param.3) | copy-start | bytes 3145732
  0.6 47.6 %copy-start.3 = (bf16[256,1024]{1,0:T(8,128)(2,1)S(1)}, bf16[256,1024]{1,0:T(8,128)(2,1)}, u32[]{:S(2)}) copy-start(bf16[256,1024]{1,0:T(8,128)(2,1)} %hidden_ref.1) | copy-start | bytes 1572868
  0.6 40.5 %collective-permute-start.1 = (bf16[256,2048]{1,0:T(8,128)(2,1)}, bf16[256,2048]{1,0:T(8,128)(2,1)S(1)}, u32[]{:S(2)}, u32[]{:S(2)}) collective-permute-start(bf16[256,2048]{1,0:T(8,128)(2,1)} %bitcast.12), channel_id=1, source_target_pairs={{0,256},{256,0},{1,257},{257,1},{2,258},{258,2},{3,259},{259,3},{4... | collective-permute-start | bytes 3145736 | tf_op jit(solution)/shard_map/ppermute | solution.py:247
  6.3 34.1 %collective-permute-start.2 = (bf16[128,2048]{1,0:T(8,128)(2,1)}, bf16[128,2048]{1,0:T(8,128)(2,1)S(1)}, u32[]{:S(2)}, u32[]{:S(2)}) collective-permute-start(bf16[128,2048]{1,0:T(8,128)(2,1)} %param.5), channel_id=1, source_target_pairs={{0,2},{1,6},{2,4},{3,0},{4,7},{5,3},{6,1},{7,5},{8,10},{9,14},{10,... | collective-permute-start | bytes 1572872 | tf_op jit(solution)/shard_map/ppermute | solution.py:27
  11.8 29.4 %collective-permute-start.3 = (bf16[128,2048]{1,0:T(8,128)(2,1)}, bf16[128,2048]{1,0:T(8,128)(2,1)}, u32[]{:S(2)}, u32[]{:S(2)}) collective-permute-start(bf16[128,2048]{1,0:T(8,128)(2,1)} %param.5), channel_id=1, source_target_pairs={{0,6},{1,2},{2,0},{3,4},{4,3},{5,7},{6,5},{7,1},{8,14},{9,10},{10,... | collective-permute-start | bytes 1572872 | tf_op jit(solution)/shard_map/ppermute | solution.py:27
  16.0 32.2 %all-to-all-start = ((f32[64,2,256]{2,1,0:T(2,128)}), f32[64,2,256]{2,1,0:T(2,128)S(1)}, u32[]{:S(2)}, u32[]{:S(2)}) async-start(f32[64,2,256]{2,1,0:T(2,128)} %row_stats.1), calls=%async_computation | async-start | bytes 262144 | tf_op jit(solution)/shard_map/all_to_all | solution.py:253
  32.5 23.8 %collective-permute-start = (bf16[128,2048]{1,0:T(8,128)(2,1)}, bf16[128,2048]{1,0:T(8,128)(2,1)}, u32[]{:S(2)}, u32[]{:S(2)}) collective-permute-start(bf16[128,2048]{1,0:T(8,128)(2,1)} %param.5), channel_id=1, source_target_pairs={{0,0},{1,4},{2,2},{3,6},{4,5},{5,1},{6,7},{7,3},{8,8},{9,12},{10,1... | collective-permute-start | bytes 1572872 | tf_op jit(solution)/shard_map/ppermute | solution.py:27
  35.3 21.0 %collective-permute-start.4 = (bf16[128,2048]{1,0:T(8,128)(2,1)}, bf16[128,2048]{1,0:T(8,128)(2,1)}, u32[]{:S(2)}, u32[]{:S(2)}) collective-permute-start(bf16[128,2048]{1,0:T(8,128)(2,1)} %param.5), channel_id=1, source_target_pairs={{0,4},{1,0},{2,6},{3,2},{4,1},{5,5},{6,3},{7,7},{8,12},{9,8},{10,1... | collective-permute-start | bytes 1572872 | tf_op jit(solution)/shard_map/ppermute | solution.py:27
  40.4 0.8 copy-start.4
  41.2 1.0 %copy-start.1 = (bf16[256,2048]{1,0:T(8,128)(2,1)}, bf16[256,2048]{1,0:T(8,128)(2,1)S(1)}, u32[]{:S(2)}) copy-start(bf16[256,2048]{1,0:T(8,128)(2,1)S(1)} %collective-permute-done.1.peer_ref) | copy-start | bytes 3145732
  48.3 1.2 %copy-start.2 = (bf16[256,2048]{1,0:T(8,128)(2,1)S(1)}, bf16[256,2048]{1,0:T(8,128)(2,1)}, u32[]{:S(2)}) copy-start(bf16[256,2048]{1,0:T(8,128)(2,1)} %copy-done.1) | copy-start | bytes 3145732
  49.5 6.8 %copy-start.5 = (bf16[128,2048]{1,0:T(8,128)(2,1)S(1)}, bf16[128,2048]{1,0:T(8,128)(2,1)}, u32[]{:S(2)}) copy-start(bf16[128,2048]{1,0:T(8,128)(2,1)} %copy-done.4) | copy-start | bytes 1572868
  51.4 7.1 %copy-start.8 = (bf16[256,512]{1,0:T(8,128)(2,1)}, bf16[256,512]{1,0:T(8,128)(2,1)S(1)}, u32[]{:S(2)}) copy-start(bf16[256,512]{1,0:T(8,128)(2,1)S(1)} %get-tuple-element.19.own_columns_ref) | copy-start | bytes 786436
  51.4 7.5 %collective-permute-start.5 = (bf16[256,2560]{1,0:T(8,128)(2,1)S(1)}, bf16[256,2560]{1,0:T(8,128)(2,1)S(1)}, u32[]{:S(2)}, u32[]{:S(2)}) collective-permute-start(bf16[256,2560]{1,0:T(8,128)(2,1)S(1)} %get-tuple-element.16.refs_4_.own_ref), channel_id=1, source_target_pairs={{0,1},{1,0},{2,3},{3,2},{4,5},{5,4},{6,7},{7,6},{8,9},{9,8},{10,11... | collective-permute-start | bytes 3932168 | tf_op jit(solution)/shard_map/ppermute | solution.py:258
  58.9 6.0 %copy-start.9 = (bf16[256,512]{1,0:T(8,128)(2,1)S(1)}, bf16[256,512]{1,0:T(8,128)(2,1)}, u32[]{:S(2)}) copy-start(bf16[256,512]{1,0:T(8,128)(2,1)} %copy-done.8) | copy-start | bytes 786436
  60.9 19.7 %all-to-all-start.1 = ((bf16[32,64,128]{2,1,0:T(8,128)(2,1)}), bf16[32,64,128]{2,1,0:T(8,128)(2,1)S(1)}, u32[]{:S(2)}, u32[]{:S(2)}) async-start(bf16[32,64,128]{2,1,0:T(8,128)(2,1)} %bitcast.5), calls=%async_computation.1 | async-start | bytes 1048576 | tf_op jit(solution)/shard_map/all_to_all | solution.py:267
  67.3 0.8 copy-start.6
  68.1 18.1 %collective-permute-start.6 = (bf16[128,2048]{1,0:T(8,128)(2,1)}, bf16[128,2048]{1,0:T(8,128)(2,1)S(1)}, u32[]{:S(2)}, u32[]{:S(2)}) collective-permute-start(bf16[128,2048]{1,0:T(8,128)(2,1)} %get-tuple-element.21), channel_id=1, source_target_pairs={{0,4},{1,5},{2,6},{3,7},{4,0},{5,1},{6,2},{7,3},{8,12},{9,13},{10,... | collective-permute-start | bytes 1572872 | tf_op jit(solution)/shard_map/ppermute | solution.py:22
  70.6 26.2 %collective-permute-start.7 = (bf16[128,2048]{1,0:T(8,128)(2,1)}, bf16[128,2048]{1,0:T(8,128)(2,1)S(1)}, u32[]{:S(2)}, u32[]{:S(2)}) collective-permute-start(bf16[128,2048]{1,0:T(8,128)(2,1)} %get-tuple-element.22), channel_id=1, source_target_pairs={{0,2},{1,3},{2,4},{3,5},{4,6},{5,7},{6,0},{7,1},{8,10},{9,11},{10,... | collective-permute-start | bytes 1572872 | tf_op jit(solution)/shard_map/ppermute | solution.py:22
  72.6 24.2 %collective-permute-start.8 = (bf16[128,2048]{1,0:T(8,128)(2,1)}, bf16[128,2048]{1,0:T(8,128)(2,1)S(1)}, u32[]{:S(2)}, u32[]{:S(2)}) collective-permute-start(bf16[128,2048]{1,0:T(8,128)(2,1)} %get-tuple-element.23), channel_id=1, source_target_pairs={{0,6},{1,7},{2,0},{3,1},{4,2},{5,3},{6,4},{7,5},{8,14},{9,15},{10,... | collective-permute-start | bytes 1572872 | tf_op jit(solution)/shard_map/ppermute | solution.py:22
  80.7 16.1 %copy-start.7 = (bf16[128,2048]{1,0:T(8,128)(2,1)S(1)}, bf16[128,2048]{1,0:T(8,128)(2,1)}, u32[]{:S(2)}) copy-start(bf16[128,2048]{1,0:T(8,128)(2,1)} %copy-done.6) | copy-start | bytes 1572868
  81.4 17.3 %all-to-all-start.2 = ((bf16[4,64,128]{2,1,0:T(8,128)(2,1)}), bf16[4,64,128]{2,1,0:T(8,128)(2,1)S(1)}, u32[]{:S(2)}, u32[]{:S(2)}) async-start(bf16[4,64,128]{2,1,0:T(8,128)(2,1)} %near_total.1), calls=%async_computation.2 | async-start | bytes 131072 | tf_op jit(solution)/shard_map/all_to_all | solution.py:270

commit v6 on v5

--- a/solution.py
+++ b/solution.py
@@ -1,3 +1,5 @@
+import functools
+
 import jax
 import jax.numpy as jnp
 from jax import lax
@@ -151,15 +153,17 @@
     )(place, parts, hidden, own, peer)
 
 
-def weight_kernel(own_columns_ref, own_ref, core_ref, *out_refs):
+def weight_kernel(ahead, own_columns_ref, own_ref, core_ref, *out_refs):
     sides = (((0,), (0,)), ((), ()))
     width = out_refs[0].shape[1]
+    here = slice(ahead[0] * 128, ahead[-1] * 128 + 128)
+    there = slice(width + ahead[0] * 128, width + ahead[-1] * 128 + 128)
     for first in range(0, width, 512):
         cut = slice(first, first + 512)
-        terms = lax.dot_general(own_columns_ref[...], own_ref[:, cut], sides, preferred_element_type=f32)
-        terms = terms + lax.dot_general(core_ref[:, width:], core_ref[:, cut], sides, preferred_element_type=f32)
-        for j, ref in enumerate(out_refs):
-            ref[:, cut] = terms[j * 128 : j * 128 + 128].astype(ref.dtype)
+        terms = lax.dot_general(own_columns_ref[:, here], own_ref[:, cut], sides, preferred_element_type=f32)
+        terms = terms + lax.dot_general(core_ref[:, there], core_ref[:, cut], sides, preferred_element_type=f32)
+        for i, ref in enumerate(out_refs):
+            ref[:, cut] = terms[i * 128 : i * 128 + 128].astype(ref.dtype)
 
 
 def sum_kernel(*refs):
@@ -260,8 +264,8 @@
     head = jax.ShapeDtypeStruct((chips * head_rows, width), bf16)
     own_terms, head = call(own_terms_kernel, (own_terms, head), 40, "own_terms", 1, whole=True)(place, *heads, pair)
     block = lambda kind: jax.ShapeDtypeStruct((head_rows, width), kind)
-    outs = (block(bf16),) * chips
-    ahead_terms = call(weight_kernel, outs, 4, "weight_terms")(own_columns, pair, core_pair)
+    sent, stays = functools.partial(weight_kernel, (1, 2, 3)), functools.partial(weight_kernel, (0,))
+    ahead_terms = call(sent, (block(bf16),) * 3, 3, "weight_terms")(own_columns, pair, core_pair)
     near = hidden_terms(place, head, core_pair, own_terms, 2)
     near = near.reshape(32, 64, half_rows)
     near = lax.all_to_all(near, ("sec", "vocab", "rows"), 0, 0, axis_index_groups=near_groups, tiled=True)
@@ -271,8 +275,9 @@
     hidden_grad = jax.ShapeDtypeStruct((1, 64, half_rows), bf16)
     hidden_grad = call(total_kernel, hidden_grad, 1, "far_total")(far[None]).transpose(0, 2, 1)
 
-    moved = [shifted(ahead_terms[j], j) for j in (2, 1, 3)]
-    weight_grad = call(sum_kernel, block(bf16), 100, "weight_total", 0, 2, [0] * 4, [0])(ahead_terms[0], *moved)
+    moved = [shifted(ahead_terms[j - 1], j) for j in (2, 1, 3)]
+    own_block = call(stays, block(bf16), 1, "own_weight_terms")(own_columns, pair, core_pair)
+    weight_grad = call(sum_kernel, block(bf16), 100, "weight_total", 0, 2, [0] * 4, [0])(own_block, *moved)
     return hidden_grad, weight_grad
 
 

time: 100 us -> 101 us (1.010)
  Pallas kernels: 12.9 us -> 14.3 us
    pallas_call x5 -> x6, Pallas kernels: 6.78 us -> 8.17 us  [run(): pl.pallas_call(kernel, out_shape=out_shape, grid=(grid,), in_specs=[pl.Bl...]
    ppermute x3, waiting for transfers between devices: 10.6 us -> 9.48 us  [shifted(): return lax.ppermute(value, 'rows', pairs)]
  transfers between devices with their start and end apart: 12 -> 12, of which waited for: 5 -> 5; matrix products, arithmetic and copies ran while one was open for 0% -> 0% of each run, Pallas kernels for 10% -> 12%
where the time goes in v6:
time: 101 us; the launch traced here: 99.6 us
  starting transfers between devices  60 us (59%)
  waiting for transfers between devices  20.6 us (20%)
  Pallas kernels  14.3 us (14%)
  local copies, waits for them, and re-layouts  3.84 us (4%)
    all_to_all x1, starting transfers between devices, body(): parts = lax.all_to_all(copies, ('sec', 'vocab'), 0, 0, tiled=True)  16.4 us
    ppermute x4, starting transfers between devices, spread(): return lax.ppermute(value, 'rows', pairs)  15.3 us
    ppermute x3, waiting for transfers between devices, shifted(): return lax.ppermute(value, 'rows', pairs)  9.48 us
    ppermute x3, starting transfers between devices, shifted(): return lax.ppermute(value, 'rows', pairs)  8.96 us
    pallas_call x6, Pallas kernels, run(): pl.pallas_call(kernel, out_shape=out_shape, grid=(grid,), in_specs=[pl.Bl...  8.17 us
    all_to_all x1, waiting for transfers between devices, body(): parts = lax.all_to_all(copies, ('sec', 'vocab'), 0, 0, tiled=True)  6.07 us
    ppermute x1, starting transfers between devices, body(): peer = lax.ppermute(own, 'sec', swap_sec)  5.61 us
    ppermute x1, starting transfers between devices, body(): core_pair = lax.ppermute(pair, 'rows', swap_core)  4.88 us
  transfers between devices with their start and end apart: 12, of which 5 were waited for; matrix products, arithmetic and copies ran while one was open for 0% of the time, Pallas kernels for 12%

profile of v6, /device:TPU:1, one launch (start us, length us, event | category | flops | bytes accessed | tf_op | source)
XLA Modules:
  0.0 99.6 jit_solution(4664730425459978817)
XLA Ops:
  0.6 5.6 %collective-permute-start.1 = (bf16[256,2048]{1,0:T(8,128)(2,1)}, bf16[256,2048]{1,0:T(8,128)(2,1)S(1)}, u32[]{:S(2)}, u32[]{:S(2)}) collective-permute-start(bf16[256,2048]{1,0:T(8,128)(2,1)} %bitcast.12), channel_id=1, source_target_pairs={{0,256},{256,0},{1,257},{257,1},{2,258},{258,2},{3,259},{259,3},{4... | collective-permute-start | bytes 3145736 | tf_op jit(solution)/shard_map/ppermute | solution.py:251
  6.3 5.5 %collective-permute-start.2 = (bf16[128,2048]{1,0:T(8,128)(2,1)}, bf16[128,2048]{1,0:T(8,128)(2,1)S(1)}, u32[]{:S(2)}, u32[]{:S(2)}) collective-permute-start(bf16[128,2048]{1,0:T(8,128)(2,1)} %param.5), channel_id=1, source_target_pairs={{0,2},{1,6},{2,4},{3,0},{4,7},{5,3},{6,1},{7,5},{8,10},{9,14},{10,... | collective-permute-start | bytes 1572872 | tf_op jit(solution)/shard_map/ppermute | solution.py:29
  11.8 2.0 %collective-permute-start.3 = (bf16[128,2048]{1,0:T(8,128)(2,1)}, bf16[128,2048]{1,0:T(8,128)(2,1)}, u32[]{:S(2)}, u32[]{:S(2)}) collective-permute-start(bf16[128,2048]{1,0:T(8,128)(2,1)} %param.5), channel_id=1, source_target_pairs={{0,6},{1,2},{2,0},{3,4},{4,3},{5,7},{6,5},{7,1},{8,14},{9,10},{10,... | collective-permute-start | bytes 1572872 | tf_op jit(solution)/shard_map/ppermute | solution.py:29
  13.8 2.2 %row_stats.1 = f32[64,2,256]{2,1,0:T(2,128)} custom-call(bf16[256,2048]{1,0:T(8,128)(2,1)} %bitcast.13), custom_call_target="tpu_custom_call" | custom-call | flops 3000000000 | bytes 9000000 | tf_op jit(solution)/shard_map/row_stats/pallas_call | solution.py:100
  16.0 16.4 %all-to-all-start = ((f32[64,2,256]{2,1,0:T(2,128)}), f32[64,2,256]{2,1,0:T(2,128)S(1)}, u32[]{:S(2)}, u32[]{:S(2)}) async-start(f32[64,2,256]{2,1,0:T(2,128)} %row_stats.1), calls=%async_computation | async-start | bytes 262144 | tf_op jit(solution)/shard_map/all_to_all | solution.py:257
  32.5 2.9 %collective-permute-start = (bf16[128,2048]{1,0:T(8,128)(2,1)}, bf16[128,2048]{1,0:T(8,128)(2,1)}, u32[]{:S(2)}, u32[]{:S(2)}) collective-permute-start(bf16[128,2048]{1,0:T(8,128)(2,1)} %param.5), channel_id=1, source_target_pairs={{0,0},{1,4},{2,2},{3,6},{4,5},{5,1},{6,7},{7,3},{8,8},{9,12},{10,1... | collective-permute-start | bytes 1572872 | tf_op jit(solution)/shard_map/ppermute | solution.py:29
  35.3 5.0 %collective-permute-start.4 = (bf16[128,2048]{1,0:T(8,128)(2,1)}, bf16[128,2048]{1,0:T(8,128)(2,1)}, u32[]{:S(2)}, u32[]{:S(2)}) collective-permute-start(bf16[128,2048]{1,0:T(8,128)(2,1)} %param.5), channel_id=1, source_target_pairs={{0,4},{1,0},{2,6},{3,2},{4,1},{5,5},{6,3},{7,7},{8,12},{9,8},{10,1... | collective-permute-start | bytes 1572872 | tf_op jit(solution)/shard_map/ppermute | solution.py:29
  41.2 1.0 %copy-done.1 = bf16[256,2048]{1,0:T(8,128)(2,1)} copy-done((bf16[256,2048]{1,0:T(8,128)(2,1)}, bf16[256,2048]{1,0:T(8,128)(2,1)S(1)}, u32[]{:S(2)}) %copy-start.1) | copy-done | bytes 1048600
  42.2 6.1 %all-to-all-done = f32[64,2,256]{2,1,0:T(2,128)S(1)} async-done(((f32[64,2,256]{2,1,0:T(2,128)}), f32[64,2,256]{2,1,0:T(2,128)S(1)}, u32[]{:S(2)}, u32[]{:S(2)}) %all-to-all-start) | async-done | bytes 131104 | tf_op jit(solution)/shard_map/all_to_all | solution.py:257
  48.3 1.2 %copy-done.2 = bf16[256,2048]{1,0:T(8,128)(2,1)S(1)} copy-done((bf16[256,2048]{1,0:T(8,128)(2,1)S(1)}, bf16[256,2048]{1,0:T(8,128)(2,1)}, u32[]{:S(2)}) %copy-start.2) | copy-done | bytes 1048600
  49.5 1.9 %logit_grad.1 = (bf16[256,2560]{1,0:T(8,128)(2,1)S(1)}, bf16[256,512]{1,0:T(8,128)(2,1)S(1)}) custom-call(s32[3]{0:T(128)S(1)} %pad_add_fusion.place_ref, f32[2,32,2,256]{3,2,1,0:T(2,128)S(1)} %bitcast.10, bf16[256,1024]{1,0:T(8,128)(2,1)S(1)} %copy-done.3, bf16[256,2048]{1,0:T(8,128)(2,1)S(1)} %bitcast.14, bf16[256,2048]{1,0:T(8,128)(2,1)S(1)} %copy-done.2), custom_call_target="tpu_custom_call" | custom-call | flops 40000000000 | bytes 120000000 | tf_op jit(solution)/shard_map/logit_grad/pallas_call | solution.py:145
  51.4 4.9 %collective-permute-start.5 = (bf16[256,2560]{1,0:T(8,128)(2,1)S(1)}, bf16[256,2560]{1,0:T(8,128)(2,1)S(1)}, u32[]{:S(2)}, u32[]{:S(2)}) collective-permute-start(bf16[256,2560]{1,0:T(8,128)(2,1)S(1)} %get-tuple-element.15.refs_4_.own_ref), channel_id=1, source_target_pairs={{0,1},{1,0},{2,3},{3,2},{4,5},{5,4},{6,7},{7,6},{8,9},{9,8},{10,11... | collective-permute-start | bytes 3932168 | tf_op jit(solution)/shard_map/ppermute | solution.py:262
  56.3 2.1 %own_terms.1 = (bf16[2,8,64,128]{3,2,1,0:T(8,128)(2,1)S(1)}, bf16[512,2048]{1,0:T(8,128)(2,1)S(1)}) custom-call(s32[3]{0:T(128)S(1)} %pad_add_fusion.place_ref, bf16[128,2048]{1,0:T(8,128)(2,1)} %collective-permute-done.refs_0_, bf16[128,2048]{1,0:T(8,128)(2,1)S(1)} %copy-done.5, bf16[128,2048]{1,0:T(8,128)(2,1)} %collective-permute-done.4.refs_2_, ...), custom_call_target="tpu_custom_call" | custom-call | flops 40000000000 | bytes 120000000 | tf_op jit(solution)/shard_map/own_terms/pallas_call | solution.py:48
  58.9 2.0 %hidden_terms.1 = bf16[2,2,8,64,128]{4,3,2,1,0:T(8,128)(2,1)} custom-call(s32[3]{0:T(128)S(1)} %pad_add_fusion.place_ref, bf16[512,2048]{1,0:T(8,128)(2,1)S(1)} %get-tuple-element.16.head_ref, bf16[256,2560]{1,0:T(8,128)(2,1)S(1)} %collective-permute-done.5.grad_ref.core_ref, bf16[2,8,64,128]{3,2,1,0:T(8,128)(2,1)S(1)} %get-tuple-element.17.own_ref), custom_call_target="tpu_custom_call" | custom-call | flops 2000000000 | bytes 6000000 | tf_op jit(solution)/shard_map/hidden_terms/pallas_call | solution.py:221
  60.9 4.0 %all-to-all-start.1 = ((bf16[32,64,128]{2,1,0:T(8,128)(2,1)}), bf16[32,64,128]{2,1,0:T(8,128)(2,1)S(1)}, u32[]{:S(2)}, u32[]{:S(2)}) async-start(bf16[32,64,128]{2,1,0:T(8,128)(2,1)} %bitcast.5), calls=%async_computation.1 | async-start | bytes 1048576 | tf_op jit(solution)/shard_map/all_to_all | solution.py:271
  64.9 2.1 %weight_terms.1 = (bf16[128,2048]{1,0:T(8,128)(2,1)}, bf16[128,2048]{1,0:T(8,128)(2,1)}, bf16[128,2048]{1,0:T(8,128)(2,1)}) custom-call(bf16[256,512]{1,0:T(8,128)(2,1)S(1)} %copy-done.9, bf16[256,2560]{1,0:T(8,128)(2,1)S(1)} %get-tuple-element.15.refs_4_.own_ref, bf16[256,2560]{1,0:T(8,128)(2,1)S(1)} %collective-permute-done.5.grad_ref.core_ref), custom_call_target="tpu_custom_call" | custom-call | flops 3000000000 | bytes 9000000 | tf_op jit(solution)/shard_map/weight_terms/pallas_call | solution.py:48
  67.0 2.5 %collective-permute-start.6 = (bf16[128,2048]{1,0:T(8,128)(2,1)}, bf16[128,2048]{1,0:T(8,128)(2,1)}, u32[]{:S(2)}, u32[]{:S(2)}) collective-permute-start(bf16[128,2048]{1,0:T(8,128)(2,1)} %get-tuple-element.19), channel_id=1, source_target_pairs={{0,4},{1,5},{2,6},{3,7},{4,0},{5,1},{6,2},{7,3},{8,12},{9,13},{10,... | collective-permute-start | bytes 1572872 | tf_op jit(solution)/shard_map/ppermute | solution.py:24
  69.5 2.0 %collective-permute-start.7 = (bf16[128,2048]{1,0:T(8,128)(2,1)}, bf16[128,2048]{1,0:T(8,128)(2,1)}, u32[]{:S(2)}, u32[]{:S(2)}) collective-permute-start(bf16[128,2048]{1,0:T(8,128)(2,1)} %get-tuple-element.20), channel_id=1, source_target_pairs={{0,2},{1,3},{2,4},{3,5},{4,6},{5,7},{6,0},{7,1},{8,10},{9,11},{10,... | collective-permute-start | bytes 1572872 | tf_op jit(solution)/shard_map/ppermute | solution.py:24
  71.5 4.5 %collective-permute-start.8 = (bf16[128,2048]{1,0:T(8,128)(2,1)}, bf16[128,2048]{1,0:T(8,128)(2,1)}, u32[]{:S(2)}, u32[]{:S(2)}) collective-permute-start(bf16[128,2048]{1,0:T(8,128)(2,1)} %get-tuple-element.21), channel_id=1, source_target_pairs={{0,6},{1,7},{2,0},{3,1},{4,2},{5,3},{6,4},{7,5},{8,14},{9,15},{10,... | collective-permute-start | bytes 1572872 | tf_op jit(solution)/shard_map/ppermute | solution.py:24
  77.3 3.5 %all-to-all-done.1 = bf16[32,64,128]{2,1,0:T(8,128)(2,1)S(1)} async-done(((bf16[32,64,128]{2,1,0:T(8,128)(2,1)}), bf16[32,64,128]{2,1,0:T(8,128)(2,1)S(1)}, u32[]{:S(2)}, u32[]{:S(2)}) %all-to-all-start.1) | async-done | bytes 524320 | tf_op jit(solution)/shard_map/all_to_all | solution.py:271
  81.5 4.9 %all-to-all-start.2 = ((bf16[4,64,128]{2,1,0:T(8,128)(2,1)}), bf16[4,64,128]{2,1,0:T(8,128)(2,1)S(1)}, u32[]{:S(2)}, u32[]{:S(2)}) async-start(bf16[4,64,128]{2,1,0:T(8,128)(2,1)} %near_total.1), calls=%async_computation.2 | async-start | bytes 131072 | tf_op jit(solution)/shard_map/all_to_all | solution.py:274
  86.3 9.5 %collective-permute-done.7.refs_2_ = bf16[128,2048]{1,0:T(8,128)(2,1)} collective-permute-done((bf16[128,2048]{1,0:T(8,128)(2,1)}, bf16[128,2048]{1,0:T(8,128)(2,1)}, u32[]{:S(2)}, u32[]{:S(2)}) %collective-permute-start.7) | collective-permute-done | bytes 524320 | tf_op jit(solution)/shard_map/ppermute | solution.py:24
  95.8 2.2 %weight_total.1 = bf16[128,2048]{1,0:T(8,128)(2,1)} custom-call(bf16[128,2048]{1,0:T(8,128)(2,1)S(1)} %copy-done.7, bf16[128,2048]{1,0:T(8,128)(2,1)} %collective-permute-done.6.refs_1_, bf16[128,2048]{1,0:T(8,128)(2,1)} %collective-permute-done.7.refs_2_, bf16[128,2048]{1,0:T(8,128)(2,1)} %collective-permute-done.8.refs_3_), custom_call_target="tpu_custom_call" | custom-call | flops 99999997952 | bytes 300000000 | tf_op jit(solution)/shard_map/weight_total/pallas_call | solution.py:48
  98.0 1.0 %all-to-all-done.2 = bf16[4,64,128]{2,1,0:T(8,128)(2,1)S(1)} async-done(((bf16[4,64,128]{2,1,0:T(8,128)(2,1)}), bf16[4,64,128]{2,1,0:T(8,128)(2,1)S(1)}, u32[]{:S(2)}, u32[]{:S(2)}) %all-to-all-start.2) | async-done | bytes 65568 | tf_op jit(solution)/shard_map/all_to_all | solution.py:274
  (30 shorter events, 4.0 us)
Async XLA Ops:
  0.6 47.6 %copy-start = (bf16[1,256,2048]{2,1,0:T(8,128)(2,1)S(1)}, bf16[1,256,2048]{2,1,0:T(8,128)(2,1)}, u32[]{:S(2)}) copy-start(bf16[1,256,2048]{2,1,0:T(8,128)(2,1)} %param.3) | copy-start | bytes 3145732
  0.6 47.6 %copy-start.3 = (bf16[256,1024]{1,0:T(8,128)(2,1)S(1)}, bf16[256,1024]{1,0:T(8,128)(2,1)}, u32[]{:S(2)}) copy-start(bf16[256,1024]{1,0:T(8,128)(2,1)} %hidden_ref.1) | copy-start | bytes 1572868
  0.6 40.5 %collective-permute-start.1 = (bf16[256,2048]{1,0:T(8,128)(2,1)}, bf16[256,2048]{1,0:T(8,128)(2,1)S(1)}, u32[]{:S(2)}, u32[]{:S(2)}) collective-permute-start(bf16[256,2048]{1,0:T(8,128)(2,1)} %bitcast.12), channel_id=1, source_target_pairs={{0,256},{256,0},{1,257},{257,1},{2,258},{258,2},{3,259},{259,3},{4... | collective-permute-start | bytes 3145736 | tf_op jit(solution)/shard_map/ppermute | solution.py:251
  6.3 34.1 %collective-permute-start.2 = (bf16[128,2048]{1,0:T(8,128)(2,1)}, bf16[128,2048]{1,0:T(8,128)(2,1)S(1)}, u32[]{:S(2)}, u32[]{:S(2)}) collective-permute-start(bf16[128,2048]{1,0:T(8,128)(2,1)} %param.5), channel_id=1, source_target_pairs={{0,2},{1,6},{2,4},{3,0},{4,7},{5,3},{6,1},{7,5},{8,10},{9,14},{10,... | collective-permute-start | bytes 1572872 | tf_op jit(solution)/shard_map/ppermute | solution.py:29
  11.8 29.4 %collective-permute-start.3 = (bf16[128,2048]{1,0:T(8,128)(2,1)}, bf16[128,2048]{1,0:T(8,128)(2,1)}, u32[]{:S(2)}, u32[]{:S(2)}) collective-permute-start(bf16[128,2048]{1,0:T(8,128)(2,1)} %param.5), channel_id=1, source_target_pairs={{0,6},{1,2},{2,0},{3,4},{4,3},{5,7},{6,5},{7,1},{8,14},{9,10},{10,... | collective-permute-start | bytes 1572872 | tf_op jit(solution)/shard_map/ppermute | solution.py:29
  16.0 32.2 %all-to-all-start = ((f32[64,2,256]{2,1,0:T(2,128)}), f32[64,2,256]{2,1,0:T(2,128)S(1)}, u32[]{:S(2)}, u32[]{:S(2)}) async-start(f32[64,2,256]{2,1,0:T(2,128)} %row_stats.1), calls=%async_computation | async-start | bytes 262144 | tf_op jit(solution)/shard_map/all_to_all | solution.py:257
  32.5 23.8 %collective-permute-start = (bf16[128,2048]{1,0:T(8,128)(2,1)}, bf16[128,2048]{1,0:T(8,128)(2,1)}, u32[]{:S(2)}, u32[]{:S(2)}) collective-permute-start(bf16[128,2048]{1,0:T(8,128)(2,1)} %param.5), channel_id=1, source_target_pairs={{0,0},{1,4},{2,2},{3,6},{4,5},{5,1},{6,7},{7,3},{8,8},{9,12},{10,1... | collective-permute-start | bytes 1572872 | tf_op jit(solution)/shard_map/ppermute | solution.py:29
  35.3 21.0 %collective-permute-start.4 = (bf16[128,2048]{1,0:T(8,128)(2,1)}, bf16[128,2048]{1,0:T(8,128)(2,1)}, u32[]{:S(2)}, u32[]{:S(2)}) collective-permute-start(bf16[128,2048]{1,0:T(8,128)(2,1)} %param.5), channel_id=1, source_target_pairs={{0,4},{1,0},{2,6},{3,2},{4,1},{5,5},{6,3},{7,7},{8,12},{9,8},{10,1... | collective-permute-start | bytes 1572872 | tf_op jit(solution)/shard_map/ppermute | solution.py:29
  40.4 0.8 copy-start.4
  41.2 1.0 %copy-start.1 = (bf16[256,2048]{1,0:T(8,128)(2,1)}, bf16[256,2048]{1,0:T(8,128)(2,1)S(1)}, u32[]{:S(2)}) copy-start(bf16[256,2048]{1,0:T(8,128)(2,1)S(1)} %collective-permute-done.1.peer_ref) | copy-start | bytes 3145732
  48.3 1.2 %copy-start.2 = (bf16[256,2048]{1,0:T(8,128)(2,1)S(1)}, bf16[256,2048]{1,0:T(8,128)(2,1)}, u32[]{:S(2)}) copy-start(bf16[256,2048]{1,0:T(8,128)(2,1)} %copy-done.1) | copy-start | bytes 3145732
  49.5 6.8 %copy-start.5 = (bf16[128,2048]{1,0:T(8,128)(2,1)S(1)}, bf16[128,2048]{1,0:T(8,128)(2,1)}, u32[]{:S(2)}) copy-start(bf16[128,2048]{1,0:T(8,128)(2,1)} %copy-done.4) | copy-start | bytes 1572868
  51.4 7.1 %copy-start.8 = (bf16[256,512]{1,0:T(8,128)(2,1)}, bf16[256,512]{1,0:T(8,128)(2,1)S(1)}, u32[]{:S(2)}) copy-start(bf16[256,512]{1,0:T(8,128)(2,1)S(1)} %get-tuple-element.18.own_columns_ref) | copy-start | bytes 786436
  51.4 7.5 %collective-permute-start.5 = (bf16[256,2560]{1,0:T(8,128)(2,1)S(1)}, bf16[256,2560]{1,0:T(8,128)(2,1)S(1)}, u32[]{:S(2)}, u32[]{:S(2)}) collective-permute-start(bf16[256,2560]{1,0:T(8,128)(2,1)S(1)} %get-tuple-element.15.refs_4_.own_ref), channel_id=1, source_target_pairs={{0,1},{1,0},{2,3},{3,2},{4,5},{5,4},{6,7},{7,6},{8,9},{9,8},{10,11... | collective-permute-start | bytes 3932168 | tf_op jit(solution)/shard_map/ppermute | solution.py:262
  58.9 6.0 %copy-start.9 = (bf16[256,512]{1,0:T(8,128)(2,1)S(1)}, bf16[256,512]{1,0:T(8,128)(2,1)}, u32[]{:S(2)}) copy-start(bf16[256,512]{1,0:T(8,128)(2,1)} %copy-done.8) | copy-start | bytes 786436
  60.9 19.8 %all-to-all-start.1 = ((bf16[32,64,128]{2,1,0:T(8,128)(2,1)}), bf16[32,64,128]{2,1,0:T(8,128)(2,1)S(1)}, u32[]{:S(2)}, u32[]{:S(2)}) async-start(bf16[32,64,128]{2,1,0:T(8,128)(2,1)} %bitcast.5), calls=%async_computation.1 | async-start | bytes 1048576 | tf_op jit(solution)/shard_map/all_to_all | solution.py:271
  67.0 19.3 %collective-permute-start.6 = (bf16[128,2048]{1,0:T(8,128)(2,1)}, bf16[128,2048]{1,0:T(8,128)(2,1)}, u32[]{:S(2)}, u32[]{:S(2)}) collective-permute-start(bf16[128,2048]{1,0:T(8,128)(2,1)} %get-tuple-element.19), channel_id=1, source_target_pairs={{0,4},{1,5},{2,6},{3,7},{4,0},{5,1},{6,2},{7,3},{8,12},{9,13},{10,... | collective-permute-start | bytes 1572872 | tf_op jit(solution)/shard_map/ppermute | solution.py:24
  69.5 26.3 %collective-permute-start.7 = (bf16[128,2048]{1,0:T(8,128)(2,1)}, bf16[128,2048]{1,0:T(8,128)(2,1)}, u32[]{:S(2)}, u32[]{:S(2)}) collective-permute-start(bf16[128,2048]{1,0:T(8,128)(2,1)} %get-tuple-element.20), channel_id=1, source_target_pairs={{0,2},{1,3},{2,4},{3,5},{4,6},{5,7},{6,0},{7,1},{8,10},{9,11},{10,... | collective-permute-start | bytes 1572872 | tf_op jit(solution)/shard_map/ppermute | solution.py:24
  71.5 24.3 %collective-permute-start.8 = (bf16[128,2048]{1,0:T(8,128)(2,1)}, bf16[128,2048]{1,0:T(8,128)(2,1)}, u32[]{:S(2)}, u32[]{:S(2)}) collective-permute-start(bf16[128,2048]{1,0:T(8,128)(2,1)} %get-tuple-element.21), channel_id=1, source_target_pairs={{0,6},{1,7},{2,0},{3,1},{4,2},{5,3},{6,4},{7,5},{8,14},{9,15},{10,... | collective-permute-start | bytes 1572872 | tf_op jit(solution)/shard_map/ppermute | solution.py:24
  76.5 0.8 copy-start.6
  80.8 15.0 %copy-start.7 = (bf16[128,2048]{1,0:T(8,128)(2,1)S(1)}, bf16[128,2048]{1,0:T(8,128)(2,1)}, u32[]{:S(2)}) copy-start(bf16[128,2048]{1,0:T(8,128)(2,1)} %copy-done.6) | copy-start | bytes 1572868
  81.5 17.5 %all-to-all-start.2 = ((bf16[4,64,128]{2,1,0:T(8,128)(2,1)}), bf16[4,64,128]{2,1,0:T(8,128)(2,1)S(1)}, u32[]{:S(2)}, u32[]{:S(2)}) async-start(bf16[4,64,128]{2,1,0:T(8,128)(2,1)} %near_total.1), calls=%async_computation.2 | async-start | bytes 131072 | tf_op jit(solution)/shard_map/all_to_all | solution.py:274
